TPU v7x, 128 devices: a whole 4x4x4 slice. The times are simulated.
128 devices in a mesh: ctx: 128 (over y, x, z, core).
Axes of the slice: x: 4, y: 4, z: 4, core: 2. Of those that a mesh axis runs over, the one named last changes fastest.
Arguments:
- layer_input: bfloat16 [16384, 576], P('ctx'), may hold values from -6 to 6
- attn_gain: float32 [576], replicated, may hold values from 0.5 to 1.5
- w_query: bfloat16 [576, 576], replicated, may hold values from -0.25 to 0.25
- w_key: bfloat16 [576, 192], replicated, may hold values from -0.25 to 0.25
- w_value: bfloat16 [576, 192], replicated, may hold values from -0.25 to 0.25
- w_out: bfloat16 [576, 576], replicated, may hold values from -0.75 to 0.75
- mlp_gain: float32 [576], replicated, may hold values from 0.5 to 1.5
- w_gate: bfloat16 [576, 1536], replicated, may hold values from -0.25 to 0.25
- w_up: bfloat16 [576, 1536], replicated, may hold values from -0.25 to 0.25
- w_down: bfloat16 [1536, 576], replicated, may hold values from -0.15625 to 0.15625
- cotangent: bfloat16 [16384, 576], P('ctx'), may hold values from -6 to 6
- segment_ids: int32 [16384], P('ctx'), may hold values from 0 to 17, as said below
- pair_table: int32 [128], P('ctx'), may hold values from 0 to 127, as said below
Outputs:
- layer_output: bfloat16 [16384, 576], P('ctx')
- grad_x: float32 [16384, 576], P('ctx')
- grad_attn_gain: float32 [576], replicated
- grad_w_query: float32 [576, 576], replicated
- grad_w_key: float32 [576, 192], replicated
- grad_w_value: float32 [576, 192], replicated
- grad_w_out: float32 [576, 576], replicated
- grad_mlp_gain: float32 [576], replicated
- grad_w_gate: float32 [576, 1536], replicated
- grad_w_up: float32 [576, 1536], replicated
- grad_w_down: float32 [1536, 576], replicated
Inputs may be any that keep to these rules, and one draw needn't show every extreme that they name: `segment_ids`: as a function of a token's place in the pack the document number never falls and rises by at most one from one place to the next; places 0 to 8191 all form document 0. `pair_table`: A permutation: each block pair is held by exactly one device.
All inputs are finite; a program needn't handle non-finite values.
Results may differ from a plain program's by a relative error of at most 0.04.
Values may be sent and summed in bfloat16 or wider, within the bound.
A program may use at most 192 MiB of HBM per device.

v0:
```python
import math

import jax
import jax.numpy as jnp
from jax import lax
from jax.sharding import PartitionSpec as P

HEADS = 9
KV_HEADS = 3
HEAD_DIM = 64


NORM_EPS = 1e-05
ROPE_THETA = 100000.0


def rms_scale(features, gain_vec):
    return (
        features
        * lax.rsqrt(jnp.mean(features * features, axis=-1, keepdims=True) + NORM_EPS)
        * gain_vec
    )


def angles(positions, head_dim):
    freq_steps = jnp.arange(head_dim // 2).astype(jnp.float32)
    frequency = ROPE_THETA ** (-2.0 * freq_steps / head_dim)
    turned = positions.astype(jnp.float32)[:, None] * frequency[None, :]
    return (jnp.cos(turned), jnp.sin(turned))


def rotate(features, cos_table, sin_table, head_dim):
    row_count = features.shape[0]
    split_heads = features.reshape(row_count, -1, head_dim)
    lower_half = split_heads[..., : head_dim // 2]
    upper_half = split_heads[..., head_dim // 2 :]
    cos_wide = cos_table[:, None, :]
    sin_wide = sin_table[:, None, :]
    turned = jnp.concatenate(
        [
            lower_half * cos_wide - upper_half * sin_wide,
            upper_half * cos_wide + lower_half * sin_wide,
        ],
        -1,
    )
    return turned.reshape(row_count, -1)


def masked_scores(
    query_heads, key_heads, query_segs, key_segs, query_places, key_places, score_scale
):
    raw_scores = (
        jnp.einsum("bgrd,tgd->grbt", query_heads, key_heads, preferred_element_type=jnp.float32)
        * score_scale
    )
    allowed = (query_segs[:, None] == key_segs[None, :]) & (
        key_places[None, :] <= query_places[:, None]
    )
    return jnp.where(allowed[None, None], raw_scores, -jnp.inf)


def outer_sum(left, right):
    return lax.dot_general(
        left, right, (((0,), (0,)), ((), ())), preferred_element_type=jnp.float32
    )


def back_dot(grad_rows, weight):
    return lax.dot_general(
        grad_rows, weight, (((1,), (1,)), ((), ())), preferred_element_type=jnp.float32
    )


def on_device(
    layer_input,
    attn_gain,
    w_query,
    w_key,
    w_value,
    w_out,
    mlp_gain,
    w_gate,
    w_up,
    w_down,
    cotangent,
    segment_ids,
    pair_table,
):
    row_count = layer_input.shape[0]
    half_rows = row_count // 2
    devices = lax.axis_size("ctx")
    per_group = HEADS // KV_HEADS
    kv_width = KV_HEADS * HEAD_DIM
    score_scale = HEAD_DIM ** (-0.5)
    own_pair = pair_table[0]
    within = jnp.arange(row_count, dtype=jnp.int32)
    blocks = jnp.where(within < half_rows, own_pair, 2 * devices - 1 - own_pair)
    places = blocks * half_rows + within % half_rows
    cos_table, sin_table = angles(places, HEAD_DIM)
    x_float = layer_input.astype(jnp.float32)
    normed = rms_scale(x_float, attn_gain).astype(jnp.bfloat16)
    queries = jnp.dot(normed, w_query, preferred_element_type=jnp.float32)
    key_proj = jnp.dot(normed, w_key, preferred_element_type=jnp.float32)
    value_rows = jnp.dot(normed, w_value, preferred_element_type=jnp.float32).astype(jnp.bfloat16)
    q_rot = rotate(queries, cos_table, sin_table, HEAD_DIM).astype(jnp.bfloat16)
    k_rot = rotate(key_proj, cos_table, sin_table, HEAD_DIM).astype(jnp.bfloat16)
    pairs_local = jnp.concatenate([k_rot, value_rows], 1)
    pairs_all, segs_all, places_all = (
        lax.all_gather(pairs_local, "ctx", axis=0, tiled=True),
        lax.all_gather(segment_ids, "ctx", axis=0, tiled=True),
        lax.all_gather(places, "ctx", axis=0, tiled=True),
    )
    key_total = pairs_all.shape[0]
    kblock = math.gcd(key_total, 1024)
    block_count = key_total // kblock
    block_numbers = jnp.arange(block_count, dtype=jnp.int32)
    query_heads = q_rot.reshape(row_count, KV_HEADS, per_group, HEAD_DIM)

    def key_piece(block_index):
        block_start = block_index * kblock
        pair_block = lax.dynamic_slice_in_dim(pairs_all, block_start, kblock, 0)
        key_heads = pair_block[:, :kv_width].reshape(kblock, KV_HEADS, HEAD_DIM)
        value_heads = pair_block[:, kv_width:].reshape(kblock, KV_HEADS, HEAD_DIM)
        seg_block = lax.dynamic_slice_in_dim(segs_all, block_start, kblock, 0)
        place_block = lax.dynamic_slice_in_dim(places_all, block_start, kblock, 0)
        scores = masked_scores(
            query_heads, key_heads, segment_ids, seg_block, places, place_block, score_scale
        )
        return (key_heads, value_heads, scores)

    def stats_step(running, block_index):
        running_max, running_sum = running
        _, _, scores = key_piece(block_index)
        new_max = jnp.maximum(running_max, jnp.max(scores, -1))
        running_sum = running_sum * jnp.exp(running_max - new_max) + jnp.sum(
            jnp.exp(scores - new_max[..., None]), -1
        )
        return ((new_max, running_sum), None)

    start_max = jnp.full((KV_HEADS, per_group, row_count), -1e30, jnp.float32)
    start_sum = jnp.zeros((KV_HEADS, per_group, row_count), jnp.float32)
    (final_max, final_sum), _ = lax.scan(stats_step, (start_max, start_sum), block_numbers)
    log_total = final_max + jnp.log(final_sum)

    def output_step(mixed, block_index):
        _, value_heads, scores = key_piece(block_index)
        attn_probs = jnp.exp(scores - log_total[..., None]).astype(jnp.bfloat16)
        return (
            mixed
            + jnp.einsum(
                "grbt,tgd->bgrd", attn_probs, value_heads, preferred_element_type=jnp.float32
            ),
            None,
        )

    mixed_start = jnp.zeros((row_count, KV_HEADS, per_group, HEAD_DIM), jnp.float32)
    mixed_out, _ = lax.scan(output_step, mixed_start, block_numbers)
    attended = mixed_out.reshape(row_count, HEADS * HEAD_DIM)
    attended_low = attended.astype(jnp.bfloat16)
    hidden = x_float + jnp.dot(attended_low, w_out, preferred_element_type=jnp.float32)
    normed_two = rms_scale(hidden, mlp_gain).astype(jnp.bfloat16)
    gate_proj = jnp.dot(normed_two, w_gate, preferred_element_type=jnp.float32)
    upward = jnp.dot(normed_two, w_up, preferred_element_type=jnp.float32)
    active = (jax.nn.silu(gate_proj) * upward).astype(jnp.bfloat16)
    result = (hidden + jnp.dot(active, w_down, preferred_element_type=jnp.float32)).astype(
        jnp.bfloat16
    )
    grad_w_down = outer_sum(active, cotangent)
    grad_active = back_dot(cotangent, w_down)
    sigmoid_gate = jax.nn.sigmoid(gate_proj)
    grad_gate = (
        grad_active * upward * sigmoid_gate * (1.0 + gate_proj * (1.0 - sigmoid_gate))
    ).astype(jnp.bfloat16)
    grad_up = (grad_active * gate_proj * sigmoid_gate).astype(jnp.bfloat16)
    grad_w_gate = outer_sum(normed_two, grad_gate)
    grad_w_up = outer_sum(normed_two, grad_up)
    grad_normed_two = back_dot(grad_gate, w_gate) + back_dot(grad_up, w_up)
    _, norm_pull_two = jax.vjp(rms_scale, hidden, mlp_gain)
    grad_hidden_norm, grad_mlp_gain = norm_pull_two(grad_normed_two)
    grad_hidden = cotangent.astype(jnp.float32) + grad_hidden_norm
    grad_attn_out = grad_hidden.astype(jnp.bfloat16)
    grad_w_out = outer_sum(attended_low, grad_attn_out)
    grad_mixed = back_dot(grad_attn_out, w_out).astype(jnp.bfloat16)
    grad_heads = grad_mixed.reshape(row_count, KV_HEADS, per_group, HEAD_DIM)
    row_delta = jnp.sum(
        (grad_mixed.astype(jnp.float32) * attended).reshape(
            row_count, KV_HEADS, per_group, HEAD_DIM
        ),
        -1,
    )
    row_delta = jnp.transpose(row_delta, (1, 2, 0))

    def query_step(grad_query, block_index):
        key_heads, value_heads, scores = key_piece(block_index)
        attn_probs = jnp.exp(scores - log_total[..., None])
        grad_probs = jnp.einsum(
            "bgrd,tgd->grbt", grad_heads, value_heads, preferred_element_type=jnp.float32
        )
        grad_scores = (attn_probs * (grad_probs - row_delta[..., None])).astype(jnp.bfloat16)
        return (
            grad_query
            + jnp.einsum(
                "grbt,tgd->bgrd", grad_scores, key_heads, preferred_element_type=jnp.float32
            ),
            None,
        )

    query_start = jnp.zeros((row_count, KV_HEADS, per_group, HEAD_DIM), jnp.float32)
    grad_query, _ = lax.scan(query_step, query_start, block_numbers)
    own_keys = k_rot.reshape(row_count, KV_HEADS, HEAD_DIM)
    own_values = value_rows.reshape(row_count, KV_HEADS, HEAD_DIM)
    log_rows = log_total.reshape(HEADS, row_count).T
    delta_rows = row_delta.reshape(HEADS, row_count).T
    empty_keys = jnp.zeros((row_count, KV_HEADS, HEAD_DIM), jnp.float32)
    fold_carry = (empty_keys, empty_keys)
    piece_queries = lax.all_gather(q_rot, "ctx", axis=0, tiled=True)
    piece_grads = lax.all_gather(grad_mixed, "ctx", axis=0, tiled=True)
    piece_logs = lax.all_gather(log_rows.astype(jnp.bfloat16), "ctx", axis=0, tiled=True).astype(
        jnp.float32
    )
    piece_deltas = lax.all_gather(
        delta_rows.astype(jnp.bfloat16), "ctx", axis=0, tiled=True
    ).astype(jnp.float32)
    piece_segs = lax.all_gather(segment_ids, "ctx", axis=0, tiled=True)
    piece_places = lax.all_gather(places, "ctx", axis=0, tiled=True)
    piece_rows = piece_queries.shape[0]
    qblock = math.gcd(piece_rows, 1024)

    def piece_step(key_carry, block_index):
        first_row = block_index * qblock
        query_block = lax.dynamic_slice_in_dim(piece_queries, first_row, qblock, 0).reshape(
            qblock, KV_HEADS, per_group, HEAD_DIM
        )
        grad_block = lax.dynamic_slice_in_dim(piece_grads, first_row, qblock, 0).reshape(
            qblock, KV_HEADS, per_group, HEAD_DIM
        )
        log_block = lax.dynamic_slice_in_dim(piece_logs, first_row, qblock, 0).T.reshape(
            KV_HEADS, per_group, qblock
        )
        delta_block = lax.dynamic_slice_in_dim(piece_deltas, first_row, qblock, 0).T.reshape(
            KV_HEADS, per_group, qblock
        )
        seg_block = lax.dynamic_slice_in_dim(piece_segs, first_row, qblock, 0)
        place_block = lax.dynamic_slice_in_dim(piece_places, first_row, qblock, 0)
        scores = masked_scores(
            query_block, own_keys, seg_block, segment_ids, place_block, places, score_scale
        )
        attn_probs = jnp.exp(scores - log_block[..., None])
        grad_probs = jnp.einsum(
            "bgrd,tgd->grbt", grad_block, own_values, preferred_element_type=jnp.float32
        )
        grad_scores = (attn_probs * (grad_probs - delta_block[..., None])).astype(jnp.bfloat16)
        key_part = key_carry[0] + jnp.einsum(
            "grbt,bgrd->tgd", grad_scores, query_block, preferred_element_type=jnp.float32
        )
        value_part = key_carry[1] + jnp.einsum(
            "grbt,bgrd->tgd",
            attn_probs.astype(jnp.bfloat16),
            grad_block,
            preferred_element_type=jnp.float32,
        )
        return ((key_part, value_part), None)

    steps_here = jnp.arange(piece_rows // qblock, dtype=jnp.int32)
    fold_carry, _ = lax.scan(piece_step, fold_carry, steps_here)
    key_sums, value_sums = fold_carry
    grad_key_rot = key_sums.reshape(row_count, kv_width) * score_scale
    grad_value_sum = value_sums.reshape(row_count, kv_width)
    grad_query_rot = grad_query.reshape(row_count, HEADS * HEAD_DIM) * score_scale
    grad_q_low = rotate(grad_query_rot, cos_table, -sin_table, HEAD_DIM).astype(jnp.bfloat16)
    grad_k_low = rotate(grad_key_rot, cos_table, -sin_table, HEAD_DIM).astype(jnp.bfloat16)
    grad_v_low = grad_value_sum.astype(jnp.bfloat16)
    grad_w_query = outer_sum(normed, grad_q_low)
    grad_w_key = outer_sum(normed, grad_k_low)
    grad_w_value = outer_sum(normed, grad_v_low)
    grad_normed = (
        back_dot(grad_q_low, w_query) + back_dot(grad_k_low, w_key) + back_dot(grad_v_low, w_value)
    )
    _, norm_pull_one = jax.vjp(rms_scale, x_float, attn_gain)
    grad_x_norm, grad_attn_gain = norm_pull_one(grad_normed)
    grad_x = grad_hidden + grad_x_norm
    summed = lax.psum(
        (
            grad_attn_gain,
            grad_w_query,
            grad_w_key,
            grad_w_value,
            grad_w_out,
            grad_mlp_gain,
            grad_w_gate,
            grad_w_up,
            grad_w_down,
        ),
        "ctx",
    )
    return (
        result,
        grad_x,
        summed[0],
        summed[1],
        summed[2],
        summed[3],
        summed[4],
        summed[5],
        summed[6],
        summed[7],
        summed[8],
    )


def solution(mesh):
    return jax.shard_map(
        on_device,
        mesh=mesh,
        in_specs=(
            P("ctx", None),
            P(),
            P(),
            P(),
            P(),
            P(),
            P(),
            P(),
            P(),
            P(),
            P("ctx", None),
            P("ctx"),
            P("ctx"),
        ),
        out_specs=(P("ctx", None), P("ctx", None), P(), P(), P(), P(), P(), P(), P(), P(), P()),
        check_vma=False,
    )
```

profile of v0, /device:TPU:1, one launch (start us, length us, event | category | flops | bytes accessed | tf_op | source)
XLA Modules:
  0.0 1231.9 jit_solution(14744649385130089809)
XLA Ops:
  15.3 34.4 %all-gather = s32[128,1,128]{2,1,0:T(1,128)S(1)} all-gather(s32[1,1,128]{2,1,0:T(1,128)S(1)} %bitcast.322), channel_id=1, replica_groups=mesh['ctx'=128] {'ctx'}, dimensions={0}, use_global_device_ids=true | all-gather | bytes 66048 | tf_op jit(solution)/shard_map/all_gather | solution.py:110
  49.8 29.9 %all-gather.1 = s32[128,1,128]{2,1,0:T(1,128)S(1)} all-gather(s32[1,1,128]{2,1,0:T(1,128)S(1)} %fusion.100), channel_id=1, replica_groups=mesh['ctx'=128] {'ctx'}, dimensions={0}, use_global_device_ids=true | all-gather | bytes 66048 | tf_op jit(solution)/shard_map/all_gather | solution.py:111
  79.7 27.1 %all-gather.6.cloned.1.call-done = bf16[16384,384]{0,1:T(8,128)(2,1)} async-done(((bf16[128,384]{0,1:T(8,128)(2,1)}), bf16[16384,384]{0,1:T(8,128)(2,1)}) %all-gather.6.cloned.1.call-update) | async-done | bytes 12582928 | tf_op jit(solution)/shard_map/all_gather | solution.py:109
  106.8 171.1 %while.48 = (s32[]{:T(128)}, f32[3,3,128]{2,1,0:T(4,128)S(1)}, f32[3,3,128]{2,1,0:T(4,128)S(1)}, s32[128]{0:T(128)S(1)}, s32[16]{0:T(128)S(1)}, /*index=5*/s32[1...) while((s32[]{:T(128)}, f32[3,3,128]{2,1,0:T(4,128)S(1)}, ...), condition=%wide.region_4.5_spmd.clone, body=%wide.region_1.4_spmd.clone.sunk | while | flops 159652736 | bytes 11243758 | solution.py:142
  120.7 3.9 fusion.207
  152.6 3.9 fusion.207
  163.3 4.0 fusion.207
  185.1 4.0 fusion.207
  206.7 3.9 fusion.207
  278.0 95.5 %while.49 = (s32[]{:T(128)}, f32[128,3,3,64]{0,3,2,1:T(8,128)S(1)}, s32[16]{0:T(128)S(1)}, bf16[16384,384]{0,1:T(8,128)(2,1)}, s32[128]{0:T(128)S(1)}, /*index=5...) while((s32[]{:T(128)}, f32[128,3,3,64]{0,3,2,1:T(8,128)S(1)}, ...), condition=%wide.region_6.7_spmd.clone, body=%wide.region_5.6_spmd.clone.sunk | while | flops 307250432 | bytes 3389701 | solution.py:157
  382.7 36.2 %all_gather.27 = bf16[16384,9]{0,1:T(8,128)(2,1)S(1)} all-gather(bf16[128,9]{0,1:T(8,128)(2,1)S(1)} %bitcast.325), channel_id=1, replica_groups=mesh['ctx'=128] {'ctx'}, dimensions={0}, use_global_device_ids=true | all-gather | bytes 297216 | tf_op jit(solution)/shard_map/all_gather | solution.py:218
  420.0 34.8 %all_gather.29 = bf16[16384,9]{0,1:T(8,128)(2,1)S(1)} all-gather(bf16[128,9]{0,1:T(8,128)(2,1)S(1)} %bitcast.326), channel_id=1, replica_groups=mesh['ctx'=128] {'ctx'}, dimensions={0}, use_global_device_ids=true | all-gather | bytes 297216 | tf_op jit(solution)/shard_map/all_gather | solution.py:221
  455.9 194.1 %while.50 = (s32[]{:T(128)}, f32[128,3,3,64]{0,3,2,1:T(8,128)}, s32[16]{0:T(128)S(1)}, bf16[16384,384]{0,1:T(8,128)(2,1)}, s32[128]{0:T(128)S(1)}, /*index=5*/s3...) while((s32[]{:T(128)}, f32[128,3,3,64]{0,3,2,1:T(8,128)}, ...), condition=%wide.region_11.12_spmd.clone, body=%wide.region_10.11_spmd.clone.sunk | while | flops 460604672 | bytes 13390641 | solution.py:209
  463.3 4.9 fusion.224
  475.4 5.2 fusion.224
  487.7 5.0 fusion.224
  499.8 4.9 fusion.224
  511.9 4.9 fusion.224
  524.0 4.9 fusion.224
  536.1 4.9 fusion.224
  548.2 4.9 fusion.224
  560.3 4.9 fusion.224
  572.4 4.9 fusion.224
  584.5 4.9 fusion.224
  596.6 4.9 fusion.224
  608.7 4.9 fusion.224
  620.8 4.9 fusion.224
  632.9 4.9 fusion.224
  645.0 4.9 fusion.224
  662.4 370.1 %while.51 = (s32[]{:T(128)}, f32[128,3,64]{0,2,1:T(8,128)}, f32[128,3,64]{0,2,1:T(8,128)}, s32[16]{0:T(128)S(1)}, bf16[16384,576]{0,1:T(8,128)(2,1)}, /*index=5*...) while((s32[]{:T(128)}, f32[128,3,64]{0,2,1:T(8,128)}, ...), condition=%wide.region_13.14_spmd.clone, body=%wide.region_12.13_spmd.clone.sunk | while | flops 616269056 | bytes 26876428 | solution.py:265
  674.2 6.8 fusion.235
  681.0 4.4 fusion.236
  697.3 6.8 fusion.235
  704.1 4.4 fusion.236
  720.4 6.8 fusion.235
  727.2 4.4 fusion.236
  743.5 6.8 fusion.235
  750.4 4.4 fusion.236
  766.7 6.8 fusion.235
  773.5 4.4 fusion.236
  789.8 6.8 fusion.235
  796.6 4.4 fusion.236
  812.9 6.8 fusion.235
  819.7 4.4 fusion.236
  836.0 6.8 fusion.235
  842.8 4.4 fusion.236
  859.1 6.8 fusion.235
  865.9 4.4 fusion.236
  882.2 6.8 fusion.235
  889.1 4.4 fusion.236
  905.4 6.8 fusion.235
  912.2 4.4 fusion.236
  928.5 6.8 fusion.235
  935.3 4.4 fusion.236
  951.6 6.8 fusion.235
  958.4 4.4 fusion.236
  974.7 6.8 fusion.235
  981.5 4.4 fusion.236
  997.8 6.8 fusion.235
  1004.6 4.4 fusion.236
  1021.0 6.8 fusion.235
  1027.8 4.4 fusion.236
  1041.8 64.5 %all-reduce = (f32[576]{0:T(1024)}, f32[576]{0:T(1024)}) all-reduce(f32[576]{0:T(1024)S(1)} %get-tuple-element.515, f32[576]{0:T(1024)S(1)} %get-tuple-element.513), channel_id=1, replica_groups=mesh['ctx'=128] {'ctx'}, use_global_device_ids=true, to_apply=%region_16.17 | all-reduce | flops 1152 | bytes 9216 | tf_op jit(solution)/shard_map/psum | solution.py:282
  1107.2 103.4 %all-reduce.4.cloned.1.call-done = (f32[576,576]{1,0:T(8,128)}, f32[576,192]{0,1:T(8,128)}, f32[576,192]{0,1:T(8,128)}, f32[576,576]{1,0:T(8,128)}, f32[576,1536...) async-done(((f32[576,576]{1,0:T(8,128)}, f32[576,192]{0,1:T(8,128)}, f32[576,192]{0,1:T(8,128)}, f32[576,576]{1,0:T(8,128)}, f32[576,1536]{1,0:T(8,128)}, ...) | async-done | bytes 14155792 | tf_op jit(solution)/shard_map/psum | solution.py:282
  (1027 shorter events, 561.8 us)
Async XLA Ops:
  7.2 371.3 %copy-start = (bf16[1536,576]{0,1:T(8,128)(2,1)S(1)}, bf16[1536,576]{0,1:T(8,128)(2,1)}, u32[]{:S(2)}) copy-start(bf16[1536,576]{0,1:T(8,128)(2,1)} %param.30) | copy-start | bytes 5308420
  7.2 8.1 copy-start.35
  7.2 99.6 %all-gather.6.cloned.1.call-start = ((), (), s32[]{:S(2)}) async-start(), calls=%async_computation | async-start | bytes 12681216 | tf_op jit(solution)/shard_map/all_gather | solution.py:109
  8.4 98.4 %copy-start.42 = (f32[128]{0:T(128)}, f32[128]{0:T(128)S(1)}, u32[]{:S(2)}) copy-start(f32[128]{0:T(128)S(1)} %fusion.90) | copy-start | bytes 1540
  9.7 97.1 %copy-start.38 = (bf16[128,192]{0,1:T(8,128)(2,1)}, bf16[128,192]{0,1:T(8,128)(2,1)S(1)}, u32[]{:S(2)}) copy-start(bf16[128,192]{0,1:T(8,128)(2,1)S(1)} %convolution_convert_fusion.1) | copy-start | bytes 147460
  11.9 639.1 %copy-start.37 = (f32[128,32]{0,1:T(8,128)}, f32[128,32]{0,1:T(8,128)S(1)}, u32[]{:S(2)}) copy-start(f32[128,32]{0,1:T(8,128)S(1)} %get-tuple-element.649) | copy-start | bytes 49156
  12.7 649.7 %all-gather.8.cloned.1.call-start = ((), (), s32[]{:S(2)}) async-start(), calls=%async_computation.1 | async-start | bytes 19021824 | tf_op jit(solution)/shard_map/all_gather | solution.py:216
  15.2 647.1 %all-gather.10.cloned.1.call-start = ((), (), s32[]{:S(2)}) async-start(), calls=%async_computation.2 | async-start | bytes 19021824 | tf_op jit(solution)/shard_map/all_gather | solution.py:217
  278.0 96.1 %copy-start.2 = (bf16[128,576]{0,1:T(8,128)(2,1)S(1)}, bf16[128,576]{0,1:T(8,128)(2,1)}, u32[]{:S(2)}) copy-start(bf16[128,576]{0,1:T(8,128)(2,1)} %param.21) | copy-start | bytes 442372
  278.0 97.8 %copy-start.39 = (f32[576]{0:T(1024)S(1)}, f32[576]{0:T(1024)}, u32[]{:S(2)}) copy-start(f32[576]{0:T(1024)} %param.27) | copy-start | bytes 6916
  381.4 74.5 %copy-start.1 = (bf16[128,3,3,64]{0,3,2,1:T(8,128)(2,1)S(1)}, bf16[128,3,3,64]{0,3,2,1:T(8,128)(2,1)}, u32[]{:S(2)}) copy-start(bf16[128,3,3,64]{0,3,2,1:T(8,128)(2,1)} %get-tuple-element.1217) | copy-start | bytes 442372
  381.6 74.3 %copy-start.5 = (f32[128,576]{0,1:T(8,128)}, f32[128,576]{0,1:T(8,128)S(1)}, u32[]{:S(2)}) copy-start(f32[128,576]{0,1:T(8,128)S(1)} %fusion.88) | copy-start | bytes 884740
  382.6 828.0 %all-reduce.4.cloned.1.call-start = ((), (), s32[]{:S(2)}) async-start(), calls=%async_computation.3 | async-start | bytes 29097984 | tf_op jit(solution)/shard_map/psum | solution.py:282
  455.9 195.2 %copy-start.36 = (f32[576]{0:T(1024)S(1)}, f32[576]{0:T(1024)}, u32[]{:S(2)}) copy-start(f32[576]{0:T(1024)} %param.22) | copy-start | bytes 6916
  455.9 7.4 copy-start.41
  468.2 7.2 copy-start.41
  480.5 7.2 copy-start.41
  492.7 7.2 copy-start.41
  504.8 7.2 copy-start.41
  516.9 7.2 copy-start.41
  529.0 7.2 copy-start.41
  541.1 7.2 copy-start.41
  553.2 7.2 copy-start.41
  565.3 7.2 copy-start.41
  577.4 7.2 copy-start.41
  589.5 7.2 copy-start.41
  601.6 7.2 copy-start.41
  613.7 7.2 copy-start.41
  625.8 7.2 copy-start.41
  637.9 7.2 copy-start.41
  662.4 7.3 copy-start.7
  662.4 7.3 copy-start.32
  685.5 7.3 copy-start.7
  685.5 7.3 copy-start.32
  708.6 7.3 copy-start.7
  708.6 7.3 copy-start.32
  731.7 7.3 copy-start.7
  731.7 7.3 copy-start.32
  754.8 7.3 copy-start.7
  754.8 7.3 copy-start.32
  777.9 7.3 copy-start.7
  777.9 7.3 copy-start.32
  801.1 7.3 copy-start.7
  801.1 7.3 copy-start.32
  824.2 7.3 copy-start.7
  824.2 7.3 copy-start.32
  847.3 7.3 copy-start.7
  847.3 7.3 copy-start.32
  870.4 7.3 copy-start.7
  870.4 7.3 copy-start.32
  893.5 7.3 copy-start.7
  893.5 7.3 copy-start.32
  916.6 7.3 copy-start.7
  916.7 7.3 copy-start.32
  939.8 7.3 copy-start.7
  939.8 7.3 copy-start.32
  962.9 7.3 copy-start.7
  962.9 7.3 copy-start.32
  986.0 7.3 copy-start.7
  986.0 7.3 copy-start.32
  1009.1 7.3 copy-start.7
  1009.1 7.3 copy-start.32
  1038.3 68.0 %copy-start.43 = (f32[128]{0:T(128)S(1)}, f32[128]{0:T(128)}, u32[]{:S(2)}) copy-start(f32[128]{0:T(128)} %copy-done.42) | copy-start | bytes 1540
  1038.3 68.0 %copy-start.6 = (f32[128,576]{0,1:T(8,128)S(1)}, f32[128,576]{0,1:T(8,128)}, u32[]{:S(2)}) copy-start(f32[128,576]{0,1:T(8,128)} %copy-done.5) | copy-start | bytes 884740
  (136 other events, 510.3 us)
Sparse Core Ops, SparseCore 0:
  12.8 93.9 all-gather.5
  110.2 106.5 all-gather.7
  382.7 108.1 all-gather.9
  1037.3 173.1 all-reduce.3
where the time goes:
time: 1240 us; the launch traced here: 1230 us
  matrix products  488 us (39%)
  local copies, waits for them, and re-layouts  213 us (17%)
  blocking collectives  200 us (16%)
  other arithmetic  138 us (11%)
  waiting for transfers between devices  131 us (11%)
  loops' own time  46.8 us (4%)
  between operations  15 us (1%)
    dot_general x48, matrix products, masked_scores(): jnp.einsum('bgrd,tgd->grbt', query_heads, key_heads, preferred_element_ty...  161 us
    dot_general x16, matrix products, piece_step(): jnp.einsum('grbt,bgrd->tgd', grad_scores, query_block, preferred_element_...  108 us
    psum x1, waiting for transfers between devices, on_device(): lax.psum((grad_attn_gain, grad_w_query, grad_w_key, grad_w_value, grad_w_...  103 us
    dot_general x16, matrix products, query_step(): jnp.einsum('grbt,tgd->bgrd', grad_scores, key_heads, preferred_element_ty...  79.3 us
    dot_general x16, matrix products, piece_step(): jnp.einsum('grbt,bgrd->tgd', attn_probs.astype(jnp.bfloat16), grad_block,...  70.4 us
    psum x1, blocking collectives, on_device(): lax.psum((grad_attn_gain, grad_w_query, grad_w_key, grad_w_value, grad_w_...  64.5 us
    reduce_sum x16, other arithmetic, stats_step(): jnp.sum(jnp.exp(scores - new_max[..., None]), -1)  54 us
    dynamic_slice x16, local copies, waits for them, and re-layouts, piece_step(): lax.dynamic_slice_in_dim(piece_grads, first_row, qblock, 0)  46.7 us
  transfers between devices with their start and end apart: 4, of which 2 were waited for; matrix products, arithmetic and copies ran while one was open for 37% of the time, Pallas kernels for 0%

commit v1 on v0

v1 whole, which is shorter than its diff:
```python
import functools
import jax
import jax.numpy as jnp
from jax import lax
from jax.experimental import pallas as pl
from jax.experimental.pallas import tpu as pltpu
from jax.sharding import PartitionSpec as P

f32 = jnp.float32
bf16 = jnp.bfloat16
D = 576
HEADS = 9
KV_HEADS = 3
HEAD_DIM = 64
PER_GROUP = HEADS // KV_HEADS
FF = 1536
NORM_EPS = 1e-05
ROPE_THETA = 100000.0
ROWS = 128
HALF = 64
N_CTX = 128
TOKENS = ROWS * N_CTX
DOCS = 18
META = 16
SLAB = ROWS + META
CHUNK = 512
PIECES = CHUNK // HALF
CHUNKS = TOKENS // CHUNK
COLS = HEADS * HALF
NEG = -1e30
SCALE = HEAD_DIM ** (-0.5)
VMEM_LIMIT = 56 * 1024 * 1024

K_AT = (0, 64, 128)
V_AT = (128, 192, 64)

GATE_AT = 0
UP_AT = GATE_AT + 12 * D
DOWN_AT = UP_AT + 12 * D
OUT_AT = DOWN_AT + 5 * FF
GAIN_AT = OUT_AT + 5 * D
BAND_ROWS = 64
FF_ROWS = 3 * N_CTX * BAND_ROWS
Q_AT = 0
KV_AT = Q_AT + 5 * D
GAIN_ONE_AT = KV_AT + 3 * D
BAND_ROWS_ONE = 16
ATT_ROWS = 3 * N_CTX * BAND_ROWS_ONE

MESH = pl.DeviceIdType.MESH
SIDE = 4
ORDERS = ((2, 1, 0), (1, 0, 2), (0, 2, 1))
STRIDES = (32, 8, 2)


def whereabouts():
    me = lax.axis_index("ctx")
    coords = (me // 32, lax.rem(me // 8, SIDE), lax.rem(me // 2, SIDE))
    return me, coords, lax.rem(me, 2)


def wrap(coord, step):
    return lax.rem(coord + (step + SIDE), SIDE)


def neighbour(me, coords, axis, step):
    return me + (wrap(coords[axis], step) - coords[axis]) * STRIDES[axis]


def greet(me, coords, core):
    barrier = pltpu.get_barrier_semaphore()
    others = [me + 1 - 2 * core]
    for axis in range(3):
        others += [neighbour(me, coords, axis, 1), neighbour(me, coords, axis, -1)]
    for other in others:
        pl.semaphore_signal(barrier, inc=1, device_id=(other,), device_id_type=MESH)
    pl.semaphore_wait(barrier, len(others))


def half_rows(rows):
    return rows // 32 * 16


class Sender:
    def __init__(self, sems):
        self.sems = sems
        self.copies = []

    def start(self, src, dst, device):
        at = len(self.copies)
        copy = pltpu.make_async_remote_copy(
            src_ref=src,
            dst_ref=dst,
            send_sem=self.sems[0].at[at],
            recv_sem=self.sems[1].at[at],
            device_id=(device,),
            device_id_type=MESH,
        )
        copy.start()
        self.copies.append(copy)
        return copy

    def finish(self):
        for copy in self.copies:
            copy.wait_send()


def at_axes(order, values):
    index = [None] * 3
    for axis, value in zip(order, values):
        index[axis] = value
    return tuple(index)


WHOLE = pl.ds(0, SIDE)


def gather_bands(own, out, sems, local_sem):
    me, coords, core = whereabouts()
    sibling = me + 1 - 2 * core
    sender = Sender(sems)
    bands = range(len(own))
    homes = []
    for band in bands:
        copy = pltpu.make_async_copy(own[band], out[band].at[coords + (core,)], local_sem.at[band])
        copy.start()
        homes.append(copy)
    for copy in homes:
        copy.wait()
    across = []

    def pass_over(band, index):
        part = out[band].at[index + (core,)]
        across.append(sender.start(part, part, sibling))

    for phase in range(3):
        subs = (None,) if phase < 2 else range(SIDE)

        def index_of(band, coord, sub):
            order = ORDERS[band % 3]
            mine = [coords[axis] for axis in order]
            values = [WHOLE] * phase + [coord] + mine[phase + 1 :]
            if sub is not None:
                values[0] = sub
            return at_axes(order, values)

        jobs = [(sub, band) for sub in subs for band in bands]
        sent, passed = {}, {}
        for sub, band in jobs:
            axis = ORDERS[band % 3][phase]
            part = out[band].at[index_of(band, coords[axis], sub) + (core,)]
            sent[sub, band] = (
                sender.start(part, part, neighbour(me, coords, axis, 1)),
                sender.start(part, part, neighbour(me, coords, axis, -1)),
            )
        if phase == 0:
            for band in bands:
                pass_over(band, coords)
        for sub, band in jobs:
            axis = ORDERS[band % 3][phase]
            rows = own[band].shape[0]
            cut = half_rows(rows)
            plus, minus = sent[sub, band]
            low = index_of(band, wrap(coords[axis], -1), sub)
            high = index_of(band, wrap(coords[axis], 1), sub)
            plus.wait_recv()
            part = out[band].at[low + (core, pl.ds(0, cut))]
            one = sender.start(part, part, neighbour(me, coords, axis, 1))
            minus.wait_recv()
            part = out[band].at[high + (core, pl.ds(cut, rows - cut))]
            two = sender.start(part, part, neighbour(me, coords, axis, -1))
            passed[sub, band] = (one, two)
            pass_over(band, low)
            pass_over(band, high)
        for sub, band in jobs:
            axis = ORDERS[band % 3][phase]
            one, two = passed[sub, band]
            one.wait_recv()
            two.wait_recv()
            pass_over(band, index_of(band, wrap(coords[axis], 2), sub))
    for copy in across:
        copy.wait_recv()
    sender.finish()


def scatter_bands(parts, done, scratch):
    n = len(parts)
    acc, sib = scratch[:n], scratch[n : 2 * n]
    landing = [scratch[2 * n + 3 * b : 2 * n + 3 * b + 3] for b in range(n)]
    send, recv, local_sem = scratch[5 * n :]
    me, coords, core = whereabouts()
    sibling = me + 1 - 2 * core
    sender = Sender((send, recv))
    bands = range(n)
    steps = (2, 1, -1, 0)
    order_of = [ORDERS[b % 3] for b in bands]

    homes, swaps = {}, {}
    for step in steps:
        for band in bands:
            order = order_of[band]
            plane = at_axes(order, (wrap(coords[order[0]], step), WHOLE, WHOLE))
            copy = pltpu.make_async_copy(
                parts[band].at[plane + (core,)], acc[band].at[plane], local_sem.at[band, step % 4]
            )
            copy.start()
            homes[band, step] = copy
        for sub in range(SIDE):
            for band in bands:
                order = order_of[band]
                line = at_axes(order, (wrap(coords[order[0]], step), sub, WHOLE))
                swaps[band, step, sub] = sender.start(
                    parts[band].at[line + (1 - core,)], sib[band].at[line], sibling
                )

    def add_swap(band, step, sub):
        order = order_of[band]
        swaps[band, step, sub].wait_recv()
        first = wrap(coords[order[0]], step)

        def body(last, carry):
            at = at_axes(order, (first, sub, last))
            acc[band][at] = acc[band][at] + sib[band][at]
            return carry

        lax.fori_loop(0, SIDE, body, 0)

    for phase in range(3):
        subs = tuple(range(SIDE)) if phase == 0 else (None,)
        jobs = [(sub, band) for sub in subs for band in bands]

        def index_of(band, step, sub):
            order = order_of[band]
            mine = [coords[axis] for axis in order]
            values = mine[:phase] + [wrap(mine[phase], step)] + [WHOLE] * (2 - phase)
            if sub is not None:
                values[1] = sub
            return at_axes(order, values)

        def land(band, slot, sub):
            return landing[band][phase].at[(slot,) if sub is None else (slot, sub)]

        def each(band, sub, body):
            if phase == 2:
                body(())
            else:

                def run(last, carry):
                    body((last,))
                    return carry

                lax.fori_loop(0, SIDE, run, 0)

        def acc_at(band, step, sub, tail):
            order = order_of[band]
            mine = [coords[axis] for axis in order]
            values = mine[:phase] + [wrap(mine[phase], step)]
            if sub is not None:
                values.append(sub)
            return at_axes(order, values + list(tail))

        def landed(slot, sub, tail):
            return (slot,) + (() if sub is None else (sub,)) + tail

        first, whole = {}, {}
        for sub, band in jobs:
            axis = order_of[band][phase]
            rows = parts[band].shape[4]
            cut = half_rows(rows)
            if phase == 0:
                if sub == 0:
                    homes[band, 2].wait()
                add_swap(band, 2, sub)
            far = index_of(band, 2, sub)
            lead = (WHOLE,) * (1 if phase < 2 else 0)
            first[sub, band] = []
            for slot, lo, size, step in ((0, 0, cut, 1), (1, cut, rows - cut, -1)):
                copy = None
                if size:
                    copy = sender.start(
                        acc[band].at[far + (pl.ds(lo, size),)],
                        land(band, slot, sub).at[lead + (pl.ds(0, size),)],
                        neighbour(me, coords, axis, step),
                    )
                first[sub, band].append(copy)
        for sub, band in jobs:
            axis = order_of[band][phase]
            rows = parts[band].shape[4]
            cut = half_rows(rows)
            for step, slot, lo, size in ((1, 0, 0, cut), (-1, 1, cut, rows - cut)):
                if phase == 0:
                    if sub == 0:
                        homes[band, step].wait()
                    add_swap(band, step, sub)
                if size:
                    first[sub, band][slot].wait_recv()

                    def body(tail, step=step, slot=slot, lo=lo, size=size):
                        at = acc_at(band, step, sub, tail) + (pl.ds(lo, size),)
                        acc[band][at] = (
                            acc[band][at]
                            + landing[band][phase][landed(slot, sub, tail) + (pl.ds(0, size),)]
                        )

                    each(band, sub, body)
                whole[sub, band, step] = sender.start(
                    acc[band].at[index_of(band, step, sub)],
                    land(band, 2 + slot, sub),
                    neighbour(me, coords, axis, step),
                )
        for sub, band in jobs:
            if phase == 0:
                if sub == 0:
                    homes[band, 0].wait()
                add_swap(band, 0, sub)
            whole[sub, band, 1].wait_recv()
            whole[sub, band, -1].wait_recv()

            def body(tail):
                at = acc_at(band, 0, sub, tail)
                total = (
                    acc[band][at].astype(f32)
                    + landing[band][phase][landed(2, sub, tail)].astype(f32)
                    + landing[band][phase][landed(3, sub, tail)].astype(f32)
                )
                if phase == 2:
                    done[band][...] = total
                else:
                    acc[band][at] = total.astype(bf16)

            each(band, sub, body)
    sender.finish()


def rms_parts(features):
    return lax.rsqrt(jnp.mean(features * features, axis=-1, keepdims=True) + NORM_EPS)


def rms_back(features, gain, grad):
    inverse = rms_parts(features)
    scaled = grad * gain
    inner = jnp.mean(scaled * features, axis=-1, keepdims=True)
    by_features = inverse * scaled - features * (inverse * inverse * inverse * inner)
    by_gain = jnp.sum(grad * features * inverse, axis=0, keepdims=True)
    return by_features, by_gain


def nt_dot(left, right):
    return lax.dot_general(left, right, (((1,), (1,)), ((), ())), preferred_element_type=f32)


def tn_dot(left, right):
    return lax.dot_general(left, right, (((0,), (0,)), ((), ())), preferred_element_type=f32)


def nn_dot(left, right):
    return jnp.dot(left, right, preferred_element_type=f32)


def turn(tile, cos_wide, sin_wide):
    lanes = lax.broadcasted_iota(jnp.int32, tile.shape, 1)
    swapped = jnp.where(
        lax.rem(lanes, HEAD_DIM) < HEAD_DIM // 2, pltpu.roll(tile, 96, 1), pltpu.roll(tile, 32, 1)
    )
    return tile * cos_wide + swapped * sin_wide


def project_kernel(
    x_ref, gain_ref, wq_ref, wk_ref, wv_ref, cos_ref, sin_ref, meta_ref,
    q_ref, n_ref, out0, out1, out2,
    own0, own1, own2, send, recv, local_sem,
):
    features = x_ref[...].astype(f32)
    normed = (features * rms_parts(features) * gain_ref[...]).astype(bf16)
    n_ref[...] = normed
    cos_wide, sin_wide = cos_ref[...], sin_ref[...]
    keys = nn_dot(normed, wk_ref[...])
    values = nn_dot(normed, wv_ref[...]).astype(bf16)
    queries = nn_dot(normed, wq_ref[...])
    own0[0:ROWS, :] = turn(keys[:, 0:128], cos_wide, sin_wide).astype(bf16)
    own0[ROWS:SLAB, :] = meta_ref[...]
    mixed = turn(jnp.concatenate([keys[:, 128:192], queries[:, 512:576]], 1), cos_wide, sin_wide)
    own1[...] = jnp.concatenate([mixed[:, 0:64].astype(bf16), values[:, 128:192]], 1)
    own2[...] = values[:, 0:128]
    for tile in range(4):
        at = slice(128 * tile, 128 * tile + 128)
        q_ref[:, at] = (turn(queries[:, at], cos_wide, sin_wide).astype(bf16).astype(f32) * SCALE).astype(bf16)
    q_ref[:, 512:576] = (mixed[:, 64:128].astype(bf16).astype(f32) * SCALE).astype(bf16)
    me, coords, core = whereabouts()
    greet(me, coords, core)
    gather_bands((own0, own1, own2), (out0, out1, out2), (send, recv), local_sem)


def project_and_gather(x, gain, wq, wk, wv, cos_wide, sin_wide, meta):
    vmem = pl.BlockSpec(memory_space=pltpu.VMEM)
    anywhere = pl.BlockSpec(memory_space=pl.ANY)
    rows = (SLAB, ROWS, ROWS)
    return pl.pallas_call(
        project_kernel,
        out_shape=(
            jax.ShapeDtypeStruct((ROWS, D), bf16),
            jax.ShapeDtypeStruct((ROWS, D), bf16),
        )
        + tuple(jax.ShapeDtypeStruct((SIDE, SIDE, SIDE, 2, r, 128), bf16) for r in rows),
        in_specs=[vmem] * 8,
        out_specs=(vmem, vmem, anywhere, anywhere, anywhere),
        scratch_shapes=[pltpu.VMEM((r, 128), bf16) for r in rows]
        + [
            pltpu.SemaphoreType.DMA((3 * 48,)),
            pltpu.SemaphoreType.DMA((3 * 48,)),
            pltpu.SemaphoreType.DMA((3,)),
        ],
        compiler_params=pltpu.CompilerParams(
            collective_id=1, has_side_effects=True, vmem_limit_bytes=VMEM_LIMIT
        ),
        name="project_and_gather",
    )(x, gain, wq, wk, wv, cos_wide, sin_wide, meta)


def needed(chunk, a_hi, b_lo, b_hi):
    return (chunk <= a_hi) | ((chunk >= b_lo) & (chunk <= b_hi))


def chunk_rows(chunk):
    return pl.ds(pl.multiple_of(chunk * CHUNK, CHUNK), CHUNK)


def wait_chunk(chunk, held, sem):
    window = held.at[chunk_rows(chunk)]
    pltpu.make_async_copy(window, window, sem.at[chunk]).wait()


def chunk_mask(chunk, place_row, start_row):
    keys = chunk * CHUNK + lax.broadcasted_iota(jnp.int32, (CHUNK, COLS), 0)
    return (keys <= place_row) & (keys >= start_row)


def layer_kernel(
    source, info,
    kv0, kv1, kv2, wo_hbm, wg_hbm, wu_hbm, wd_hbm,
    q_ref, rows_ref, x_ref, c_ref, gain_ref,
    result_ref, gh_ref, dq_ref, dkv0, dkv1, dkv2, dw0, dw1, dw2,
    held, sem, wo_ref, wg_ref, wu_ref, wd_ref, w_sem, q_spread, g_spread, mixed, top, total, att_ref,
    delta_ref, dw, dw_sem, staged, blank, out_sem, blank_sem, gain_rows,
):
    a_hi, b_lo, b_hi = info[0], info[1], info[2]
    kvs, dkvs, dws = (kv0, kv1, kv2), (dkv0, dkv1, dkv2), (dw0, dw1, dw2)

    def issue(chunk, carry):
        @pl.when(needed(chunk, a_hi, b_lo, b_hi))
        def _():
            for piece in range(PIECES):
                slot = source[chunk * PIECES + piece]
                rows = pl.ds(pl.multiple_of(chunk * CHUNK + piece * HALF, HALF), HALF)
                for band in range(3):
                    row = slot + (slot // ROWS * META if band == 0 else 0)
                    pltpu.make_async_copy(
                        kvs[band].at[pl.ds(pl.multiple_of(row, 16), HALF)],
                        held.at[rows, 128 * band : 128 * band + 128],
                        sem.at[chunk],
                    ).start()

        return carry

    lax.fori_loop(0, CHUNKS, issue, 0)
    weights = [
        pltpu.make_async_copy(src, dst, w_sem.at[i])
        for i, (src, dst) in enumerate(
            ((wo_hbm, wo_ref), (wg_hbm, wg_ref), (wu_hbm, wu_ref), (wd_hbm, wd_ref))
        )
    ]
    for copy in weights:
        copy.start()

    def spread(rows, place, windows):
        for block in range(2):
            for head in range(HEADS):
                tile = rows[block * HALF : (block + 1) * HALF, head * HEAD_DIM : (head + 1) * HEAD_DIM]
                at = windows[head // PER_GROUP]
                place[block, head * HALF : (head + 1) * HALF, at : at + HEAD_DIM] = tile

    def unspread(columns, place, block, windows):
        for head in range(HEADS):
            at = windows[head // PER_GROUP]
            tile = columns[at : at + HEAD_DIM, head * HALF : (head + 1) * HALF]
            place[block * HALF : (block + 1) * HALF, head * HEAD_DIM : (head + 1) * HEAD_DIM] = tile.T

    q_spread[...] = jnp.zeros_like(q_spread)
    g_spread[...] = jnp.zeros_like(g_spread)
    spread(q_ref[...], q_spread, K_AT)
    mixed[...] = jnp.zeros_like(mixed)
    top[...] = jnp.full_like(top, NEG)
    total[...] = jnp.zeros_like(total)
    blank[...] = jnp.zeros_like(blank)

    def mask_of(block, chunk):
        return chunk_mask(
            chunk, rows_ref[2 * block : 2 * block + 1, :], rows_ref[2 * block + 1 : 2 * block + 2, :]
        )

    def forward(block, chunk, masked):
        window = chunk_rows(chunk)
        scores = nt_dot(held[window, 0:256], q_spread[block])
        if masked:
            scores = jnp.where(mask_of(block, chunk), scores, NEG)
        old = top[block : block + 1, :]
        new = jnp.maximum(old, jnp.max(scores, axis=0, keepdims=True))
        probs = jnp.exp(scores - new)
        shrink = jnp.exp(old - new)
        top[block : block + 1, :] = new
        total[block : block + 1, :] = total[block : block + 1, :] * shrink + jnp.sum(
            probs, axis=0, keepdims=True
        )
        mixed[block] = mixed[block] * shrink + tn_dot(held[window, 128:384], probs.astype(bf16))

    def forward_step(chunk, carry):
        in_b = (chunk >= b_lo) & (chunk <= b_hi)

        @pl.when(needed(chunk, a_hi, b_lo, b_hi))
        def _():
            wait_chunk(chunk, held, sem)

        @pl.when(chunk < a_hi)
        def _():
            forward(0, chunk, False)

        @pl.when(chunk == a_hi)
        def _():
            forward(0, chunk, True)

        @pl.when(in_b)
        def _():
            forward(1, chunk, True)

        return carry

    lax.fori_loop(0, CHUNKS, forward_step, 0)
    for block in range(2):
        sums = total[block : block + 1, :]
        top[block : block + 1, :] = top[block : block + 1, :] + jnp.log(sums)
        mixed[block] = mixed[block] / sums
        unspread(mixed.at[block], att_ref, block, V_AT)

    attended = att_ref[...].astype(bf16)
    cotangent = c_ref[...]
    gain = gain_ref[...]
    for copy in weights:
        copy.wait()
    hidden = x_ref[...].astype(f32) + nn_dot(attended, wo_ref[...])
    normed = (hidden * rms_parts(hidden) * gain).astype(bf16)
    gate = nn_dot(normed, wg_ref[...])
    upward = nn_dot(normed, wu_ref[...])
    open_gate = jax.nn.sigmoid(gate)
    silu = gate * open_gate
    active = (silu * upward).astype(bf16)
    result_ref[...] = (hidden + nn_dot(active, wd_ref[...])).astype(bf16)
    grad_active = nt_dot(cotangent, wd_ref[...])
    grad_gate = (grad_active * upward * open_gate * (1.0 + gate * (1.0 - open_gate))).astype(bf16)
    grad_up = (grad_active * silu).astype(bf16)
    grad_normed = nt_dot(grad_gate, wg_ref[...]) + nt_dot(grad_up, wu_ref[...])
    by_hidden, by_gain = rms_back(hidden, gain, grad_normed)
    grad_hidden = cotangent.astype(f32) + by_hidden
    gh_ref[...] = grad_hidden
    grad_out = grad_hidden.astype(bf16)
    spread(nt_dot(grad_out, wo_ref[...]).astype(bf16), g_spread, V_AT)
    for block in range(2):
        turned = g_spread[block].astype(f32).T
        delta_ref[block : block + 1, :] = jnp.sum(turned * mixed[block], axis=0, keepdims=True)

    def pack(at, grads):
        rows = grads.shape[0]
        for tile in range(grads.shape[1] // 128):
            dw[at + tile * rows : at + (tile + 1) * rows, :] = grads[:, 128 * tile : 128 * tile + 128].astype(bf16)
        if grads.shape[1] % 128:
            tile = grads.shape[1] // 128
            dw[at + tile * rows : at + (tile + 1) * rows, 0:64] = grads[:, 128 * tile : 128 * tile + 64].astype(bf16)
            dw[at + tile * rows : at + (tile + 1) * rows, 64:128] = jnp.zeros((rows, 64), bf16)

    pack(GATE_AT, tn_dot(normed, grad_gate))
    pack(UP_AT, tn_dot(normed, grad_up))
    pack(DOWN_AT, tn_dot(active, cotangent))
    pack(OUT_AT, tn_dot(attended, grad_out))
    gain_rows[...] = jnp.zeros_like(gain_rows)
    for tile in range(4):
        gain_rows[tile : tile + 1, :] = by_gain[:, 128 * tile : 128 * tile + 128]
    gain_rows[4:5, 0:64] = by_gain[:, 512:576]
    dw[GAIN_AT : GAIN_AT + 16, :] = gain_rows[...].astype(bf16)
    dw[GAIN_AT + 16 : FF_ROWS, :] = jnp.zeros((FF_ROWS - GAIN_AT - 16, 128), bf16)
    band_rows = FF_ROWS // 3
    dw_copies = [
        pltpu.make_async_copy(dw.at[pl.ds(band * band_rows, band_rows)], dws[band], dw_sem.at[band])
        for band in range(3)
    ]
    for copy in dw_copies:
        copy.start()

    mixed[...] = jnp.zeros_like(mixed)

    def backward(block, chunk, masked, mode):
        window = chunk_rows(chunk)
        keys = held[window, 0:256]
        values = held[window, 128:384]
        scores = nt_dot(keys, q_spread[block])
        probs = jnp.exp(scores - top[block : block + 1, :])
        if masked:
            probs = jnp.where(mask_of(block, chunk), probs, 0.0)
        grad_probs = nt_dot(values, g_spread[block])
        grad_scores = (probs * (grad_probs - delta_ref[block : block + 1, :])).astype(bf16)
        mixed[block] += tn_dot(keys, grad_scores)
        dk = nn_dot(grad_scores, q_spread[block])
        dv = nn_dot(probs.astype(bf16), g_spread[block])
        parts = (dk[:, 0:128], dk[:, 128:256] + dv[:, 0:128], dv[:, 128:256])
        for band in range(3):
            at = slice(128 * band, 128 * band + 128)
            if mode == "first":
                staged[:, at] = parts[band]
            elif mode == "second":
                held[window, at] = (staged[:, at] + parts[band]).astype(bf16)
            else:
                held[window, at] = parts[band].astype(bf16)

    def zero_copy(band, row):
        return pltpu.make_async_copy(blank, dkvs[band].at[pl.ds(row, HALF)], blank_sem)

    def backward_step(chunk, carry):
        in_a = chunk <= a_hi
        in_b = (chunk >= b_lo) & (chunk <= b_hi)

        @pl.when((chunk < a_hi) & jnp.logical_not(in_b))
        def _():
            backward(0, chunk, False, "only")

        @pl.when((chunk == a_hi) & jnp.logical_not(in_b))
        def _():
            backward(0, chunk, True, "only")

        @pl.when(in_b & jnp.logical_not(in_a))
        def _():
            backward(1, chunk, True, "only")

        @pl.when(in_a & in_b)
        def _():
            backward(0, chunk, True, "first")
            backward(1, chunk, True, "second")

        use = in_a | in_b

        @pl.when(use)
        def _():
            for piece in range(PIECES):
                row = pl.multiple_of(source[chunk * PIECES + piece], HALF)
                rows = pl.ds(pl.multiple_of(chunk * CHUNK + piece * HALF, HALF), HALF)
                for band in range(3):
                    pltpu.make_async_copy(
                        held.at[rows, 128 * band : 128 * band + 128],
                        dkvs[band].at[pl.ds(row, HALF)],
                        out_sem.at[chunk],
                    ).start()

        @pl.when(jnp.logical_not(use))
        def _():
            for piece in range(PIECES):
                row = pl.multiple_of(source[chunk * PIECES + piece], HALF)
                for band in range(3):
                    zero_copy(band, row).start()

        return carry

    lax.fori_loop(0, CHUNKS, backward_step, 0)
    for block in range(2):
        unspread(mixed.at[block], dq_ref, block, K_AT)

    def drain(chunk, carry):
        use = needed(chunk, a_hi, b_lo, b_hi)

        @pl.when(use)
        def _():
            wait_chunk(chunk, held, out_sem)

        @pl.when(jnp.logical_not(use))
        def _():
            for _piece in range(PIECES):
                for band in range(3):
                    zero_copy(band, 0).wait()

        return carry

    lax.fori_loop(0, CHUNKS, drain, 0)
    for copy in dw_copies:
        copy.wait()


def layer(source, info, kvs, weights, q, row_info, x, cotangent, gain):
    vmem = pl.BlockSpec(memory_space=pltpu.VMEM)
    anywhere = pl.BlockSpec(memory_space=pl.ANY)
    return pl.pallas_call(
        layer_kernel,
        out_shape=(
            jax.ShapeDtypeStruct((ROWS, D), bf16),
            jax.ShapeDtypeStruct((ROWS, D), f32),
            jax.ShapeDtypeStruct((ROWS, D), f32),
        )
        + (jax.ShapeDtypeStruct((TOKENS, 128), bf16),) * 3
        + (jax.ShapeDtypeStruct((FF_ROWS // 3, 128), bf16),) * 3,
        grid_spec=pltpu.PrefetchScalarGridSpec(
            num_scalar_prefetch=2,
            in_specs=[anywhere] * 7 + [vmem] * 5,
            out_specs=(vmem,) * 3 + (anywhere,) * 6,
            scratch_shapes=[
                pltpu.VMEM((TOKENS, 384), bf16),
                pltpu.SemaphoreType.DMA((CHUNKS,)),
                pltpu.VMEM((D, D), bf16),
                pltpu.VMEM((D, FF), bf16),
                pltpu.VMEM((D, FF), bf16),
                pltpu.VMEM((FF, D), bf16),
                pltpu.SemaphoreType.DMA((4,)),
                pltpu.VMEM((2, COLS, 256), bf16),
                pltpu.VMEM((2, COLS, 256), bf16),
                pltpu.VMEM((2, 256, COLS), f32),
                pltpu.VMEM((2, COLS), f32),
                pltpu.VMEM((2, COLS), f32),
                pltpu.VMEM((ROWS, D), f32),
                pltpu.VMEM((2, COLS), f32),
                pltpu.VMEM((FF_ROWS, 128), bf16),
                pltpu.SemaphoreType.DMA((3,)),
                pltpu.VMEM((CHUNK, 384), f32),
                pltpu.VMEM((HALF, 128), bf16),
                pltpu.SemaphoreType.DMA((CHUNKS,)),
                pltpu.SemaphoreType.DMA,
                pltpu.VMEM((16, 128), f32),
            ],
        ),
        compiler_params=pltpu.CompilerParams(vmem_limit_bytes=VMEM_LIMIT),
        name="layer",
    )(source, info, *kvs, *weights, q, row_info, x, cotangent, gain)


SCATTERED = (ROWS, ROWS, ROWS, BAND_ROWS, BAND_ROWS, BAND_ROWS)
FINAL_ROWS = BAND_ROWS + BAND_ROWS_ONE


def scatter_scratch(rows):
    shapes = [pltpu.VMEM((SIDE, SIDE, SIDE, r, 128), bf16) for r in rows] * 2
    for r in rows:
        shapes += [
            pltpu.VMEM((4, SIDE, SIDE, r, 128), bf16),
            pltpu.VMEM((4, SIDE, r, 128), bf16),
            pltpu.VMEM((4, r, 128), bf16),
        ]
    count = len(rows) * 44
    return shapes + [
        pltpu.SemaphoreType.DMA((count,)),
        pltpu.SemaphoreType.DMA((count,)),
        pltpu.SemaphoreType.DMA((len(rows), SIDE)),
    ]


def reduce_kernel(*refs):
    dkv, dws = refs[0:3], refs[3:6]
    dq_ref, n_ref, x_ref, gh_ref, cos_ref, sin_ref, gain_ref, wq_ref, wk_ref, wv_ref = refs[6:16]
    gx_ref, outs = refs[16], refs[17:20]
    rest = refs[20:]
    done, rest = rest[:6], rest[6:]
    first, rest = rest[:33], rest[33:]
    parts, rest = rest[:3], rest[3:]
    done_one, rest = rest[:3], rest[3:]
    second, rest = rest[:18], rest[18:]
    own, rest = rest[:3], rest[3:]
    gain_rows, send, recv, local_sem = rest
    me, coords, core = whereabouts()
    greet(me, coords, core)
    scatter_bands(tuple(dkv) + tuple(dws), done, first)

    cos_wide, sin_wide = cos_ref[...], -sin_ref[...]
    tiles = [turn(dq_ref[:, 128 * t : 128 * t + 128] * SCALE, cos_wide, sin_wide).astype(bf16) for t in range(4)]
    mixed = turn(
        jnp.concatenate([done[1][:, 0:64], dq_ref[:, 512:576] * SCALE], 1), cos_wide, sin_wide
    ).astype(bf16)
    grad_q = jnp.concatenate(tiles + [mixed[:, 64:128]], 1)
    grad_k = jnp.concatenate([turn(done[0][...], cos_wide, sin_wide).astype(bf16), mixed[:, 0:64]], 1)
    grad_v = jnp.concatenate([done[2][...], done[1][:, 64:128]], 1).astype(bf16)
    normed = n_ref[...]
    features = x_ref[...].astype(f32)
    grad_normed = nt_dot(grad_q, wq_ref[...]) + nt_dot(grad_k, wk_ref[...]) + nt_dot(grad_v, wv_ref[...])
    by_x, by_gain = rms_back(features, gain_ref[...], grad_normed)
    gx_ref[...] = gh_ref[...] + by_x

    def put(at, rows16):
        block = at // 16
        band, device = divmod(block, N_CTX)
        index = (device // 32, device // 8 % 4, device // 2 % 4, device % 2)
        parts[band][index] = rows16

    def pack(at, grads):
        width = grads.shape[1]
        if width % 128:
            grads = jnp.concatenate([grads, jnp.zeros((D, 128 - width % 128), f32)], 1)
        grads = grads.astype(bf16)
        for tile in range(grads.shape[1] // 128):
            for row in range(0, D, 16):
                put(at + tile * D + row, grads[row : row + 16, 128 * tile : 128 * tile + 128])

    pack(Q_AT, tn_dot(normed, grad_q))
    pack(KV_AT, tn_dot(normed, jnp.concatenate([grad_k, grad_v], 1)))
    gain_rows[...] = jnp.zeros_like(gain_rows)
    for tile in range(4):
        gain_rows[tile : tile + 1, :] = by_gain[:, 128 * tile : 128 * tile + 128]
    gain_rows[4:5, 0:64] = by_gain[:, 512:576]
    put(GAIN_ONE_AT, gain_rows[...].astype(bf16))
    for at in range(GAIN_ONE_AT + 16, ATT_ROWS, 16):
        put(at, jnp.zeros((16, 128), bf16))
    scatter_bands(parts, done_one, second)
    for band in range(3):
        own[band][0:BAND_ROWS, :] = done[3 + band][...].astype(bf16)
        own[band][BAND_ROWS:FINAL_ROWS, :] = done_one[band][...].astype(bf16)
    gather_bands(own, outs, (send, recv), local_sem)


def reduce_all(dkvs, dws, dq, normed, x, grad_hidden, cos_wide, sin_wide, gain, wq, wk, wv):
    vmem = pl.BlockSpec(memory_space=pltpu.VMEM)
    anywhere = pl.BlockSpec(memory_space=pl.ANY)
    one = (BAND_ROWS_ONE,) * 3
    return pl.pallas_call(
        reduce_kernel,
        out_shape=(jax.ShapeDtypeStruct((ROWS, D), f32),)
        + (jax.ShapeDtypeStruct((SIDE, SIDE, SIDE, 2, FINAL_ROWS, 128), bf16),) * 3,
        in_specs=[anywhere] * 6 + [vmem] * 10,
        out_specs=(vmem,) + (anywhere,) * 3,
        scratch_shapes=[pltpu.VMEM((r, 128), f32) for r in SCATTERED]
        + scatter_scratch(SCATTERED)
        + [pltpu.VMEM((SIDE, SIDE, SIDE, 2, r, 128), bf16) for r in one]
        + [pltpu.VMEM((r, 128), f32) for r in one]
        + scatter_scratch(one)
        + [pltpu.VMEM((FINAL_ROWS, 128), bf16)] * 3
        + [
            pltpu.VMEM((16, 128), f32),
            pltpu.SemaphoreType.DMA((3 * 48,)),
            pltpu.SemaphoreType.DMA((3 * 48,)),
            pltpu.SemaphoreType.DMA((3,)),
        ],
        compiler_params=pltpu.CompilerParams(
            collective_id=2, has_side_effects=True, vmem_limit_bytes=VMEM_LIMIT
        ),
        name="reduce_all",
    )(*dkvs, *dws, dq, normed, x, grad_hidden, cos_wide, sin_wide, gain, wq, wk, wv)


def unpack_kernel(
    sums0, sums1, sums2,
    ga_ref, gq_ref, gk_ref, gv_ref, go_ref, gm_ref, gg_ref, gu_ref, gd_ref,
):
    sums = (sums0, sums1, sums2)

    def fetch(at, size):
        band, row = divmod(at, N_CTX * BAND_ROWS)
        device, row = divmod(row, BAND_ROWS)
        return sums[band][device, row : row + size, :].astype(f32)

    def fetch_one(at):
        band, row = divmod(at, N_CTX * BAND_ROWS_ONE)
        return sums[band][row // BAND_ROWS_ONE, BAND_ROWS:FINAL_ROWS, :].astype(f32)

    def fill(ref, at):
        rows, columns = ref.shape
        for tile in range((columns + 127) // 128):
            width = min(128, columns - 128 * tile)
            for row in range(0, rows, BAND_ROWS):
                piece = fetch(at + tile * rows + row, BAND_ROWS)
                ref[row : row + BAND_ROWS, 128 * tile : 128 * tile + width] = piece[:, 0:width]

    fill(gg_ref, GATE_AT)
    fill(gu_ref, UP_AT)
    fill(gd_ref, DOWN_AT)
    fill(go_ref, OUT_AT)
    for row in range(0, D, 16):
        rows = slice(row, row + 16)
        for tile in range(5):
            width = min(128, D - 128 * tile)
            gq_ref[rows, 128 * tile : 128 * tile + width] = fetch_one(Q_AT + tile * D + row)[:, 0:width]
        tiles = [fetch_one(KV_AT + tile * D + row) for tile in range(3)]
        gk_ref[rows, 0:128] = tiles[0]
        gk_ref[rows, 128:192] = tiles[1][:, 0:64]
        gv_ref[rows, :] = jnp.concatenate([tiles[1][:, 64:128], tiles[2]], 1)
    for ref, piece in ((gm_ref, fetch(GAIN_AT, 16)), (ga_ref, fetch_one(GAIN_ONE_AT))):
        for tile in range(5):
            width = min(128, D - 128 * tile)
            ref[:, 128 * tile : 128 * tile + width] = piece[tile : tile + 1, 0:width]


def unpack(sums):
    vmem = pl.BlockSpec(memory_space=pltpu.VMEM)
    shapes = ((1, D), (D, D), (D, 192), (D, 192), (D, D), (1, D), (D, FF), (D, FF), (FF, D))
    return pl.pallas_call(
        unpack_kernel,
        out_shape=tuple(jax.ShapeDtypeStruct(s, f32) for s in shapes),
        in_specs=[vmem] * 3,
        out_specs=(vmem,) * len(shapes),
        compiler_params=pltpu.CompilerParams(vmem_limit_bytes=VMEM_LIMIT),
        name="unpack",
    )(*[s.reshape(N_CTX, FINAL_ROWS, 128) for s in sums])


def on_device(
    layer_input,
    attn_gain,
    w_query,
    w_key,
    w_value,
    w_out,
    mlp_gain,
    w_gate,
    w_up,
    w_down,
    cotangent,
    segment_ids,
    pair_table,
):
    own_pair = pair_table[0]
    within = jnp.arange(ROWS, dtype=jnp.int32)
    blocks = jnp.where(within < HALF, own_pair, 2 * N_CTX - 1 - own_pair)
    places = blocks * HALF + within % HALF
    lanes = jnp.arange(128, dtype=jnp.int32)
    frequency = ROPE_THETA ** (-2.0 * (lanes % (HEAD_DIM // 2)).astype(f32) / HEAD_DIM)
    turned = places.astype(f32)[:, None] * frequency[None, :]
    cos_wide = jnp.cos(turned)
    sin_wide = jnp.sin(turned) * jnp.where(lanes % HEAD_DIM < HEAD_DIM // 2, -1.0, 1.0)[None, :]

    documents = jnp.arange(DOCS, dtype=jnp.int32)
    earlier = jnp.sum((segment_ids[None, :] < documents[:, None]).astype(f32), axis=1)
    meta = jnp.concatenate([own_pair.astype(f32)[None], earlier]).astype(bf16)
    meta = jnp.pad(meta[None, :], ((0, META - 1), (0, 128 - DOCS - 1)))
    gain_one, gain_two = attn_gain[None, :], mlp_gain[None, :]
    q_rot, normed, kv0, kv1, kv2 = project_and_gather(
        layer_input, gain_one, w_query, w_key, w_value, cos_wide, sin_wide, meta
    )
    metas = kv0.reshape(N_CTX, SLAB, 128)[:, ROWS, : DOCS + 1].astype(f32)
    pairs = metas[:, 0].astype(jnp.int32)
    starts = jnp.sum(metas[:, 1:], axis=0).astype(jnp.int32)
    numbers = jnp.arange(N_CTX, dtype=jnp.int32)
    holder = jnp.sum(jnp.where(pairs[None, :] == numbers[:, None], numbers[None, :], 0), axis=1)
    source = jnp.concatenate([holder * ROWS, holder[::-1] * ROWS + HALF])
    doc_start = jnp.sum(
        jnp.where(segment_ids[:, None] == documents[None, :], starts[None, :], 0), axis=1
    )
    row_info = jnp.tile(
        jnp.stack([places[:HALF], doc_start[:HALF], places[HALF:], doc_start[HALF:]]), (1, HEADS)
    )
    info = jnp.stack(
        [own_pair // PIECES, doc_start[HALF] // CHUNK, (2 * N_CTX - 1 - own_pair) // PIECES]
    )
    result, grad_hidden, dq, dkv0, dkv1, dkv2, dw0, dw1, dw2 = layer(
        source,
        info,
        [kv0.reshape(N_CTX * SLAB, 128), kv1.reshape(TOKENS, 128), kv2.reshape(TOKENS, 128)],
        [w_out, w_gate, w_up, w_down],
        q_rot,
        row_info,
        layer_input,
        cotangent,
        gain_two,
    )
    lead = (SIDE, SIDE, SIDE, 2)
    grad_x, *sums = reduce_all(
        [d.reshape(lead + (ROWS, 128)) for d in (dkv0, dkv1, dkv2)],
        [d.reshape(lead + (BAND_ROWS, 128)) for d in (dw0, dw1, dw2)],
        dq,
        normed,
        layer_input,
        grad_hidden,
        cos_wide,
        sin_wide,
        gain_one,
        w_query,
        w_key,
        w_value,
    )
    ga, gq, gk, gv, go, gm, gg, gu, gd = unpack(sums)
    return (result, grad_x, ga[0], gq, gk, gv, go, gm[0], gg, gu, gd)


def solution(mesh):
    return jax.shard_map(
        on_device,
        mesh=mesh,
        in_specs=(
            P("ctx", None),
            P(),
            P(),
            P(),
            P(),
            P(),
            P(),
            P(),
            P(),
            P(),
            P("ctx", None),
            P("ctx"),
            P("ctx"),
        ),
        out_specs=(P("ctx", None), P("ctx", None), P(), P(), P(), P(), P(), P(), P(), P(), P()),
        check_vma=False,
    )
```

time: 1240 us -> 274 us (0.22)
  matrix products: 488 us -> 0 us
  Pallas kernels: 0 us -> 235 us
  blocking collectives: 200 us -> 0 us
  local copies, waits for them, and re-layouts: 213 us -> 27.4 us
  other arithmetic: 138 us -> 6.55 us
  waiting for transfers between devices: 131 us -> 0 us
  loops' own time: 46.8 us -> 0 us
    dot_general x133 -> x0, matrix products: 488 us -> none  [the longest x48 161 us: masked_scores(): jnp.einsum('bgrd,tgd->grbt', query_heads, key_heads, preferred_element_ty...]
    pallas_call x0 -> x4, Pallas kernels: none -> 235 us  [the longest x1 148 us: reduce_all(): pl.pallas_call(reduce_kernel, out_shape=(jax.ShapeDtypeStruct((ROWS, D),...]
    all_gather x4 -> x0, blocking collectives: 135 us -> none  [the longest x1 36.2 us: on_device(): lax.all_gather(log_rows.astype(jnp.bfloat16), 'ctx', axis=0, tiled=True)]
    dynamic_slice x208 -> x0, local copies, waits for them, and re-layouts: 107 us -> none  [the longest x16 46.7 us: piece_step(): lax.dynamic_slice_in_dim(piece_grads, first_row, qblock, 0)]
    psum x1 -> x0, waiting for transfers between devices: 103 us -> none  [on_device(): lax.psum((grad_attn_gain, grad_w_query, grad_w_key, grad_w_value, grad_w_...]
    psum x1 -> x0, blocking collectives: 64.5 us -> none  [on_device(): lax.psum((grad_attn_gain, grad_w_query, grad_w_key, grad_w_value, grad_w_...]
    reduce_sum x18 -> x4, other arithmetic: 55.1 us -> 1.09 us  [the longest x1 0.77 us: on_device(): jnp.sum((segment_ids[None, :] < documents[:, None]).astype(f32), axis=1)]
    slice x48 -> x2, local copies, waits for them, and re-layouts: 54.3 us -> 1.57 us  [the longest x1 0.99 us: on_device(): metas = kv0.reshape(N_CTX, SLAB, 128)[:, ROWS, :DOCS + 1].astype(f32)]
  transfers between devices with their start and end apart: 4 -> 0, of which waited for: 2 -> 0; matrix products, arithmetic and copies ran while one was open for 37% -> 0% of each run, Pallas kernels for 0% -> 0%
where the time goes in v1:
time: 274 us; the launch traced here: 273 us
  Pallas kernels  235 us (86%)
  local copies, waits for them, and re-layouts  27.4 us (10%)
  other arithmetic  6.55 us (2%)
  between operations  4.17 us (2%)
    pallas_call x1, Pallas kernels, reduce_all(): pl.pallas_call(reduce_kernel, out_shape=(jax.ShapeDtypeStruct((ROWS, D),...  148 us
    pallas_call x1, Pallas kernels, project_and_gather(): pl.pallas_call(project_kernel, out_shape=(jax.ShapeDtypeStruct((ROWS, D),...  51.7 us
    pallas_call x1, Pallas kernels, layer(): pl.pallas_call(layer_kernel, out_shape=(jax.ShapeDtypeStruct((ROWS, D), b...  25.9 us
    unnamed x15, local copies, waits for them, and re-layouts  22.4 us
    pallas_call x1, Pallas kernels, unpack(): pl.pallas_call(unpack_kernel, out_shape=tuple((jax.ShapeDtypeStruct(s, f3...  8.92 us

profile of v1, /device:TPU:1, one launch (start us, length us, event | category | flops | bytes accessed | tf_op | source)
XLA Modules:
  0.0 273.2 jit_solution(3801452907755967584)
XLA Ops:
  0.6 0.0 copy-start
  1.5 0.8 convert_reduce_fusion
  2.3 0.1 slice_bitcast_fusion.3
  2.3 1.3 broadcast_in_dim.59.gain_ref.refs_12_
  3.6 1.3 broadcast_in_dim.68.gain_ref
  4.9 0.7 fusion.6.meta_ref
  5.6 1.0 fusion
  6.5 1.7 copy.54.x_ref.refs_8_
  8.2 1.7 copy.60.c_ref
  9.9 1.8 copy.55.wk_ref.refs_14_
  11.7 1.8 copy.56.wv_ref.refs_15_
  13.6 0.0 copy-done
  13.6 0.0 copy-start.1
  13.6 2.3 copy.58.wd_hbm
  15.9 51.7 %project_and_gather.1 = (bf16[128,576]{1,0:T(8,128)(2,1)}, bf16[128,576]{1,0:T(8,128)(2,1)}, bf16[4,4,4,2,144,128]{5,4,3,2,1,0:T(8,128)(2,1)}, bf16[4,4,4,2,128,...) custom-call(bf16[128,576]{1,0:T(8,128)(2,1)} %copy.54.x_ref.refs_8_, f32[1,576]{1,0:T(1,128)} %broadcast_in_dim.59.gain_ref.refs_12_, ...), custom_call_target="tpu_custom_call" | custom-call | tf_op jit(solution)/shard_map/project_and_gather/pallas_call | solution.py:398
  67.7 1.0 slice.32
  68.6 0.1 copy.69
  68.7 0.1 slice_reduce_fusion
  68.9 0.1 select_reduce_fusion
  69.0 0.0 copy-done.1
  69.0 0.1 select_reduce_fusion.1
  69.1 0.6 slice.27
  72.3 0.7 pad_add_fusion.2.info
  72.9 0.1 rev.3
  73.0 0.6 pad_add_fusion.1.source
  73.6 0.1 slice_bitcast_fusion.2
  73.7 0.7 tile.10.rows_ref
  74.4 25.9 %layer.1 = (bf16[128,576]{1,0:T(8,128)(2,1)}, f32[128,576]{1,0:T(8,128)}, f32[128,576]{1,0:T(8,128)}, bf16[16384,128]{1,0:T(8,128)(2,1)}, bf16[16384,128]{1,0:T(...) custom-call(s32[256]{0:T(256)} %pad_add_fusion.1.source, ...), custom_call_target="tpu_custom_call" | custom-call | tf_op jit(solution)/shard_map/layer/pallas_call | solution.py:696
  100.3 1.7 copy.64
  102.0 148.5 %reduce_all.1 = (f32[128,576]{1,0:T(8,128)}, bf16[4,4,4,2,80,128]{5,4,3,2,1,0:T(8,128)(2,1)}, bf16[4,4,4,2,80,128]{5,4,3,2,1,0:T(8,128)(2,1)}, bf16[4,4,4,2,80,128]{5,4,3,2,1,0:T(8,128)(2,1)}) custom-call(bf16[4,4,4,2,128,128]{5,4,3,2,1,0:T(8,128)(2,1)} %bitcast.46, bf16[4,4,4,2,128,128]{5,4,3,2,1,0:T(8,128)(2,1)} %bitcast.47, ...), custom_call_target="tpu_custom_call" | custom-call | tf_op jit(solution)/shard_map/reduce_all/pallas_call | solution.py:823
  250.5 1.8 copy.65
  252.3 8.9 %unpack.1 = (f32[1,576]{1,0:T(1,128)}, f32[576,576]{1,0:T(8,128)}, f32[576,192]{1,0:T(8,128)}, f32[576,192]{1,0:T(8,128)}, f32[576,576]{1,0:T(8,128)}, /*index=5...) custom-call(bf16[128,80,128]{2,1,0:T(8,128)(2,1)} %bitcast.49, ...), custom_call_target="tpu_custom_call" | custom-call | tf_op jit(solution)/shard_map/unpack/pallas_call | solution.py:893
  261.3 1.3 reduce
  262.5 1.3 reduce.1
  263.8 2.1 copy.66
  265.9 2.1 copy.67
  267.9 5.3 %copy.68 = f32[1536,576]{0,1:T(8,128)} copy(f32[1536,576]{1,0:T(8,128)} %get-tuple-element.97) | data formatting | bytes 7077888
  (9 shorter events, 0.1 us)
Async XLA Ops:
  0.6 12.9 %copy-start = (bf16[1536,576]{0,1:T(8,128)(2,1)S(1)}, bf16[1536,576]{0,1:T(8,128)(2,1)}, u32[]{:S(2)}) copy-start(bf16[1536,576]{0,1:T(8,128)(2,1)} %param.22) | copy-start | bytes 5308420
  13.6 55.4 %copy-start.1 = (s32[128]{0:T(128)S(1)}, s32[128]{0:T(128)}, u32[]{:S(2)}) copy-start(s32[128]{0:T(128)} %param.24) | copy-start | bytes 1540

commit v2 on v1

v2 whole, which is shorter than its diff:
```python
import functools
import jax
import jax.numpy as jnp
from jax import lax
from jax.experimental import pallas as pl
from jax.experimental.pallas import tpu as pltpu
from jax.sharding import PartitionSpec as P

f32 = jnp.float32
bf16 = jnp.bfloat16
D = 576
HEADS = 9
KV_HEADS = 3
HEAD_DIM = 64
PER_GROUP = HEADS // KV_HEADS
FF = 1536
NORM_EPS = 1e-05
ROPE_THETA = 100000.0
ROWS = 128
HALF = 64
N_CTX = 128
TOKENS = ROWS * N_CTX
DOCS = 18
META = 16
SLAB = ROWS + META
CHUNK = 512
PIECES = CHUNK // HALF
CHUNKS = TOKENS // CHUNK
COLS = HEADS * HALF
NEG = -1e30
SCALE = HEAD_DIM ** (-0.5)
VMEM_LIMIT = 56 * 1024 * 1024

K_AT = (0, 64, 128)
V_AT = (128, 192, 64)

GATE_AT = 0
UP_AT = GATE_AT + 12 * D
DOWN_AT = UP_AT + 12 * D
OUT_AT = DOWN_AT + 12 * D
GAIN_AT = OUT_AT + 5 * D
BAND_ROWS = 64
FF_ROWS = 3 * N_CTX * BAND_ROWS
Q_AT = 0
KV_AT = Q_AT + 5 * D
GAIN_ONE_AT = KV_AT + 5 * 384
BAND_ROWS_ONE = 16
ATT_ROWS = 3 * N_CTX * BAND_ROWS_ONE

MESH = pl.DeviceIdType.MESH
SIDE = 4
ORDERS = ((2, 1, 0), (1, 0, 2), (0, 2, 1))
STRIDES = (32, 8, 2)


def whereabouts():
    me = lax.axis_index("ctx")
    coords = (me // 32, lax.rem(me // 8, SIDE), lax.rem(me // 2, SIDE))
    return me, coords, lax.rem(me, 2)


def wrap(coord, step):
    return lax.rem(coord + (step + SIDE), SIDE)


def neighbour(me, coords, axis, step):
    return me + (wrap(coords[axis], step) - coords[axis]) * STRIDES[axis]


def greet(me, coords, core):
    barrier = pltpu.get_barrier_semaphore()
    others = [me + 1 - 2 * core]
    for axis in range(3):
        others += [neighbour(me, coords, axis, step) for step in (1, -1, 2)]
    for other in others:
        pl.semaphore_signal(barrier, inc=1, device_id=(other,), device_id_type=MESH)
    pl.semaphore_wait(barrier, len(others))


def half_rows(rows):
    return rows // 32 * 16


class Pool:
    def __init__(self, sems):
        self.sems = sems
        self.used = 0

    def new(self):
        self.used += 1
        return self.sems.at[self.used - 1]


def send(src, dst, device, send_sem, recv_sem):
    pltpu.make_async_remote_copy(
        src_ref=src,
        dst_ref=dst,
        send_sem=send_sem,
        recv_sem=recv_sem,
        device_id=(device,),
        device_id_type=MESH,
    ).start()


def wait_for(ref, sem):
    pltpu.make_async_copy(ref, ref, sem).wait()


def at_axes(order, values):
    index = [None] * 3
    for axis, value in zip(order, values):
        index[axis] = value
    return tuple(index)


WHOLE = pl.ds(0, SIDE)


def gather_steps(own, out, pool, ring=True):
    me, coords, core = whereabouts()
    sibling = me + 1 - 2 * core
    bands = range(len(own))
    orders = [ORDERS[band % 3] for band in bands]
    lines = (0, 1, -1, 2)
    steps = (1, -1, 2)

    def place(band, *values):
        return out[band].at[at_axes(orders[band], values) + (core,)]

    def mine(band, phase, step=0):
        return wrap(coords[orders[band][phase]], step)

    def device(band, phase, step):
        return neighbour(me, coords, orders[band][phase], step)

    homes = [pool.new() for band in bands]
    sent = [[pool.new() for phase in range(3)] for band in bands]
    across = [(pool.new(), pool.new()) for band in bands]
    came = [[pool.new() for phase in range(3)] for band in bands]
    ends = {}
    for step in steps:
        for phase in (1, 0):
            for band in bands:
                part = place(band, *(mine(band, p) for p in range(3)))
                send(own[band], part, device(band, phase, step), sent[band][0], came[band][phase])
    for band in bands:
        part = place(band, *(mine(band, p) for p in range(3)))
        pltpu.make_async_copy(own[band], part, homes[band]).start()

    def send_line(band, line):
        part = place(band, mine(band, 0, line), WHOLE, mine(band, 2))
        if ring:
            ends[band, line] = (pool.new(), pool.new(), pool.new())
            send(part, part, device(band, 2, 1), sent[band][2], ends[band, line][0])
            send(part, part, device(band, 2, -1), sent[band][2], ends[band, line][1])
        else:
            if line == 0:
                ends[band] = pool.new()
            for step in steps:
                send(part, part, device(band, 2, step), sent[band][2], ends[band])

    yield
    for band in bands:
        wait_for(own[band], homes[band])
        wait_for(out[band].at[0, 0, 0:3, 0], came[band][1])
        send_line(band, 0)
    for band in bands:
        wait_for(out[band].at[0, 0, 0:3, 0], came[band][0])
        for line in lines[1:]:
            part = place(band, mine(band, 0, line), mine(band, 1), mine(band, 2))
            for step in steps:
                send(part, part, device(band, 1, step), sent[band][1], came[band][2])
    yield
    for band in bands:
        wait_for(out[band].at[0, 0:3, 0:3, 0], came[band][2])
        for line in lines[1:]:
            send_line(band, line)
    for band in bands:
        part = place(band, WHOLE, WHOLE, mine(band, 2))
        send(part, part, sibling, *across[band])
    if ring:
        for line in lines:
            yield
            for band in bands:
                rows = own[band].shape[0]
                cut = half_rows(rows)
                for side, step, lo, size in ((0, -1, 0, cut), (1, 1, cut, rows - cut)):
                    part = place(band, mine(band, 0, line), WHOLE, mine(band, 2, step))
                    wait_for(part, ends[band, line][side])
                    half = part.at[:, pl.ds(lo, size)]
                    send(half, half, device(band, 2, -step), sent[band][2], ends[band, line][2])
                    send(part, part, sibling, *across[band])
        for line in lines:
            yield
            for band in bands:
                part = place(band, mine(band, 0, line), WHOLE, mine(band, 2, 2))
                wait_for(part, ends[band, line][2])
                send(part, part, sibling, *across[band])
    else:
        yield
        for band in bands:
            wait_for(out[band].at[0:3, :, :, 0], ends[band])
            for step in steps:
                part = place(band, WHOLE, WHOLE, mine(band, 2, step))
                send(part, part, sibling, *across[band])
    yield
    for band in bands:
        wait_for(out[band].at[:, :, :, 0], across[band][1])
        wait_for(out[band].at[:, :, :, 0], across[band][0])
        wait_for(out[band].at[0, 0:2, 0:3, 0], sent[band][0])
        wait_for(out[band].at[0, 0:3, 0:3, 0], sent[band][1])
        wait_for(out[band].at[0:3, :, :, 0], sent[band][2])


GATHER_SEMS = 3 * (1 + 3 + 2 + 3 + 12)
GATHER_SEMS_ONE = 3 * (1 + 3 + 2 + 3 + 1)


def run(steps):
    for _ in steps:
        pass


def scatter_scratch(rows, ring):
    shapes = [pltpu.VMEM((SIDE, SIDE, SIDE, rows, 128), bf16)] * 6
    for _ in range(3):
        shapes += [
            pltpu.VMEM((3, SIDE, SIDE, rows, 128), bf16),
            pltpu.VMEM((3, SIDE, rows, 128), bf16),
            pltpu.VMEM((3, rows, 128), bf16),
        ]
    return shapes + [pltpu.SemaphoreType.DMA((3 * (4 + 16 + 4 + 8 + 2 if ring else 4 + 1 + 1 + 3),))]


SCATTER_REFS = 16


def scatter_steps(parts, done, scratch, ring):
    acc, sib = scratch[0:3], scratch[3:6]
    landing = [scratch[6 + 3 * b : 9 + 3 * b] for b in range(3)]
    pool = Pool(scratch[15])
    me, coords, core = whereabouts()
    sibling = me + 1 - 2 * core
    bands = range(3)
    steps = (2, 1, -1, 0)
    rows = acc[0].shape[3]
    cut = half_rows(rows)
    sent = [[pool.new() for phase in range(4)] for band in bands]
    homes, swaps = {}, {}
    if ring:
        for step in steps:
            for band in bands:
                order = ORDERS[band]
                plane = at_axes(order, (wrap(coords[order[0]], step), WHOLE, WHOLE))
                homes[band, step] = pool.new()
                top = 0
                for part in parts[band]:
                    size = part.shape[4]
                    pltpu.make_async_copy(
                        part.at[plane + (core,)],
                        acc[band].at[plane + (pl.ds(top, size),)],
                        homes[band, step],
                    ).start()
                    top += size
            for sub in range(SIDE):
                for band in bands:
                    order = ORDERS[band]
                    line = at_axes(order, (wrap(coords[order[0]], step), sub, WHOLE))
                    swaps[band, step, sub] = pool.new()
                    top = 0
                    for part in parts[band]:
                        size = part.shape[4]
                        send(
                            part.at[line + (1 - core,)],
                            sib[band].at[line + (pl.ds(top, size),)],
                            sibling,
                            sent[band][3],
                            swaps[band, step, sub],
                        )
                        top += size
    else:
        for band in bands:
            homes[band], swaps[band] = pool.new(), pool.new()
            (part,) = parts[band]
            pltpu.make_async_copy(part.at[:, :, :, core], acc[band], homes[band]).start()
            send(part.at[:, :, :, 1 - core], sib[band], sibling, sent[band][3], swaps[band])

    def add_swap(band, step, sub):
        order = ORDERS[band]
        first = wrap(coords[order[0]], step)
        if sub == 0:
            plane = acc[band].at[at_axes(order, (first, WHOLE, WHOLE))]
            wait_for(plane, homes[band, step])
        wait_for(sib[band].at[at_axes(order, (first, sub, WHOLE))], swaps[band, step, sub])

        def body(last, carry):
            at = at_axes(order, (first, sub, last))
            acc[band][at] = acc[band][at] + sib[band][at]
            return carry

        lax.fori_loop(0, SIDE, body, 0)

    jobs = [(sub, band) for sub in range(SIDE) for band in bands]

    def line_at(band, step, sub):
        order = ORDERS[band]
        return at_axes(order, (wrap(coords[order[0]], step), sub, WHOLE))

    def sum_up(band, index_of, landed):
        def body(last, carry):
            at = index_of(last)
            total = acc[band][at].astype(f32)
            for ref in landed(last):
                total = total + ref.astype(f32)
            acc[band][at] = total.astype(bf16)
            return carry

        lax.fori_loop(0, SIDE, body, 0)

    if ring:
        passing, ending = {}, {}
        for sub, band in jobs:
            if band == 0:
                yield
            axis = ORDERS[band][0]
            add_swap(band, 2, sub)
            far = acc[band].at[line_at(band, 2, sub)]
            passing[sub, band], ending[sub, band] = pool.new(), pool.new()
            for slot, lo, size, step in ((0, 0, cut, 1), (0, cut, rows - cut, -1)):
                send(
                    far.at[:, pl.ds(lo, size)],
                    landing[band][0].at[slot, sub, :, pl.ds(lo, size)],
                    neighbour(me, coords, axis, step),
                    sent[band][0],
                    passing[sub, band],
                )
        for sub, band in jobs:
            if band == 0:
                yield
            axis = ORDERS[band][0]
            add_swap(band, 1, sub)
            add_swap(band, -1, sub)
            wait_for(landing[band][0].at[0, sub], passing[sub, band])
            for slot, lo, size, step in ((1, 0, cut, 1), (2, cut, rows - cut, -1)):

                def body(last, carry, lo=lo, size=size, step=step):
                    order = ORDERS[band]
                    at = at_axes(order, (wrap(coords[order[0]], step), sub, last)) + (pl.ds(lo, size),)
                    acc[band][at] = acc[band][at] + landing[band][0][0, sub, last, lo : lo + size]
                    return carry

                lax.fori_loop(0, SIDE, body, 0)
                send(
                    acc[band].at[line_at(band, step, sub)],
                    landing[band][0].at[slot, sub],
                    neighbour(me, coords, axis, step),
                    sent[band][0],
                    ending[sub, band],
                )
        for sub, band in jobs:
            if band == 0:
                yield
            order = ORDERS[band]
            add_swap(band, 0, sub)
            wait_for(landing[band][0].at[1:3, sub], ending[sub, band])
            sum_up(
                band,
                lambda last: at_axes(order, (coords[order[0]], sub, last)),
                lambda last: [landing[band][0][slot, sub, last] for slot in (1, 2)],
            )
    else:
        came = [pool.new() for band in bands]
        yield
        for band in bands:
            axis = ORDERS[band][0]
            wait_for(acc[band], homes[band])
            wait_for(sib[band], swaps[band])
            acc[band][...] = acc[band][...] + sib[band][...]
            for slot, step in enumerate((2, 1, -1)):
                plane = at_axes(ORDERS[band], (wrap(coords[axis], step), WHOLE, WHOLE))
                send(
                    acc[band].at[plane],
                    landing[band][0].at[slot],
                    neighbour(me, coords, axis, step),
                    sent[band][0],
                    came[band],
                )
        yield
        for band in bands:
            plane = at_axes(ORDERS[band], (coords[ORDERS[band][0]], WHOLE, WHOLE))
            wait_for(landing[band][0], came[band])
            total = acc[band][plane].astype(f32)
            for slot in range(3):
                total = total + landing[band][0][slot].astype(f32)
            acc[band][plane] = total.astype(bf16)
    came = [pool.new() for band in bands]
    for slot, step in enumerate((2, 1, -1)):
        for band in bands:
            order = ORDERS[band]
            line = at_axes(order, (coords[order[0]], wrap(coords[order[1]], step), WHOLE))
            send(
                acc[band].at[line],
                landing[band][1].at[slot],
                neighbour(me, coords, order[1], step),
                sent[band][1],
                came[band],
            )
    yield
    ends = [pool.new() for band in bands]
    for band in bands:
        order = ORDERS[band]
        wait_for(landing[band][1], came[band])
        sum_up(
            band,
            lambda last: at_axes(order, (coords[order[0]], coords[order[1]], last)),
            lambda last: [landing[band][1][slot, last] for slot in range(3)],
        )
        for slot, step in enumerate((2, 1, -1)):
            at = at_axes(order, (coords[order[0]], coords[order[1]], wrap(coords[order[2]], step)))
            send(
                acc[band].at[at],
                landing[band][2].at[slot],
                neighbour(me, coords, order[2], step),
                sent[band][2],
                ends[band],
            )
    yield
    for band in bands:
        wait_for(landing[band][2], ends[band])
        total = acc[band][coords].astype(f32)
        for slot in range(3):
            total = total + landing[band][2][slot].astype(f32)
        done[band][...] = total
    for band in bands:
        wait_for(acc[band].at[0:3], sent[band][0])
        wait_for(acc[band].at[0, 0:3], sent[band][1])
        wait_for(acc[band].at[0, 0, 0:3], sent[band][2])
        wait_for(acc[band], sent[band][3])


def rms_parts(features):
    return lax.rsqrt(jnp.mean(features * features, axis=-1, keepdims=True) + NORM_EPS)


def rms_back(features, gain, grad):
    inverse = rms_parts(features)
    scaled = grad * gain
    inner = jnp.mean(scaled * features, axis=-1, keepdims=True)
    by_features = inverse * scaled - features * (inverse * inverse * inverse * inner)
    by_gain = jnp.sum(grad * features * inverse, axis=0, keepdims=True)
    return by_features, by_gain


def nt_dot(left, right):
    return lax.dot_general(left, right, (((1,), (1,)), ((), ())), preferred_element_type=f32)


def tn_dot(left, right):
    return lax.dot_general(left, right, (((0,), (0,)), ((), ())), preferred_element_type=f32)


def nn_dot(left, right):
    return jnp.dot(left, right, preferred_element_type=f32)


def turn(tile, cos_wide, sin_wide):
    lanes = lax.broadcasted_iota(jnp.int32, tile.shape, 1)
    swapped = jnp.where(
        lax.rem(lanes, HEAD_DIM) < HEAD_DIM // 2, pltpu.roll(tile, 96, 1), pltpu.roll(tile, 32, 1)
    )
    return tile * cos_wide + swapped * sin_wide


def project_kernel(
    pair_ref, x_ref, gain_ref, wq_ref, wk_ref, wv_ref, cos_ref, sin_ref, seg_ref,
    q_ref, n_ref, out0, out1, out2,
    own0, own1, own2, sems,
):
    me, coords, core = whereabouts()
    features = x_ref[...].astype(f32).T
    normed = (features * rms_parts(features) * gain_ref[...].reshape(1, D)).astype(bf16)
    n_ref[...] = normed
    cos_wide, sin_wide = cos_ref[...], sin_ref[...]
    keys = nt_dot(normed, wk_ref[...])
    values = nt_dot(normed, wv_ref[...]).astype(bf16)
    queries = nn_dot(normed, wq_ref[...])
    own0[0:ROWS, :] = turn(keys[:, 0:128], cos_wide, sin_wide).astype(bf16)
    segments = jnp.broadcast_to(seg_ref[...].astype(f32), (ROWS, ROWS)).T
    lanes = lax.broadcasted_iota(jnp.int32, (ROWS, ROWS), 1)
    earlier = jnp.sum(jnp.where(segments < (lanes - 1).astype(f32), 1.0, 0.0), axis=0, keepdims=True)
    meta = jnp.where(lanes[0:1] == 0, pair_ref[0].astype(f32), earlier)
    own0[ROWS:SLAB, :] = jnp.broadcast_to(meta, (META, 128)).astype(bf16)
    mixed = turn(jnp.concatenate([keys[:, 128:192], queries[:, 512:576]], 1), cos_wide, sin_wide)
    own1[...] = jnp.concatenate([mixed[:, 0:64].astype(bf16), values[:, 128:192]], 1)
    own2[...] = values[:, 0:128]
    greet(me, coords, core)
    steps = gather_steps((own0, own1, own2), (out0, out1, out2), Pool(sems))
    next(steps)
    for tile in range(4):
        at = slice(128 * tile, 128 * tile + 128)
        q_ref[:, at] = (turn(queries[:, at], cos_wide, sin_wide).astype(bf16).astype(f32) * SCALE).astype(bf16)
    q_ref[:, 512:576] = (mixed[:, 64:128].astype(bf16).astype(f32) * SCALE).astype(bf16)
    run(steps)


def project_and_gather(pair, x, gain, wq, wk, wv, cos_wide, sin_wide, segments):
    vmem = pl.BlockSpec(memory_space=pltpu.VMEM)
    anywhere = pl.BlockSpec(memory_space=pl.ANY)
    rows = (SLAB, ROWS, ROWS)
    return pl.pallas_call(
        project_kernel,
        out_shape=(
            jax.ShapeDtypeStruct((ROWS, D), bf16),
            jax.ShapeDtypeStruct((ROWS, D), bf16),
        )
        + tuple(jax.ShapeDtypeStruct((SIDE, SIDE, SIDE, 2, r, 128), bf16) for r in rows),
        in_specs=[pl.BlockSpec(memory_space=pltpu.SMEM)] + [vmem] * 8,
        out_specs=(vmem, vmem, anywhere, anywhere, anywhere),
        scratch_shapes=[pltpu.VMEM((r, 128), bf16) for r in rows]
        + [pltpu.SemaphoreType.DMA((GATHER_SEMS,))],
        compiler_params=pltpu.CompilerParams(
            collective_id=1, has_side_effects=True, vmem_limit_bytes=VMEM_LIMIT
        ),
        name="project_and_gather",
    )(pair, x, gain, wq, wk, wv, cos_wide, sin_wide, segments)


def needed(chunk, a_hi, b_lo, b_hi):
    return (chunk <= a_hi) | ((chunk >= b_lo) & (chunk <= b_hi))


def chunk_rows(chunk, count=1):
    return pl.ds(pl.multiple_of(chunk * CHUNK, CHUNK), count * CHUNK)


def wait_chunk(chunk, held, sem):
    window = held.at[chunk_rows(chunk)]
    pltpu.make_async_copy(window, window, sem.at[chunk]).wait()


def chunk_mask(chunk, place_row, start_row):
    keys = chunk * CHUNK + lax.broadcasted_iota(jnp.int32, (CHUNK, COLS), 0)
    return (keys <= place_row) & (keys >= start_row)


def layer_kernel(
    pair_ref,
    kv0, kv1, kv2, wo_hbm, wg_hbm, wu_hbm, wd_hbm,
    q_ref, seg_ref, x_ref, c_ref, gain_ref,
    result_ref, gh_ref, dq_ref, dkv0, dkv1, dkv2, dw0, dw1, dw2,
    held, sem, wo_ref, wg_ref, wu_ref, wd_ref, w_sem, q_spread, g_spread, mixed, top, total, att_ref,
    delta_ref, dw, dw_sem, staged, blank, out_sem, blank_sem, gain_rows,
    rows_ref, meta_ref, meta_sem, table_ref, table,
):
    kvs, dkvs, dws = (kv0, kv1, kv2), (dkv0, dkv1, dkv2), (dw0, dw1, dw2)
    weights = [
        pltpu.make_async_copy(src, dst, w_sem.at[i])
        for i, (src, dst) in enumerate(
            ((wo_hbm, wo_ref), (wg_hbm, wg_ref), (wu_hbm, wu_ref), (wd_hbm, wd_ref))
        )
    ]
    metas = pltpu.make_async_copy(kv0.at[:, pl.ds(ROWS, META)], meta_ref, meta_sem.at[0])
    metas.start()
    for copy in weights:
        copy.start()
    pair = pair_ref[0]
    metas.wait()
    columns = meta_ref[:, 0, :].astype(f32)
    starts = jnp.sum(columns, axis=0, keepdims=True)
    numbers = lax.broadcasted_iota(jnp.int32, (N_CTX, N_CTX), 0).astype(f32)
    lanes = lax.broadcasted_iota(jnp.int32, (N_CTX, N_CTX), 1).astype(f32)
    holders = jnp.sum(jnp.where(columns[:, 0:1] == lanes, numbers, 0.0), axis=0, keepdims=True)
    segments = seg_ref[...].astype(f32)
    row_starts = jnp.zeros((1, ROWS), f32)
    for document in range(DOCS):
        row_starts = jnp.where(
            segments == float(document), starts[:, document + 1 : document + 2], row_starts
        )
    for block in range(2):
        first = pair if block == 0 else 2 * N_CTX - 1 - pair
        places = first * HALF + lax.rem(lax.broadcasted_iota(jnp.int32, (1, COLS), 1), HALF)
        rows_ref[2 * block : 2 * block + 1, :] = places
        mine = row_starts[:, block * HALF : (block + 1) * HALF].astype(jnp.int32)
        rows_ref[2 * block + 1 : 2 * block + 2, :] = jnp.concatenate([mine] * HEADS, 1)
    table_ref[...] = jnp.zeros_like(table_ref)
    table_ref[0:1, :] = holders.astype(jnp.int32)
    table_ref[1:2, :] = row_starts.astype(jnp.int32)
    tables = pltpu.make_async_copy(table_ref, table, meta_sem.at[1])
    tables.start()
    tables.wait()
    a_hi, b_lo, b_hi = pair // PIECES, table[1, HALF] // CHUNK, (2 * N_CTX - 1 - pair) // PIECES

    def slot_of(block_number):
        low = table[0, jnp.minimum(block_number, 2 * N_CTX - 1 - block_number)]
        return low * ROWS + jnp.where(block_number < N_CTX, 0, HALF)


    def issue(chunk, carry):
        @pl.when(needed(chunk, a_hi, b_lo, b_hi))
        def _():
            for piece in range(PIECES):
                slot = slot_of(chunk * PIECES + piece)
                rows = pl.ds(pl.multiple_of(chunk * CHUNK + piece * HALF, HALF), HALF)
                device, top = slot // ROWS, pl.multiple_of(lax.rem(slot, ROWS), HALF)
                for band in range(3):
                    pltpu.make_async_copy(
                        kvs[band].at[device, pl.ds(top, HALF)],
                        held.at[rows, 128 * band : 128 * band + 128],
                        sem.at[chunk],
                    ).start()

        return carry

    lax.fori_loop(0, CHUNKS, issue, 0)

    def spread(rows, place, windows):
        for block in range(2):
            for head in range(HEADS):
                tile = rows[block * HALF : (block + 1) * HALF, head * HEAD_DIM : (head + 1) * HEAD_DIM]
                at = windows[head // PER_GROUP]
                place[block, head * HALF : (head + 1) * HALF, at : at + HEAD_DIM] = tile

    def unspread(columns, place, block, windows):
        for head in range(HEADS):
            at = windows[head // PER_GROUP]
            tile = columns[at : at + HEAD_DIM, head * HALF : (head + 1) * HALF]
            place[block * HALF : (block + 1) * HALF, head * HEAD_DIM : (head + 1) * HEAD_DIM] = tile.T

    blank[...] = jnp.zeros_like(blank)

    def zero_copy(band, row):
        return pltpu.make_async_copy(blank, dkvs[band].at[pl.ds(row, HALF)], blank_sem)

    def clear(chunk, carry):
        @pl.when(jnp.logical_not(needed(chunk, a_hi, b_lo, b_hi)))
        def _():
            for piece in range(PIECES):
                row = pl.multiple_of(slot_of(chunk * PIECES + piece), HALF)
                for band in range(3):
                    zero_copy(band, row).start()

        return carry

    lax.fori_loop(0, CHUNKS, clear, 0)
    q_spread[...] = jnp.zeros_like(q_spread)
    g_spread[...] = jnp.zeros_like(g_spread)
    spread(q_ref[...], q_spread, K_AT)
    mixed[...] = jnp.zeros_like(mixed)
    top[...] = jnp.full_like(top, NEG)
    total[...] = jnp.zeros_like(total)

    def mask_of(block, chunk):
        return chunk_mask(
            chunk, rows_ref[2 * block : 2 * block + 1, :], rows_ref[2 * block + 1 : 2 * block + 2, :]
        )

    def forward(block, chunk, masked, count=1):
        window = chunk_rows(chunk, count)
        scores = nt_dot(held[window, 0:256], q_spread[block])
        if masked:
            scores = jnp.where(mask_of(block, chunk), scores, NEG)
        old = top[block : block + 1, :]
        new = jnp.maximum(old, jnp.max(scores, axis=0, keepdims=True))
        probs = jnp.exp(scores - new)
        shrink = jnp.exp(old - new)
        top[block : block + 1, :] = new
        total[block : block + 1, :] = total[block : block + 1, :] * shrink + jnp.sum(
            probs, axis=0, keepdims=True
        )
        values = held[window, 128:384].T[64:256]
        mixed[block, 64:256] = mixed[block, 64:256] * shrink + nn_dot(values, probs.astype(bf16))

    def forward_step(chunk, carry):
        in_b = (chunk >= b_lo) & (chunk <= b_hi)

        @pl.when(needed(chunk, a_hi, b_lo, b_hi))
        def _():
            wait_chunk(chunk, held, sem)

        @pl.when(chunk <= a_hi)
        def _():
            forward(0, chunk, True)

        @pl.when(in_b)
        def _():
            forward(1, chunk, True)

        return carry

    def forward_pair(pair_of, carry):
        wait_chunk(2 * pair_of, held, sem)
        wait_chunk(2 * pair_of + 1, held, sem)
        forward(0, 2 * pair_of, False, 2)
        return carry

    plain = jnp.minimum(a_hi, b_lo) // 2
    lax.fori_loop(0, plain, forward_pair, 0)
    lax.fori_loop(2 * plain, b_hi + 1, forward_step, 0)
    for block in range(2):
        sums = total[block : block + 1, :]
        top[block : block + 1, :] = top[block : block + 1, :] + jnp.log(sums)
        mixed[block] = mixed[block] / sums
        unspread(mixed.at[block], att_ref, block, V_AT)

    attended = att_ref[...].astype(bf16)
    cotangent = c_ref[...].astype(f32).T.astype(bf16)
    gain = gain_ref[...].reshape(1, D)
    for copy in weights:
        copy.wait()
    hidden = x_ref[...].astype(f32).T + nn_dot(attended, wo_ref[...])
    normed = (hidden * rms_parts(hidden) * gain).astype(bf16)
    gate = nn_dot(normed, wg_ref[...])
    upward = nn_dot(normed, wu_ref[...])
    open_gate = jax.nn.sigmoid(gate)
    silu = gate * open_gate
    active = (silu * upward).astype(bf16)
    result_ref[...] = (hidden + nt_dot(active, wd_ref[...])).T.astype(bf16)
    grad_active = nn_dot(cotangent, wd_ref[...])
    grad_gate = (grad_active * upward * open_gate * (1.0 + gate * (1.0 - open_gate))).astype(bf16)
    grad_up = (grad_active * silu).astype(bf16)
    grad_normed = nt_dot(grad_gate, wg_ref[...]) + nt_dot(grad_up, wu_ref[...])
    by_hidden, by_gain = rms_back(hidden, gain, grad_normed)
    grad_hidden = cotangent.astype(f32) + by_hidden
    gh_ref[...] = grad_hidden
    grad_out = grad_hidden.astype(bf16)
    spread(nt_dot(grad_out, wo_ref[...]).astype(bf16), g_spread, V_AT)
    for block in range(2):
        turned = g_spread[block].astype(f32).T
        delta_ref[block : block + 1, :] = jnp.sum(turned * mixed[block], axis=0, keepdims=True)

    def pack(at, grads):
        rows = grads.shape[0]
        for tile in range(grads.shape[1] // 128):
            dw[at + tile * rows : at + (tile + 1) * rows, :] = grads[:, 128 * tile : 128 * tile + 128].astype(bf16)
        if grads.shape[1] % 128:
            tile = grads.shape[1] // 128
            dw[at + tile * rows : at + (tile + 1) * rows, 0:64] = grads[:, 128 * tile : 128 * tile + 64].astype(bf16)
            dw[at + tile * rows : at + (tile + 1) * rows, 64:128] = jnp.zeros((rows, 64), bf16)

    pack(GATE_AT, tn_dot(normed, grad_gate))
    pack(UP_AT, tn_dot(normed, grad_up))
    pack(DOWN_AT, tn_dot(cotangent, active))
    pack(OUT_AT, tn_dot(attended, grad_out))
    gain_rows[...] = jnp.zeros_like(gain_rows)
    for tile in range(4):
        gain_rows[tile : tile + 1, :] = by_gain[:, 128 * tile : 128 * tile + 128]
    gain_rows[4:5, 0:64] = by_gain[:, 512:576]
    dw[GAIN_AT : GAIN_AT + 16, :] = gain_rows[...].astype(bf16)
    dw[GAIN_AT + 16 : FF_ROWS, :] = jnp.zeros((FF_ROWS - GAIN_AT - 16, 128), bf16)
    band_rows = FF_ROWS // 3
    dw_copies = [
        pltpu.make_async_copy(dw.at[pl.ds(band * band_rows, band_rows)], dws[band], dw_sem.at[band])
        for band in range(3)
    ]
    for copy in dw_copies:
        copy.start()

    mixed[...] = jnp.zeros_like(mixed)

    def backward(block, chunk, masked, mode, count=1):
        window = chunk_rows(chunk, count)
        keys = held[window, 0:256]
        values = held[window, 128:384]
        scores = nt_dot(keys, q_spread[block])
        probs = jnp.exp(scores - top[block : block + 1, :])
        if masked:
            probs = jnp.where(mask_of(block, chunk), probs, 0.0)
        grad_probs = nt_dot(values, g_spread[block])
        grad_scores = (probs * (grad_probs - delta_ref[block : block + 1, :])).astype(bf16)
        mixed[block, 0:192] += nn_dot(keys.T[0:192], grad_scores)
        dk = nn_dot(grad_scores, q_spread[block])
        dv = nn_dot(probs.astype(bf16), g_spread[block])
        parts = (dk[:, 0:128], dk[:, 128:256] + dv[:, 0:128], dv[:, 128:256])
        for band in range(3):
            at = slice(128 * band, 128 * band + 128)
            if mode == "first":
                staged[:, at] = parts[band]
            elif mode == "second":
                held[window, at] = (staged[:, at] + parts[band]).astype(bf16)
            else:
                held[window, at] = parts[band].astype(bf16)

    def put_back(chunk):
        for piece in range(PIECES):
            row = pl.multiple_of(slot_of(chunk * PIECES + piece), HALF)
            rows = pl.ds(pl.multiple_of(chunk * CHUNK + piece * HALF, HALF), HALF)
            for band in range(3):
                pltpu.make_async_copy(
                    held.at[rows, 128 * band : 128 * band + 128],
                    dkvs[band].at[pl.ds(row, HALF)],
                    out_sem.at[chunk],
                ).start()

    def backward_step(chunk, carry):
        in_a = chunk <= a_hi
        in_b = (chunk >= b_lo) & (chunk <= b_hi)

        @pl.when(in_a & jnp.logical_not(in_b))
        def _():
            backward(0, chunk, True, "only")

        @pl.when(in_b & jnp.logical_not(in_a))
        def _():
            backward(1, chunk, True, "only")

        @pl.when(in_a & in_b)
        def _():
            backward(0, chunk, True, "first")
            backward(1, chunk, True, "second")

        @pl.when(in_a | in_b)
        def _():
            put_back(chunk)

        return carry

    def backward_pair(pair_of, carry):
        backward(0, 2 * pair_of, False, "only", 2)
        put_back(2 * pair_of)
        put_back(2 * pair_of + 1)
        return carry

    lax.fori_loop(0, plain, backward_pair, 0)
    lax.fori_loop(2 * plain, b_hi + 1, backward_step, 0)
    for block in range(2):
        unspread(mixed.at[block], dq_ref, block, K_AT)

    def drain(chunk, carry):
        use = needed(chunk, a_hi, b_lo, b_hi)

        @pl.when(use)
        def _():
            wait_chunk(chunk, held, out_sem)

        @pl.when(jnp.logical_not(use))
        def _():
            for _piece in range(PIECES):
                for band in range(3):
                    zero_copy(band, 0).wait()

        return carry

    lax.fori_loop(0, CHUNKS, drain, 0)
    for copy in dw_copies:
        copy.wait()


def layer(pair, kvs, weights, q, segments, x, cotangent, gain):
    vmem = pl.BlockSpec(memory_space=pltpu.VMEM)
    anywhere = pl.BlockSpec(memory_space=pl.ANY)
    return pl.pallas_call(
        layer_kernel,
        out_shape=(
            jax.ShapeDtypeStruct((D, ROWS), bf16),
            jax.ShapeDtypeStruct((ROWS, D), f32),
            jax.ShapeDtypeStruct((ROWS, D), f32),
        )
        + (jax.ShapeDtypeStruct((TOKENS, 128), bf16),) * 3
        + (jax.ShapeDtypeStruct((FF_ROWS // 3, 128), bf16),) * 3,
        grid_spec=pltpu.PrefetchScalarGridSpec(
            num_scalar_prefetch=1,
            in_specs=[anywhere] * 7 + [vmem] * 5,
            out_specs=(vmem,) * 3 + (anywhere,) * 6,
            scratch_shapes=[
                pltpu.VMEM((TOKENS, 384), bf16),
                pltpu.SemaphoreType.DMA((CHUNKS,)),
                pltpu.VMEM((D, D), bf16),
                pltpu.VMEM((D, FF), bf16),
                pltpu.VMEM((D, FF), bf16),
                pltpu.VMEM((D, FF), bf16),
                pltpu.SemaphoreType.DMA((4,)),
                pltpu.VMEM((2, COLS, 256), bf16),
                pltpu.VMEM((2, COLS, 256), bf16),
                pltpu.VMEM((2, 256, COLS), f32),
                pltpu.VMEM((2, COLS), f32),
                pltpu.VMEM((2, COLS), f32),
                pltpu.VMEM((ROWS, D), f32),
                pltpu.VMEM((2, COLS), f32),
                pltpu.VMEM((FF_ROWS, 128), bf16),
                pltpu.SemaphoreType.DMA((3,)),
                pltpu.VMEM((CHUNK, 384), f32),
                pltpu.VMEM((HALF, 128), bf16),
                pltpu.SemaphoreType.DMA((CHUNKS,)),
                pltpu.SemaphoreType.DMA,
                pltpu.VMEM((16, 128), f32),
                pltpu.VMEM((4, COLS), jnp.int32),
                pltpu.VMEM((N_CTX, META, 128), bf16),
                pltpu.SemaphoreType.DMA((2,)),
                pltpu.VMEM((8, 128), jnp.int32),
                pltpu.SMEM((8, 128), jnp.int32),
            ],
        ),
        compiler_params=pltpu.CompilerParams(vmem_limit_bytes=VMEM_LIMIT),
        name="layer",
    )(pair, *kvs, *weights, q, segments, x, cotangent, gain)


def reduce_kernel(*refs):
    dkv, dws = refs[0:3], refs[3:6]
    dq_ref, n_ref, x_ref, gh_ref, cos_ref, sin_ref, gain_ref, wq_ref, wk_ref, wv_ref = refs[6:16]
    gx_ref, outs, outs_one = refs[16], refs[17:20], refs[20:23]
    rest = refs[23:]
    done, done_ff, done_one, rest = rest[0:3], rest[3:6], rest[6:9], rest[9:]
    first, rest = rest[:SCATTER_REFS], rest[SCATTER_REFS:]
    second, rest = rest[:SCATTER_REFS], rest[SCATTER_REFS:]
    third, rest = rest[:SCATTER_REFS], rest[SCATTER_REFS:]
    parts, own, own_one, rest = rest[0:3], rest[3:6], rest[6:9], rest[9:]
    gain_rows, sems, sems_one = rest
    me, coords, core = whereabouts()
    greet(me, coords, core)

    def feed_forward():
        yield from scatter_steps([(dw,) for dw in dws], done_ff, second, True)
        for band in range(3):
            own[band][...] = done_ff[band][...].astype(bf16)
        yield from gather_steps(own, outs, Pool(sems))

    def small():
        yield from scatter_steps([(part,) for part in parts], done_one, third, False)
        for band in range(3):
            own_one[band][...] = done_one[band][...].astype(bf16)
        yield from gather_steps(own_one, outs_one, Pool(sems_one), False)

    def advance(steps, count):
        for _ in range(count):
            next(steps)

    scatter = scatter_steps([(d,) for d in dkv], done, first, True)
    other = feed_forward()
    advance(scatter, 1)
    advance(other, 1)
    advance(scatter, 12)
    advance(other, SIDE)
    run(scatter)

    cos_wide, sin_wide = cos_ref[...], -sin_ref[...]
    tiles = [turn(dq_ref[:, 128 * t : 128 * t + 128] * SCALE, cos_wide, sin_wide).astype(bf16) for t in range(4)]
    mixed = turn(
        jnp.concatenate([done[1][0:ROWS, 0:64], dq_ref[:, 512:576] * SCALE], 1), cos_wide, sin_wide
    ).astype(bf16)
    grad_q = jnp.concatenate(tiles + [mixed[:, 64:128]], 1)
    grad_k = jnp.concatenate(
        [turn(done[0][0:ROWS, :], cos_wide, sin_wide).astype(bf16), mixed[:, 0:64]], 1
    )
    grad_v = jnp.concatenate([done[2][0:ROWS, :], done[1][0:ROWS, 64:128]], 1).astype(bf16)
    normed = n_ref[...]
    features = x_ref[...].astype(f32).T
    grad_normed = nt_dot(grad_q, wq_ref[...]) + nn_dot(grad_k, wk_ref[...]) + nn_dot(grad_v, wv_ref[...])
    by_x, by_gain = rms_back(features, gain_ref[...].reshape(1, D), grad_normed)

    def put(at, rows16):
        block = at // 16
        band, device = divmod(block, N_CTX)
        index = (device // 32, device // 8 % 4, device // 2 % 4, device % 2)
        parts[band][index] = rows16

    def pack(at, grads):
        height, width = grads.shape
        grads = jnp.concatenate([grads, jnp.zeros((height, 128 - width % 128), f32)], 1).astype(bf16)
        for tile in range(grads.shape[1] // 128):
            for row in range(0, height, 16):
                put(at + tile * height + row, grads[row : row + 16, 128 * tile : 128 * tile + 128])

    pack(Q_AT, tn_dot(normed, grad_q))
    pack(KV_AT, tn_dot(jnp.concatenate([grad_k, grad_v], 1), normed))
    gain_rows[...] = jnp.zeros_like(gain_rows)
    for tile in range(4):
        gain_rows[tile : tile + 1, :] = by_gain[:, 128 * tile : 128 * tile + 128]
    gain_rows[4:5, 0:64] = by_gain[:, 512:576]
    put(GAIN_ONE_AT, gain_rows[...].astype(bf16))
    for at in range(GAIN_ONE_AT + 16, ATT_ROWS, 16):
        put(at, jnp.zeros((16, 128), bf16))

    chain = small()
    advance(chain, 1)
    gx_ref[...] = gh_ref[...] + by_x
    turns = [(chain, 1), (other, 2)]
    while turns:
        for steps, count in list(turns):
            try:
                advance(steps, count)
            except StopIteration:
                turns.remove((steps, count))


def reduce_all(dkvs, dws, dq, normed, x, grad_hidden, cos_wide, sin_wide, gain, wq, wk, wv):
    vmem = pl.BlockSpec(memory_space=pltpu.VMEM)
    anywhere = pl.BlockSpec(memory_space=pl.ANY)
    one = BAND_ROWS_ONE
    return pl.pallas_call(
        reduce_kernel,
        out_shape=(jax.ShapeDtypeStruct((ROWS, D), f32),)
        + (jax.ShapeDtypeStruct((SIDE, SIDE, SIDE, 2, BAND_ROWS, 128), bf16),) * 3
        + (jax.ShapeDtypeStruct((SIDE, SIDE, SIDE, 2, one, 128), bf16),) * 3,
        in_specs=[anywhere] * 6 + [vmem] * 10,
        out_specs=(vmem,) + (anywhere,) * 6,
        scratch_shapes=[pltpu.VMEM((ROWS, 128), f32)] * 3
        + [pltpu.VMEM((BAND_ROWS, 128), f32)] * 3
        + [pltpu.VMEM((one, 128), f32)] * 3
        + scatter_scratch(ROWS, True)
        + scatter_scratch(BAND_ROWS, True)
        + scatter_scratch(one, False)
        + [pltpu.VMEM((SIDE, SIDE, SIDE, 2, one, 128), bf16)] * 3
        + [pltpu.VMEM((BAND_ROWS, 128), bf16)] * 3
        + [pltpu.VMEM((one, 128), bf16)] * 3
        + [
            pltpu.VMEM((16, 128), f32),
            pltpu.SemaphoreType.DMA((GATHER_SEMS,)),
            pltpu.SemaphoreType.DMA((GATHER_SEMS_ONE,)),
        ],
        compiler_params=pltpu.CompilerParams(
            collective_id=2, has_side_effects=True, vmem_limit_bytes=VMEM_LIMIT
        ),
        name="reduce_all",
    )(*dkvs, *dws, dq, normed, x, grad_hidden, cos_wide, sin_wide, gain, wq, wk, wv)


FF_PARTS = ((GATE_AT, D, FF), (UP_AT, D, FF), (DOWN_AT, D, FF), (OUT_AT, D, D))


def unpack_kernel(
    sums0, sums1, sums2, ones0, ones1, ones2, gx_ref,
    xt_ref, ga_ref, gq_ref, gk_ref, gv_ref, gm_ref, gg_hbm, gu_hbm, gd_hbm, go_hbm,
    held, held_one, full0, full1, full2, full3, sem_in, sem_one, sem_out,
):
    sums = (sums0, sums1, sums2)
    fulls = (full0, full1, full2, full3)
    spots = (gg_hbm, gu_hbm, gd_hbm, go_hbm)
    band_blocks = N_CTX
    copies = []
    edges = [0]
    for at, rows, columns in FF_PARTS:
        edges.append((at + (columns + 127) // 128 * rows) // BAND_ROWS)
    edges[-1] = 3 * band_blocks
    for part in range(4):
        mine = []
        lo = edges[part]
        while lo < edges[part + 1]:
            band = lo // band_blocks
            hi = min(edges[part + 1], (band + 1) * band_blocks)
            mine.append(
                pltpu.make_async_copy(
                    sums[band].at[pl.ds(lo - band * band_blocks, hi - lo)],
                    held.at[pl.ds(lo, hi - lo)],
                    sem_in.at[part, len(mine)],
                )
            )
            mine[-1].start()
            lo = hi
        copies.append(mine)
    small = [
        pltpu.make_async_copy(ref, held_one.at[band], sem_one.at[band])
        for band, ref in enumerate((ones0, ones1, ones2))
    ]
    for copy in small:
        copy.start()
    xt_ref[...] = gx_ref[...].T
    outs = []
    for part, (at, rows, columns) in enumerate(FF_PARTS):
        for copy in copies[part]:
            copy.wait()
        for tile in range((columns + 127) // 128):
            width = min(128, columns - 128 * tile)
            for row in range(0, rows, BAND_ROWS):
                piece = held[(at + tile * rows + row) // BAND_ROWS].astype(f32)
                fulls[part][row : row + BAND_ROWS, 128 * tile : 128 * tile + width] = piece[:, 0:width]
        outs.append(pltpu.make_async_copy(fulls[part], spots[part], sem_out.at[part]))
        outs[-1].start()
    for copy in small:
        copy.wait()

    def fetch_one(at):
        band, block = divmod(at // BAND_ROWS_ONE, N_CTX)
        return held_one[band, block].astype(f32)

    for tile in range(5):
        width = min(128, D - 128 * tile)
        lanes = slice(128 * tile, 128 * tile + width)
        for row in range(0, D, 16):
            gq_ref[row : row + 16, lanes] = fetch_one(Q_AT + tile * D + row)[:, 0:width]
        for row in range(0, 192, 16):
            gk_ref[row : row + 16, lanes] = fetch_one(KV_AT + tile * 384 + row)[:, 0:width]
            gv_ref[row : row + 16, lanes] = fetch_one(KV_AT + tile * 384 + 192 + row)[:, 0:width]
        ga_ref[lanes] = fetch_one(GAIN_ONE_AT)[tile, 0:width]
        gm_ref[lanes] = held[GAIN_AT // BAND_ROWS].astype(f32)[tile, 0:width]
    for copy in outs:
        copy.wait()


def unpack(sums, ones, grad_x):
    vmem = pl.BlockSpec(memory_space=pltpu.VMEM)
    anywhere = pl.BlockSpec(memory_space=pl.ANY)
    shapes = ((D, ROWS), (D,), (D, D), (192, D), (192, D), (D,), (D, FF), (D, FF), (D, FF), (D, D))
    return pl.pallas_call(
        unpack_kernel,
        out_shape=tuple(jax.ShapeDtypeStruct(s, f32) for s in shapes),
        in_specs=[anywhere] * 6 + [vmem],
        out_specs=(vmem,) * 6 + (anywhere,) * 4,
        scratch_shapes=[
            pltpu.VMEM((3 * N_CTX, BAND_ROWS, 128), bf16),
            pltpu.VMEM((3, N_CTX, BAND_ROWS_ONE, 128), bf16),
            pltpu.VMEM((D, FF), f32),
            pltpu.VMEM((D, FF), f32),
            pltpu.VMEM((D, FF), f32),
            pltpu.VMEM((D, D), f32),
            pltpu.SemaphoreType.DMA((4, 2)),
            pltpu.SemaphoreType.DMA((3,)),
            pltpu.SemaphoreType.DMA((4,)),
        ],
        compiler_params=pltpu.CompilerParams(vmem_limit_bytes=VMEM_LIMIT),
        name="unpack",
    )(
        *[s.reshape(N_CTX, BAND_ROWS, 128) for s in sums],
        *[s.reshape(N_CTX, BAND_ROWS_ONE, 128) for s in ones],
        grad_x,
    )


def on_device(
    layer_input,
    attn_gain,
    w_query,
    w_key,
    w_value,
    w_out,
    mlp_gain,
    w_gate,
    w_up,
    w_down,
    cotangent,
    segment_ids,
    pair_table,
):
    own_pair = pair_table[0]
    within = jnp.arange(ROWS, dtype=jnp.int32)
    blocks = jnp.where(within < HALF, own_pair, 2 * N_CTX - 1 - own_pair)
    places = blocks * HALF + within % HALF
    lanes = jnp.arange(128, dtype=jnp.int32)
    frequency = ROPE_THETA ** (-2.0 * (lanes % (HEAD_DIM // 2)).astype(f32) / HEAD_DIM)
    turned = places.astype(f32)[:, None] * frequency[None, :]
    cos_wide = jnp.cos(turned)
    sin_wide = jnp.sin(turned) * jnp.where(lanes % HEAD_DIM < HEAD_DIM // 2, -1.0, 1.0)[None, :]

    segments = segment_ids[None, :]
    x_turned = layer_input.T
    wk_turned, wv_turned = w_key.T, w_value.T
    q_rot, normed, *kvs = project_and_gather(
        pair_table, x_turned, attn_gain, w_query, wk_turned, wv_turned, cos_wide, sin_wide, segments
    )
    result, grad_hidden, dq, *rest = layer(
        pair_table,
        [kv.reshape(N_CTX, kv.shape[4], 128) for kv in kvs],
        [w_out, w_gate, w_up, w_down.T],
        q_rot,
        segments,
        x_turned,
        cotangent.T,
        mlp_gain,
    )
    lead = (SIDE, SIDE, SIDE, 2)
    grad_x, *sums = reduce_all(
        [d.reshape(lead + (ROWS, 128)) for d in rest[0:3]],
        [d.reshape(lead + (BAND_ROWS, 128)) for d in rest[3:6]],
        dq,
        normed,
        x_turned,
        grad_hidden,
        cos_wide,
        sin_wide,
        attn_gain,
        w_query,
        wk_turned,
        wv_turned,
    )
    gx, ga, gq, gk, gv, gm, gg, gu, gd, go = unpack(sums[0:3], sums[3:6], grad_x)
    return (result.T, gx.T, ga, gq, gk.T, gv.T, go, gm, gg, gu, gd.T)


def solution(mesh):
    return jax.shard_map(
        on_device,
        mesh=mesh,
        in_specs=(
            P("ctx", None),
            P(),
            P(),
            P(),
            P(),
            P(),
            P(),
            P(),
            P(),
            P(),
            P("ctx", None),
            P("ctx"),
            P("ctx"),
        ),
        out_specs=(P("ctx", None), P("ctx", None), P(), P(), P(), P(), P(), P(), P(), P(), P()),
        check_vma=False,
    )
```

time: 274 us -> 200 us (0.73)
  Pallas kernels: 235 us -> 198 us
  local copies, waits for them, and re-layouts: 27.4 us -> 0 us
  other arithmetic: 6.55 us -> 0.98 us
    pallas_call x1, Pallas kernels: 148 us -> 89.3 us  [reduce_all(): pl.pallas_call(reduce_kernel, out_shape=(jax.ShapeDtypeStruct((ROWS, D),...]
    pallas_call x1, Pallas kernels: 25.9 us -> 55.2 us  [layer(): pl.pallas_call(layer_kernel, out_shape=(jax.ShapeDtypeStruct((D, ROWS), b...]
    unnamed x15 -> x0, local copies, waits for them, and re-layouts: 22.4 us -> none
    pallas_call x1, Pallas kernels: 51.7 us -> 44.5 us  [project_and_gather(): pl.pallas_call(project_kernel, out_shape=(jax.ShapeDtypeStruct((ROWS, D),...]
where the time goes in v2:
time: 200 us; the launch traced here: 201 us
  Pallas kernels  198 us (99%)
    pallas_call x1, Pallas kernels, reduce_all(): pl.pallas_call(reduce_kernel, out_shape=(jax.ShapeDtypeStruct((ROWS, D),...  89.3 us
    pallas_call x1, Pallas kernels, layer(): pl.pallas_call(layer_kernel, out_shape=(jax.ShapeDtypeStruct((D, ROWS), b...  55.2 us
    pallas_call x1, Pallas kernels, project_and_gather(): pl.pallas_call(project_kernel, out_shape=(jax.ShapeDtypeStruct((ROWS, D),...  44.5 us
    pallas_call x1, Pallas kernels, unpack(): pl.pallas_call(unpack_kernel, out_shape=tuple((jax.ShapeDtypeStruct(s, f3...  9.07 us

profile of v2, /device:TPU:1, one launch (start us, length us, event | category | flops | bytes accessed | tf_op | source)
XLA Modules:
  0.0 200.7 jit_solution(14139809231770868414)
XLA Ops:
  1.3 1.0 fusion
  2.3 44.5 %project_and_gather.1 = (bf16[128,576]{1,0:T(8,128)(2,1)}, bf16[128,576]{1,0:T(8,128)(2,1)}, bf16[4,4,4,2,144,128]{5,4,3,2,1,0:T(8,128)(2,1)}, bf16[4,4,4,2,128,...) custom-call(s32[1]{0:T(128)} %copy.24.pair_ref, bf16[576,128]{1,0:T(8,128)(2,1)} %bitcast.42, f32[576]{0:T(1024)} %refs_12_.1, ...), custom_call_target="tpu_custom_call" | custom-call | tf_op jit(solution)/shard_map/project_and_gather/pallas_call | solution.py:510
  46.8 55.2 %layer.1 = (bf16[576,128]{1,0:T(8,128)(2,1)}, f32[128,576]{1,0:T(8,128)}, f32[128,576]{1,0:T(8,128)}, bf16[16384,128]{1,0:T(8,128)(2,1)}, bf16[16384,128]{1,0:T(...) custom-call(s32[1]{0:T(128)} %copy.24.pair_ref, ...), custom_call_target="tpu_custom_call" | custom-call | tf_op jit(solution)/shard_map/layer/pallas_call | solution.py:851
  102.0 89.3 %reduce_all.1 = (f32[128,576]{1,0:T(8,128)}, bf16[4,4,4,2,64,128]{5,4,3,2,1,0:T(8,128)(2,1)}, bf16[4,4,4,2,64,128]{5,4,3,2,1,0:T(8,128)(2,1)}, bf16[4,4,4,2,64,1...) custom-call(bf16[4,4,4,2,128,128]{5,4,3,2,1,0:T(8,128)(2,1)} %bitcas, ...), custom_call_target="tpu_custom_call" | custom-call | tf_op jit(solution)/shard_map/reduce_all/pallas_call | solution.py:990
  191.4 9.1 %unpack.1 = (f32[576,128]{1,0:T(8,128)}, f32[576]{0:T(1024)}, f32[576,576]{1,0:T(8,128)}, f32[192,576]{1,0:T(8,128)}, f32[192,576]{1,0:T(8,128)}, /*index=5*/f32...) custom-call(bf16[128,64,128]{2,1,0:T(8,128)(2,1)} %bitcast.38, ...), custom_call_target="tpu_custom_call" | custom-call | tf_op jit(solution)/shard_map/unpack/pallas_call | solution.py:1094
  (2 shorter events, 0.0 us)

commit v3 on v2

--- a/solution.py
+++ b/solution.py
@@ -22,10 +22,10 @@
 TOKENS = ROWS * N_CTX
 DOCS = 18
 META = 16
-SLAB = ROWS + META
 CHUNK = 512
 PIECES = CHUNK // HALF
 CHUNKS = TOKENS // CHUNK
+BLANK = 4096
 COLS = HEADS * HALF
 NEG = -1e30
 SCALE = HEAD_DIM ** (-0.5)
@@ -45,6 +45,7 @@
 KV_AT = Q_AT + 5 * D
 GAIN_ONE_AT = KV_AT + 5 * 384
 BAND_ROWS_ONE = 16
+FINAL_ROWS = BAND_ROWS + BAND_ROWS_ONE
 ATT_ROWS = 3 * N_CTX * BAND_ROWS_ONE
 
 MESH = pl.DeviceIdType.MESH
@@ -67,14 +68,21 @@
     return me + (wrap(coords[axis], step) - coords[axis]) * STRIDES[axis]
 
 
+PARTNERS = 10
+
+
 def greet(me, coords, core):
-    barrier = pltpu.get_barrier_semaphore()
     others = [me + 1 - 2 * core]
     for axis in range(3):
         others += [neighbour(me, coords, axis, step) for step in (1, -1, 2)]
     for other in others:
-        pl.semaphore_signal(barrier, inc=1, device_id=(other,), device_id_type=MESH)
-    pl.semaphore_wait(barrier, len(others))
+        pl.semaphore_signal(
+            pltpu.get_barrier_semaphore(), inc=1, device_id=(other,), device_id_type=MESH
+        )
+
+
+def meet():
+    pl.semaphore_wait(pltpu.get_barrier_semaphore(), PARTNERS)
 
 
 def half_rows(rows):
@@ -116,7 +124,7 @@
 WHOLE = pl.ds(0, SIDE)
 
 
-def gather_steps(own, out, pool, ring=True):
+def gather_steps(own, out, pool):
     me, coords, core = whereabouts()
     sibling = me + 1 - 2 * core
     bands = range(len(own))
@@ -133,87 +141,118 @@
     def device(band, phase, step):
         return neighbour(me, coords, orders[band][phase], step)
 
-    homes = [pool.new() for band in bands]
-    sent = [[pool.new() for phase in range(3)] for band in bands]
+    def blocks(*shape):
+        return out[0].at[tuple(pl.ds(0, size) for size in shape)]
+
+    home, came, gone = pool.new(), [pool.new() for phase in range(3)], [pool.new(), pool.new()]
+    ringed = [pool.new() for band in bands]
     across = [(pool.new(), pool.new()) for band in bands]
-    came = [[pool.new() for phase in range(3)] for band in bands]
-    ends = {}
+    ends = {line: (pool.new(), pool.new(), pool.new()) for line in lines}
     for step in steps:
         for phase in (1, 0):
             for band in bands:
                 part = place(band, *(mine(band, p) for p in range(3)))
-                send(own[band], part, device(band, phase, step), sent[band][0], came[band][phase])
+                send(own[band], part, device(band, phase, step), gone[0], came[phase])
     for band in bands:
         part = place(band, *(mine(band, p) for p in range(3)))
-        pltpu.make_async_copy(own[band], part, homes[band]).start()
+        pltpu.make_async_copy(own[band], part, home).start()
 
     def send_line(band, line):
         part = place(band, mine(band, 0, line), WHOLE, mine(band, 2))
-        if ring:
-            ends[band, line] = (pool.new(), pool.new(), pool.new())
-            send(part, part, device(band, 2, 1), sent[band][2], ends[band, line][0])
-            send(part, part, device(band, 2, -1), sent[band][2], ends[band, line][1])
-        else:
-            if line == 0:
-                ends[band] = pool.new()
-            for step in steps:
-                send(part, part, device(band, 2, step), sent[band][2], ends[band])
+        send(part, part, device(band, 2, 1), ringed[band], ends[line][0])
+        send(part, part, device(band, 2, -1), ringed[band], ends[line][1])
 
     yield
+    wait_for(blocks(1, 1, 3, 1), home)
+    wait_for(blocks(1, 3, 3, 1), came[1])
     for band in bands:
-        wait_for(own[band], homes[band])
-        wait_for(out[band].at[0, 0, 0:3, 0], came[band][1])
         send_line(band, 0)
+    wait_for(blocks(1, 3, 3, 1), came[0])
     for band in bands:
-        wait_for(out[band].at[0, 0, 0:3, 0], came[band][0])
         for line in lines[1:]:
             part = place(band, mine(band, 0, line), mine(band, 1), mine(band, 2))
             for step in steps:
-                send(part, part, device(band, 1, step), sent[band][1], came[band][2])
+                send(part, part, device(band, 1, step), gone[1], came[2])
     yield
-    for band in bands:
-        wait_for(out[band].at[0, 0:3, 0:3, 0], came[band][2])
-        for line in lines[1:]:
+    wait_for(blocks(3, 3, 3, 1), came[2])
+    for line in lines[1:]:
+        for band in bands:
             send_line(band, line)
     for band in bands:
         part = place(band, WHOLE, WHOLE, mine(band, 2))
         send(part, part, sibling, *across[band])
-    if ring:
-        for line in lines:
-            yield
+    for line in lines:
+        yield
+        for side, step in ((0, -1), (1, 1)):
+            wait_for(blocks(1, 3, 4, 1), ends[line][side])
             for band in bands:
                 rows = own[band].shape[0]
                 cut = half_rows(rows)
-                for side, step, lo, size in ((0, -1, 0, cut), (1, 1, cut, rows - cut)):
-                    part = place(band, mine(band, 0, line), WHOLE, mine(band, 2, step))
-                    wait_for(part, ends[band, line][side])
-                    half = part.at[:, pl.ds(lo, size)]
-                    send(half, half, device(band, 2, -step), sent[band][2], ends[band, line][2])
-                    send(part, part, sibling, *across[band])
-        for line in lines:
-            yield
-            for band in bands:
-                part = place(band, mine(band, 0, line), WHOLE, mine(band, 2, 2))
-                wait_for(part, ends[band, line][2])
+                part = place(band, mine(band, 0, line), WHOLE, mine(band, 2, step))
+                half = part.at[:, pl.ds(0, cut) if side == 0 else pl.ds(cut, rows - cut)]
+                send(half, half, device(band, 2, -step), ringed[band], ends[line][2])
                 send(part, part, sibling, *across[band])
-    else:
+    for line in lines:
         yield
+        wait_for(blocks(1, 3, 4, 1), ends[line][2])
         for band in bands:
-            wait_for(out[band].at[0:3, :, :, 0], ends[band])
-            for step in steps:
-                part = place(band, WHOLE, WHOLE, mine(band, 2, step))
-                send(part, part, sibling, *across[band])
+            part = place(band, mine(band, 0, line), WHOLE, mine(band, 2, 2))
+            send(part, part, sibling, *across[band])
     yield
     for band in bands:
         wait_for(out[band].at[:, :, :, 0], across[band][1])
         wait_for(out[band].at[:, :, :, 0], across[band][0])
-        wait_for(out[band].at[0, 0:2, 0:3, 0], sent[band][0])
-        wait_for(out[band].at[0, 0:3, 0:3, 0], sent[band][1])
-        wait_for(out[band].at[0:3, :, :, 0], sent[band][2])
-
-
-GATHER_SEMS = 3 * (1 + 3 + 2 + 3 + 12)
-GATHER_SEMS_ONE = 3 * (1 + 3 + 2 + 3 + 1)
+        wait_for(out[band].at[0:3, :, :, 0], ringed[band])
+    wait_for(blocks(3, 3, 1, 2), gone[0])
+    wait_for(blocks(3, 3, 3, 1), gone[1])
+
+
+GATHER_SEMS = 1 + 3 + 2 + 3 + 6 + 12
+
+
+def gather_small_steps(own, out, pool):
+    me, coords, core = whereabouts()
+    sibling = me + 1 - 2 * core
+    bands = range(len(own))
+    homes = [pool.new() for band in bands]
+    for band in bands:
+        pltpu.make_async_copy(own[band], out[band].at[coords + (core,)], homes[band]).start()
+    sent = []
+    for phase in range(3):
+        came = [pool.new() for band in bands]
+        gone = [pool.new() for band in bands]
+        for band in bands:
+            order = ORDERS[band % 3]
+            mine = [coords[axis] for axis in order]
+            part = out[band].at[at_axes(order, [WHOLE] * phase + mine[phase:]) + (core,)]
+            for step in (1, -1, 2):
+                send(
+                    own[band] if phase == 0 else part,
+                    part,
+                    neighbour(me, coords, order[phase], step),
+                    gone[band],
+                    came[band],
+                )
+        yield
+        for band in bands:
+            if phase == 0:
+                wait_for(own[band], homes[band])
+            three = (0, 0, pl.ds(0, 3), 0), (0, pl.ds(0, 3), WHOLE, 0), (pl.ds(0, 3), WHOLE, WHOLE, 0)
+            wait_for(out[band].at[three[phase]], came[band])
+            sent.append((out[band].at[three[phase]], gone[band]))
+    across = [(pool.new(), pool.new()) for band in bands]
+    for band in bands:
+        part = out[band].at[:, :, :, core]
+        send(part, part, sibling, *across[band])
+    yield
+    for band in bands:
+        wait_for(out[band].at[:, :, :, 0], across[band][1])
+        wait_for(out[band].at[:, :, :, 0], across[band][0])
+    for ref, sem in sent:
+        wait_for(ref, sem)
+
+
+GATHER_SMALL_SEMS = 1 + 3 * 2 + 2
 
 
 def run(steps):
@@ -229,7 +268,7 @@
             pltpu.VMEM((3, SIDE, rows, 128), bf16),
             pltpu.VMEM((3, rows, 128), bf16),
         ]
-    return shapes + [pltpu.SemaphoreType.DMA((3 * (4 + 16 + 4 + 8 + 2 if ring else 4 + 1 + 1 + 3),))]
+    return shapes + [pltpu.SemaphoreType.DMA((6 + 2 + 4 + 16 + 8 + 2 if ring else 6 + 2 + 6 + 3 + 2,))]
 
 
 SCATTER_REFS = 16
@@ -245,28 +284,37 @@
     steps = (2, 1, -1, 0)
     rows = acc[0].shape[3]
     cut = half_rows(rows)
-    sent = [[pool.new() for phase in range(4)] for band in bands]
+    def blocks(*shape):
+        return acc[0].at[tuple(pl.ds(0, size) for size in shape)]
+
+    sent = [[pool.new(), None, None, pool.new()] for band in bands]
+    for phase in (1, 2):
+        shared = pool.new()
+        for band in bands:
+            sent[band][phase] = shared
     homes, swaps = {}, {}
     if ring:
         for step in steps:
             for band in bands:
                 order = ORDERS[band]
                 plane = at_axes(order, (wrap(coords[order[0]], step), WHOLE, WHOLE))
-                homes[band, step] = pool.new()
+                if band == 0:
+                    homes[step] = pool.new()
                 top = 0
                 for part in parts[band]:
                     size = part.shape[4]
                     pltpu.make_async_copy(
                         part.at[plane + (core,)],
                         acc[band].at[plane + (pl.ds(top, size),)],
-                        homes[band, step],
+                        homes[step],
                     ).start()
                     top += size
             for sub in range(SIDE):
                 for band in bands:
                     order = ORDERS[band]
                     line = at_axes(order, (wrap(coords[order[0]], step), sub, WHOLE))
-                    swaps[band, step, sub] = pool.new()
+                    if band == 0:
+                        swaps[step, sub] = pool.new()
                     top = 0
                     for part in parts[band]:
                         size = part.shape[4]
@@ -275,7 +323,7 @@
                             sib[band].at[line + (pl.ds(top, size),)],
                             sibling,
                             sent[band][3],
-                            swaps[band, step, sub],
+                            swaps[step, sub],
                         )
                         top += size
     else:
@@ -288,17 +336,13 @@
     def add_swap(band, step, sub):
         order = ORDERS[band]
         first = wrap(coords[order[0]], step)
-        if sub == 0:
-            plane = acc[band].at[at_axes(order, (first, WHOLE, WHOLE))]
-            wait_for(plane, homes[band, step])
-        wait_for(sib[band].at[at_axes(order, (first, sub, WHOLE))], swaps[band, step, sub])
-
-        def body(last, carry):
-            at = at_axes(order, (first, sub, last))
-            acc[band][at] = acc[band][at] + sib[band][at]
-            return carry
-
-        lax.fori_loop(0, SIDE, body, 0)
+        if band == 0:
+            if sub == 0:
+                wait_for(blocks(3, 4, 4), homes[step])
+            wait_for(blocks(1, 3, 4), swaps[step, sub])
+
+        line = at_axes(order, (first, sub, WHOLE))
+        acc[band][line] = acc[band][line] + sib[band][line]
 
     jobs = [(sub, band) for sub in range(SIDE) for band in bands]
 
@@ -306,68 +350,57 @@
         order = ORDERS[band]
         return at_axes(order, (wrap(coords[order[0]], step), sub, WHOLE))
 
-    def sum_up(band, index_of, landed):
-        def body(last, carry):
-            at = index_of(last)
-            total = acc[band][at].astype(f32)
-            for ref in landed(last):
-                total = total + ref.astype(f32)
-            acc[band][at] = total.astype(bf16)
-            return carry
-
-        lax.fori_loop(0, SIDE, body, 0)
+    def sum_up(band, region, landed):
+        total = acc[band][region].astype(f32)
+        for ref in landed:
+            total = total + ref[...].astype(f32)
+        acc[band][region] = total.astype(bf16)
 
     if ring:
         passing, ending = {}, {}
-        for sub, band in jobs:
-            if band == 0:
-                yield
-            axis = ORDERS[band][0]
-            add_swap(band, 2, sub)
-            far = acc[band].at[line_at(band, 2, sub)]
-            passing[sub, band], ending[sub, band] = pool.new(), pool.new()
-            for slot, lo, size, step in ((0, 0, cut, 1), (0, cut, rows - cut, -1)):
-                send(
-                    far.at[:, pl.ds(lo, size)],
-                    landing[band][0].at[slot, sub, :, pl.ds(lo, size)],
-                    neighbour(me, coords, axis, step),
-                    sent[band][0],
-                    passing[sub, band],
+        for sub in range(SIDE):
+            yield
+            passing[sub], ending[sub] = pool.new(), pool.new()
+            for band in bands:
+                axis = ORDERS[band][0]
+                add_swap(band, 2, sub)
+                far = acc[band].at[line_at(band, 2, sub)]
+                for lo, size, step in ((0, cut, 1), (cut, rows - cut, -1)):
+                    send(
+                        far.at[:, pl.ds(lo, size)],
+                        landing[band][0].at[0, sub, :, pl.ds(lo, size)],
+                        neighbour(me, coords, axis, step),
+                        sent[band][0],
+                        passing[sub],
+                    )
+        for sub in range(SIDE):
+            yield
+            for step in (1, -1):
+                for band in bands:
+                    add_swap(band, step, sub)
+            wait_for(blocks(1, 3, 4), passing[sub])
+            for band in bands:
+                order = ORDERS[band]
+                for slot, lo, size, step in ((1, 0, cut, 1), (2, cut, rows - cut, -1)):
+                    half = line_at(band, step, sub) + (pl.ds(lo, size),)
+                    acc[band][half] = acc[band][half] + landing[band][0][0, sub, :, lo : lo + size]
+                    send(
+                        acc[band].at[line_at(band, step, sub)],
+                        landing[band][0].at[slot, sub],
+                        neighbour(me, coords, order[0], step),
+                        sent[band][0],
+                        ending[sub],
+                    )
+        for sub in range(SIDE):
+            yield
+            for band in bands:
+                add_swap(band, 0, sub)
+            wait_for(blocks(2, 3, 4), ending[sub])
+            for band in bands:
+                order = ORDERS[band]
+                sum_up(
+                    band, line_at(band, 0, sub), [landing[band][0].at[slot, sub] for slot in (1, 2)]
                 )
-        for sub, band in jobs:
-            if band == 0:
-                yield
-            axis = ORDERS[band][0]
-            add_swap(band, 1, sub)
-            add_swap(band, -1, sub)
-            wait_for(landing[band][0].at[0, sub], passing[sub, band])
-            for slot, lo, size, step in ((1, 0, cut, 1), (2, cut, rows - cut, -1)):
-
-                def body(last, carry, lo=lo, size=size, step=step):
-                    order = ORDERS[band]
-                    at = at_axes(order, (wrap(coords[order[0]], step), sub, last)) + (pl.ds(lo, size),)
-                    acc[band][at] = acc[band][at] + landing[band][0][0, sub, last, lo : lo + size]
-                    return carry
-
-                lax.fori_loop(0, SIDE, body, 0)
-                send(
-                    acc[band].at[line_at(band, step, sub)],
-                    landing[band][0].at[slot, sub],
-                    neighbour(me, coords, axis, step),
-                    sent[band][0],
-                    ending[sub, band],
-                )
-        for sub, band in jobs:
-            if band == 0:
-                yield
-            order = ORDERS[band]
-            add_swap(band, 0, sub)
-            wait_for(landing[band][0].at[1:3, sub], ending[sub, band])
-            sum_up(
-                band,
-                lambda last: at_axes(order, (coords[order[0]], sub, last)),
-                lambda last: [landing[band][0][slot, sub, last] for slot in (1, 2)],
-            )
     else:
         came = [pool.new() for band in bands]
         yield
@@ -393,7 +426,7 @@
             for slot in range(3):
                 total = total + landing[band][0][slot].astype(f32)
             acc[band][plane] = total.astype(bf16)
-    came = [pool.new() for band in bands]
+    came = pool.new()
     for slot, step in enumerate((2, 1, -1)):
         for band in bands:
             order = ORDERS[band]
@@ -403,18 +436,15 @@
                 landing[band][1].at[slot],
                 neighbour(me, coords, order[1], step),
                 sent[band][1],
-                came[band],
+                came,
             )
     yield
-    ends = [pool.new() for band in bands]
+    ends = pool.new()
+    wait_for(blocks(3, 3, 4), came)
     for band in bands:
         order = ORDERS[band]
-        wait_for(landing[band][1], came[band])
-        sum_up(
-            band,
-            lambda last: at_axes(order, (coords[order[0]], coords[order[1]], last)),
-            lambda last: [landing[band][1][slot, last] for slot in range(3)],
-        )
+        line = at_axes(order, (coords[order[0]], coords[order[1]], WHOLE))
+        sum_up(band, line, [landing[band][1].at[slot] for slot in range(3)])
         for slot, step in enumerate((2, 1, -1)):
             at = at_axes(order, (coords[order[0]], coords[order[1]], wrap(coords[order[2]], step)))
             send(
@@ -422,20 +452,20 @@
                 landing[band][2].at[slot],
                 neighbour(me, coords, order[2], step),
                 sent[band][2],
-                ends[band],
+                ends,
             )
     yield
+    wait_for(blocks(1, 3, 3), ends)
     for band in bands:
-        wait_for(landing[band][2], ends[band])
         total = acc[band][coords].astype(f32)
         for slot in range(3):
             total = total + landing[band][2][slot].astype(f32)
         done[band][...] = total
     for band in bands:
         wait_for(acc[band].at[0:3], sent[band][0])
-        wait_for(acc[band].at[0, 0:3], sent[band][1])
-        wait_for(acc[band].at[0, 0, 0:3], sent[band][2])
         wait_for(acc[band], sent[band][3])
+    wait_for(blocks(3, 3, 4), sent[0][1])
+    wait_for(blocks(1, 3, 3), sent[0][2])
 
 
 def rms_parts(features):
@@ -473,10 +503,16 @@
 
 def project_kernel(
     pair_ref, x_ref, gain_ref, wq_ref, wk_ref, wv_ref, cos_ref, sin_ref, seg_ref,
-    q_ref, n_ref, out0, out1, out2,
-    own0, own1, own2, sems,
+    q_ref, n_ref, table_ref, out0, out1, out2,
+    own0, own1, own2, own_meta, metas, sems, meta_sems,
 ):
     me, coords, core = whereabouts()
+    greet(me, coords, core)
+    segments = jnp.broadcast_to(seg_ref[...].astype(f32), (ROWS, ROWS)).T
+    lanes = lax.broadcasted_iota(jnp.int32, (ROWS, ROWS), 1)
+    earlier = jnp.sum(jnp.where(segments < (lanes - 1).astype(f32), 1.0, 0.0), axis=0, keepdims=True)
+    meta = jnp.where(lanes[0:1] == 0, pair_ref[0].astype(f32), earlier)
+    own_meta[...] = jnp.broadcast_to(meta, (META, 128)).astype(bf16)
     features = x_ref[...].astype(f32).T
     normed = (features * rms_parts(features) * gain_ref[...].reshape(1, D)).astype(bf16)
     n_ref[...] = normed
@@ -484,40 +520,66 @@
     keys = nt_dot(normed, wk_ref[...])
     values = nt_dot(normed, wv_ref[...]).astype(bf16)
     queries = nn_dot(normed, wq_ref[...])
-    own0[0:ROWS, :] = turn(keys[:, 0:128], cos_wide, sin_wide).astype(bf16)
-    segments = jnp.broadcast_to(seg_ref[...].astype(f32), (ROWS, ROWS)).T
-    lanes = lax.broadcasted_iota(jnp.int32, (ROWS, ROWS), 1)
-    earlier = jnp.sum(jnp.where(segments < (lanes - 1).astype(f32), 1.0, 0.0), axis=0, keepdims=True)
-    meta = jnp.where(lanes[0:1] == 0, pair_ref[0].astype(f32), earlier)
-    own0[ROWS:SLAB, :] = jnp.broadcast_to(meta, (META, 128)).astype(bf16)
+    own0[...] = turn(keys[:, 0:128], cos_wide, sin_wide).astype(bf16)
     mixed = turn(jnp.concatenate([keys[:, 128:192], queries[:, 512:576]], 1), cos_wide, sin_wide)
     own1[...] = jnp.concatenate([mixed[:, 0:64].astype(bf16), values[:, 128:192]], 1)
     own2[...] = values[:, 0:128]
-    greet(me, coords, core)
+    meet()
     steps = gather_steps((own0, own1, own2), (out0, out1, out2), Pool(sems))
+    small = gather_small_steps((own_meta,), (metas,), Pool(meta_sems))
+    next(small)
     next(steps)
+    next(small)
     for tile in range(4):
         at = slice(128 * tile, 128 * tile + 128)
         q_ref[:, at] = (turn(queries[:, at], cos_wide, sin_wide).astype(bf16).astype(f32) * SCALE).astype(bf16)
     q_ref[:, 512:576] = (mixed[:, 64:128].astype(bf16).astype(f32) * SCALE).astype(bf16)
+    next(steps)
+    next(small)
+    for _ in range(3):
+        next(steps)
+    next(small)
+    for _ in range(3):
+        next(steps)
+    run(small)
+    columns = metas[:, :, :, :, 0, :].astype(f32).reshape(N_CTX, 128)
+    starts = jnp.sum(columns, axis=0, keepdims=True)
+    numbers = lax.broadcasted_iota(jnp.int32, (N_CTX, N_CTX), 0).astype(f32)
+    holders = jnp.sum(
+        jnp.where(columns[:, 0:1] == lanes.astype(f32), numbers, 0.0), axis=0, keepdims=True
+    )
+    segment_row = seg_ref[...].astype(f32)
+    row_starts = jnp.zeros((1, ROWS), f32)
+    for document in range(DOCS):
+        row_starts = jnp.where(
+            segment_row == float(document), starts[:, document + 1 : document + 2], row_starts
+        )
+    table_ref[...] = jnp.concatenate(
+        [holders, row_starts, jnp.zeros((6, 128), f32)], 0
+    ).astype(jnp.int32)
     run(steps)
 
 
 def project_and_gather(pair, x, gain, wq, wk, wv, cos_wide, sin_wide, segments):
     vmem = pl.BlockSpec(memory_space=pltpu.VMEM)
     anywhere = pl.BlockSpec(memory_space=pl.ANY)
-    rows = (SLAB, ROWS, ROWS)
     return pl.pallas_call(
         project_kernel,
         out_shape=(
             jax.ShapeDtypeStruct((ROWS, D), bf16),
             jax.ShapeDtypeStruct((ROWS, D), bf16),
+            jax.ShapeDtypeStruct((8, 128), jnp.int32),
         )
-        + tuple(jax.ShapeDtypeStruct((SIDE, SIDE, SIDE, 2, r, 128), bf16) for r in rows),
+        + (jax.ShapeDtypeStruct((SIDE, SIDE, SIDE, 2, ROWS, 128), bf16),) * 3,
         in_specs=[pl.BlockSpec(memory_space=pltpu.SMEM)] + [vmem] * 8,
-        out_specs=(vmem, vmem, anywhere, anywhere, anywhere),
-        scratch_shapes=[pltpu.VMEM((r, 128), bf16) for r in rows]
-        + [pltpu.SemaphoreType.DMA((GATHER_SEMS,))],
+        out_specs=(vmem, vmem, vmem, anywhere, anywhere, anywhere),
+        scratch_shapes=[pltpu.VMEM((ROWS, 128), bf16)] * 3
+        + [
+            pltpu.VMEM((META, 128), bf16),
+            pltpu.VMEM((SIDE, SIDE, SIDE, 2, META, 128), bf16),
+            pltpu.SemaphoreType.DMA((GATHER_SEMS,)),
+            pltpu.SemaphoreType.DMA((GATHER_SMALL_SEMS,)),
+        ],
         compiler_params=pltpu.CompilerParams(
             collective_id=1, has_side_effects=True, vmem_limit_bytes=VMEM_LIMIT
         ),
@@ -544,13 +606,13 @@
 
 
 def layer_kernel(
-    pair_ref,
+    pair_ref, table,
     kv0, kv1, kv2, wo_hbm, wg_hbm, wu_hbm, wd_hbm,
-    q_ref, seg_ref, x_ref, c_ref, gain_ref,
+    q_ref, starts_ref, x_ref, c_ref, gain_ref,
     result_ref, gh_ref, dq_ref, dkv0, dkv1, dkv2, dw0, dw1, dw2,
     held, sem, wo_ref, wg_ref, wu_ref, wd_ref, w_sem, q_spread, g_spread, mixed, top, total, att_ref,
     delta_ref, dw, dw_sem, staged, blank, out_sem, blank_sem, gain_rows,
-    rows_ref, meta_ref, meta_sem, table_ref, table,
+    rows_ref,
 ):
     kvs, dkvs, dws = (kv0, kv1, kv2), (dkv0, dkv1, dkv2), (dw0, dw1, dw2)
     weights = [
@@ -559,35 +621,16 @@
             ((wo_hbm, wo_ref), (wg_hbm, wg_ref), (wu_hbm, wu_ref), (wd_hbm, wd_ref))
         )
     ]
-    metas = pltpu.make_async_copy(kv0.at[:, pl.ds(ROWS, META)], meta_ref, meta_sem.at[0])
-    metas.start()
     for copy in weights:
         copy.start()
     pair = pair_ref[0]
-    metas.wait()
-    columns = meta_ref[:, 0, :].astype(f32)
-    starts = jnp.sum(columns, axis=0, keepdims=True)
-    numbers = lax.broadcasted_iota(jnp.int32, (N_CTX, N_CTX), 0).astype(f32)
-    lanes = lax.broadcasted_iota(jnp.int32, (N_CTX, N_CTX), 1).astype(f32)
-    holders = jnp.sum(jnp.where(columns[:, 0:1] == lanes, numbers, 0.0), axis=0, keepdims=True)
-    segments = seg_ref[...].astype(f32)
-    row_starts = jnp.zeros((1, ROWS), f32)
-    for document in range(DOCS):
-        row_starts = jnp.where(
-            segments == float(document), starts[:, document + 1 : document + 2], row_starts
-        )
+    row_starts = starts_ref[1:2, :]
     for block in range(2):
         first = pair if block == 0 else 2 * N_CTX - 1 - pair
         places = first * HALF + lax.rem(lax.broadcasted_iota(jnp.int32, (1, COLS), 1), HALF)
         rows_ref[2 * block : 2 * block + 1, :] = places
-        mine = row_starts[:, block * HALF : (block + 1) * HALF].astype(jnp.int32)
+        mine = row_starts[:, block * HALF : (block + 1) * HALF]
         rows_ref[2 * block + 1 : 2 * block + 2, :] = jnp.concatenate([mine] * HEADS, 1)
-    table_ref[...] = jnp.zeros_like(table_ref)
-    table_ref[0:1, :] = holders.astype(jnp.int32)
-    table_ref[1:2, :] = row_starts.astype(jnp.int32)
-    tables = pltpu.make_async_copy(table_ref, table, meta_sem.at[1])
-    tables.start()
-    tables.wait()
     a_hi, b_lo, b_hi = pair // PIECES, table[1, HALF] // CHUNK, (2 * N_CTX - 1 - pair) // PIECES
 
     def slot_of(block_number):
@@ -628,20 +671,13 @@
 
     blank[...] = jnp.zeros_like(blank)
 
-    def zero_copy(band, row):
-        return pltpu.make_async_copy(blank, dkvs[band].at[pl.ds(row, HALF)], blank_sem)
-
-    def clear(chunk, carry):
-        @pl.when(jnp.logical_not(needed(chunk, a_hi, b_lo, b_hi)))
-        def _():
-            for piece in range(PIECES):
-                row = pl.multiple_of(slot_of(chunk * PIECES + piece), HALF)
-                for band in range(3):
-                    zero_copy(band, row).start()
-
-        return carry
-
-    lax.fori_loop(0, CHUNKS, clear, 0)
+    clears = [
+        pltpu.make_async_copy(blank, dkvs[band].at[pl.ds(row, BLANK)], blank_sem.at[band, row // BLANK])
+        for band in range(3)
+        for row in range(0, TOKENS, BLANK)
+    ]
+    for copy in clears:
+        copy.start()
     q_spread[...] = jnp.zeros_like(q_spread)
     g_spread[...] = jnp.zeros_like(g_spread)
     spread(q_ref[...], q_spread, K_AT)
@@ -755,6 +791,8 @@
     for copy in dw_copies:
         copy.start()
 
+    for copy in clears:
+        copy.wait()
     mixed[...] = jnp.zeros_like(mixed)
 
     def backward(block, chunk, masked, mode, count=1):
@@ -832,12 +870,6 @@
         def _():
             wait_chunk(chunk, held, out_sem)
 
-        @pl.when(jnp.logical_not(use))
-        def _():
-            for _piece in range(PIECES):
-                for band in range(3):
-                    zero_copy(band, 0).wait()
-
         return carry
 
     lax.fori_loop(0, CHUNKS, drain, 0)
@@ -845,7 +877,7 @@
         copy.wait()
 
 
-def layer(pair, kvs, weights, q, segments, x, cotangent, gain):
+def layer(pair, table, kvs, weights, q, x, cotangent, gain):
     vmem = pl.BlockSpec(memory_space=pltpu.VMEM)
     anywhere = pl.BlockSpec(memory_space=pl.ANY)
     return pl.pallas_call(
@@ -858,7 +890,7 @@
         + (jax.ShapeDtypeStruct((TOKENS, 128), bf16),) * 3
         + (jax.ShapeDtypeStruct((FF_ROWS // 3, 128), bf16),) * 3,
         grid_spec=pltpu.PrefetchScalarGridSpec(
-            num_scalar_prefetch=1,
+            num_scalar_prefetch=2,
             in_specs=[anywhere] * 7 + [vmem] * 5,
             out_specs=(vmem,) * 3 + (anywhere,) * 6,
             scratch_shapes=[
@@ -879,74 +911,52 @@
                 pltpu.VMEM((FF_ROWS, 128), bf16),
                 pltpu.SemaphoreType.DMA((3,)),
                 pltpu.VMEM((CHUNK, 384), f32),
-                pltpu.VMEM((HALF, 128), bf16),
+                pltpu.VMEM((BLANK, 128), bf16),
                 pltpu.SemaphoreType.DMA((CHUNKS,)),
-                pltpu.SemaphoreType.DMA,
+                pltpu.SemaphoreType.DMA((3, TOKENS // BLANK)),
                 pltpu.VMEM((16, 128), f32),
                 pltpu.VMEM((4, COLS), jnp.int32),
-                pltpu.VMEM((N_CTX, META, 128), bf16),
-                pltpu.SemaphoreType.DMA((2,)),
-                pltpu.VMEM((8, 128), jnp.int32),
-                pltpu.SMEM((8, 128), jnp.int32),
             ],
         ),
         compiler_params=pltpu.CompilerParams(vmem_limit_bytes=VMEM_LIMIT),
         name="layer",
-    )(pair, *kvs, *weights, q, segments, x, cotangent, gain)
+    )(pair, table, *kvs, *weights, q, table, x, cotangent, gain)
 
 
 def reduce_kernel(*refs):
     dkv, dws = refs[0:3], refs[3:6]
     dq_ref, n_ref, x_ref, gh_ref, cos_ref, sin_ref, gain_ref, wq_ref, wk_ref, wv_ref = refs[6:16]
-    gx_ref, outs, outs_one = refs[16], refs[17:20], refs[20:23]
-    rest = refs[23:]
+    gx_ref, outs = refs[16], refs[17:20]
+    rest = refs[20:]
     done, done_ff, done_one, rest = rest[0:3], rest[3:6], rest[6:9], rest[9:]
     first, rest = rest[:SCATTER_REFS], rest[SCATTER_REFS:]
     second, rest = rest[:SCATTER_REFS], rest[SCATTER_REFS:]
     third, rest = rest[:SCATTER_REFS], rest[SCATTER_REFS:]
-    parts, own, own_one, rest = rest[0:3], rest[3:6], rest[6:9], rest[9:]
-    gain_rows, sems, sems_one = rest
+    parts, own, rest = rest[0:3], rest[3:6], rest[6:]
+    gain_rows, sems = rest
     me, coords, core = whereabouts()
     greet(me, coords, core)
-
-    def feed_forward():
-        yield from scatter_steps([(dw,) for dw in dws], done_ff, second, True)
-        for band in range(3):
-            own[band][...] = done_ff[band][...].astype(bf16)
-        yield from gather_steps(own, outs, Pool(sems))
-
-    def small():
-        yield from scatter_steps([(part,) for part in parts], done_one, third, False)
-        for band in range(3):
-            own_one[band][...] = done_one[band][...].astype(bf16)
-        yield from gather_steps(own_one, outs_one, Pool(sems_one), False)
+    meet()
 
     def advance(steps, count):
         for _ in range(count):
             next(steps)
 
     scatter = scatter_steps([(d,) for d in dkv], done, first, True)
-    other = feed_forward()
+    other = scatter_steps([(dw,) for dw in dws], done_ff, second, True)
     advance(scatter, 1)
     advance(other, 1)
     advance(scatter, 12)
-    advance(other, SIDE)
-    run(scatter)
 
     cos_wide, sin_wide = cos_ref[...], -sin_ref[...]
-    tiles = [turn(dq_ref[:, 128 * t : 128 * t + 128] * SCALE, cos_wide, sin_wide).astype(bf16) for t in range(4)]
-    mixed = turn(
-        jnp.concatenate([done[1][0:ROWS, 0:64], dq_ref[:, 512:576] * SCALE], 1), cos_wide, sin_wide
-    ).astype(bf16)
-    grad_q = jnp.concatenate(tiles + [mixed[:, 64:128]], 1)
-    grad_k = jnp.concatenate(
-        [turn(done[0][0:ROWS, :], cos_wide, sin_wide).astype(bf16), mixed[:, 0:64]], 1
-    )
-    grad_v = jnp.concatenate([done[2][0:ROWS, :], done[1][0:ROWS, 64:128]], 1).astype(bf16)
     normed = n_ref[...]
     features = x_ref[...].astype(f32).T
-    grad_normed = nt_dot(grad_q, wq_ref[...]) + nn_dot(grad_k, wk_ref[...]) + nn_dot(grad_v, wv_ref[...])
-    by_x, by_gain = rms_back(features, gain_ref[...].reshape(1, D), grad_normed)
+    tiles = [turn(dq_ref[:, 128 * t : 128 * t + 128] * SCALE, cos_wide, sin_wide).astype(bf16) for t in range(4)]
+    last = turn(
+        jnp.concatenate([dq_ref[:, 512:576], jnp.zeros((ROWS, 64), f32)], 1) * SCALE, cos_wide, sin_wide
+    ).astype(bf16)
+    grad_q = jnp.concatenate(tiles + [last[:, 0:64]], 1)
+    grad_normed = nt_dot(grad_q, wq_ref[...])
 
     def put(at, rows16):
         block = at // 16
@@ -962,25 +972,39 @@
                 put(at + tile * height + row, grads[row : row + 16, 128 * tile : 128 * tile + 128])
 
     pack(Q_AT, tn_dot(normed, grad_q))
+    for at in range(GAIN_ONE_AT + 16, ATT_ROWS, 16):
+        put(at, jnp.zeros((16, 128), bf16))
+    gain_rows[...] = jnp.zeros_like(gain_rows)
+    advance(other, SIDE)
+    run(scatter)
+
+    last = turn(
+        jnp.concatenate([done[1][:, 0:64], jnp.zeros((ROWS, 64), f32)], 1), cos_wide, sin_wide
+    ).astype(bf16)
+    grad_k = jnp.concatenate([turn(done[0][...], cos_wide, sin_wide).astype(bf16), last[:, 0:64]], 1)
+    grad_v = jnp.concatenate([done[2][...], done[1][:, 64:128]], 1).astype(bf16)
     pack(KV_AT, tn_dot(jnp.concatenate([grad_k, grad_v], 1), normed))
-    gain_rows[...] = jnp.zeros_like(gain_rows)
+    grad_normed = grad_normed + nn_dot(grad_k, wk_ref[...]) + nn_dot(grad_v, wv_ref[...])
+    by_x, by_gain = rms_back(features, gain_ref[...].reshape(1, D), grad_normed)
     for tile in range(4):
         gain_rows[tile : tile + 1, :] = by_gain[:, 128 * tile : 128 * tile + 128]
     gain_rows[4:5, 0:64] = by_gain[:, 512:576]
     put(GAIN_ONE_AT, gain_rows[...].astype(bf16))
-    for at in range(GAIN_ONE_AT + 16, ATT_ROWS, 16):
-        put(at, jnp.zeros((16, 128), bf16))
-
-    chain = small()
-    advance(chain, 1)
+
+    small = scatter_steps([(part,) for part in parts], done_one, third, False)
+    advance(small, 1)
     gx_ref[...] = gh_ref[...] + by_x
-    turns = [(chain, 1), (other, 2)]
+    turns = [(other, 3), (small, 1)]
     while turns:
         for steps, count in list(turns):
             try:
                 advance(steps, count)
             except StopIteration:
                 turns.remove((steps, count))
+    for band in range(3):
+        own[band][0:BAND_ROWS, :] = done_ff[band][...].astype(bf16)
+        own[band][BAND_ROWS:FINAL_ROWS, :] = done_one[band][...].astype(bf16)
+    run(gather_steps(own, outs, Pool(sems)))
 
 
 def reduce_all(dkvs, dws, dq, normed, x, grad_hidden, cos_wide, sin_wide, gain, wq, wk, wv):
@@ -990,10 +1014,9 @@
     return pl.pallas_call(
         reduce_kernel,
         out_shape=(jax.ShapeDtypeStruct((ROWS, D), f32),)
-        + (jax.ShapeDtypeStruct((SIDE, SIDE, SIDE, 2, BAND_ROWS, 128), bf16),) * 3
-        + (jax.ShapeDtypeStruct((SIDE, SIDE, SIDE, 2, one, 128), bf16),) * 3,
+        + (jax.ShapeDtypeStruct((SIDE, SIDE, SIDE, 2, FINAL_ROWS, 128), bf16),) * 3,
         in_specs=[anywhere] * 6 + [vmem] * 10,
-        out_specs=(vmem,) + (anywhere,) * 6,
+        out_specs=(vmem,) + (anywhere,) * 3,
         scratch_shapes=[pltpu.VMEM((ROWS, 128), f32)] * 3
         + [pltpu.VMEM((BAND_ROWS, 128), f32)] * 3
         + [pltpu.VMEM((one, 128), f32)] * 3
@@ -1001,13 +1024,8 @@
         + scatter_scratch(BAND_ROWS, True)
         + scatter_scratch(one, False)
         + [pltpu.VMEM((SIDE, SIDE, SIDE, 2, one, 128), bf16)] * 3
-        + [pltpu.VMEM((BAND_ROWS, 128), bf16)] * 3
-        + [pltpu.VMEM((one, 128), bf16)] * 3
-        + [
-            pltpu.VMEM((16, 128), f32),
-            pltpu.SemaphoreType.DMA((GATHER_SEMS,)),
-            pltpu.SemaphoreType.DMA((GATHER_SEMS_ONE,)),
-        ],
+        + [pltpu.VMEM((FINAL_ROWS, 128), bf16)] * 3
+        + [pltpu.VMEM((16, 128), f32), pltpu.SemaphoreType.DMA((GATHER_SEMS,))],
         compiler_params=pltpu.CompilerParams(
             collective_id=2, has_side_effects=True, vmem_limit_bytes=VMEM_LIMIT
         ),
@@ -1019,7 +1037,7 @@
 
 
 def unpack_kernel(
-    sums0, sums1, sums2, ones0, ones1, ones2, gx_ref,
+    sums0, sums1, sums2, gx_ref,
     xt_ref, ga_ref, gq_ref, gk_ref, gv_ref, gm_ref, gg_hbm, gu_hbm, gd_hbm, go_hbm,
     held, held_one, full0, full1, full2, full3, sem_in, sem_one, sem_out,
 ):
@@ -1040,7 +1058,7 @@
             hi = min(edges[part + 1], (band + 1) * band_blocks)
             mine.append(
                 pltpu.make_async_copy(
-                    sums[band].at[pl.ds(lo - band * band_blocks, hi - lo)],
+                    sums[band].at[pl.ds(lo - band * band_blocks, hi - lo), pl.ds(0, BAND_ROWS)],
                     held.at[pl.ds(lo, hi - lo)],
                     sem_in.at[part, len(mine)],
                 )
@@ -1049,8 +1067,10 @@
             lo = hi
         copies.append(mine)
     small = [
-        pltpu.make_async_copy(ref, held_one.at[band], sem_one.at[band])
-        for band, ref in enumerate((ones0, ones1, ones2))
+        pltpu.make_async_copy(
+            sums[band].at[:, pl.ds(BAND_ROWS, BAND_ROWS_ONE)], held_one.at[band], sem_one.at[band]
+        )
+        for band in range(3)
     ]
     for copy in small:
         copy.start()
@@ -1087,14 +1107,14 @@
         copy.wait()
 
 
-def unpack(sums, ones, grad_x):
+def unpack(sums, grad_x):
     vmem = pl.BlockSpec(memory_space=pltpu.VMEM)
     anywhere = pl.BlockSpec(memory_space=pl.ANY)
     shapes = ((D, ROWS), (D,), (D, D), (192, D), (192, D), (D,), (D, FF), (D, FF), (D, FF), (D, D))
     return pl.pallas_call(
         unpack_kernel,
         out_shape=tuple(jax.ShapeDtypeStruct(s, f32) for s in shapes),
-        in_specs=[anywhere] * 6 + [vmem],
+        in_specs=[anywhere] * 3 + [vmem],
         out_specs=(vmem,) * 6 + (anywhere,) * 4,
         scratch_shapes=[
             pltpu.VMEM((3 * N_CTX, BAND_ROWS, 128), bf16),
@@ -1110,8 +1130,7 @@
         compiler_params=pltpu.CompilerParams(vmem_limit_bytes=VMEM_LIMIT),
         name="unpack",
     )(
-        *[s.reshape(N_CTX, BAND_ROWS, 128) for s in sums],
-        *[s.reshape(N_CTX, BAND_ROWS_ONE, 128) for s in ones],
+        *[s.reshape(N_CTX, FINAL_ROWS, 128) for s in sums],
         grad_x,
     )
 
@@ -1144,15 +1163,15 @@
     segments = segment_ids[None, :]
     x_turned = layer_input.T
     wk_turned, wv_turned = w_key.T, w_value.T
-    q_rot, normed, *kvs = project_and_gather(
+    q_rot, normed, table, *kvs = project_and_gather(
         pair_table, x_turned, attn_gain, w_query, wk_turned, wv_turned, cos_wide, sin_wide, segments
     )
     result, grad_hidden, dq, *rest = layer(
         pair_table,
-        [kv.reshape(N_CTX, kv.shape[4], 128) for kv in kvs],
+        table,
+        [kv.reshape(N_CTX, ROWS, 128) for kv in kvs],
         [w_out, w_gate, w_up, w_down.T],
         q_rot,
-        segments,
         x_turned,
         cotangent.T,
         mlp_gain,
@@ -1172,7 +1191,7 @@
         wk_turned,
         wv_turned,
     )
-    gx, ga, gq, gk, gv, gm, gg, gu, gd, go = unpack(sums[0:3], sums[3:6], grad_x)
+    gx, ga, gq, gk, gv, gm, gg, gu, gd, go = unpack(sums, grad_x)
     return (result.T, gx.T, ga, gq, gk.T, gv.T, go, gm, gg, gu, gd.T)
 
 

time: 200 us -> 189 us (0.945)
  Pallas kernels: 198 us -> 187 us
    pallas_call x1, Pallas kernels: 55.2 us -> 42 us  [layer(): pl.pallas_call(layer_kernel, out_shape=(jax.ShapeDtypeStruct((D, ROWS), b...]
    pallas_call x1, Pallas kernels: 89.3 us -> 92.6 us  [reduce_all(): pl.pallas_call(reduce_kernel, out_shape=(jax.ShapeDtypeStruct((ROWS, D),...]
where the time goes in v3:
time: 189 us
  Pallas kernels  187 us (99%)
    pallas_call x1, Pallas kernels, reduce_all(): pl.pallas_call(reduce_kernel, out_shape=(jax.ShapeDtypeStruct((ROWS, D),...  92.6 us
    pallas_call x1, Pallas kernels, project_and_gather(): pl.pallas_call(project_kernel, out_shape=(jax.ShapeDtypeStruct((ROWS, D),...  43.2 us
    pallas_call x1, Pallas kernels, layer(): pl.pallas_call(layer_kernel, out_shape=(jax.ShapeDtypeStruct((D, ROWS), b...  42 us
    pallas_call x1, Pallas kernels, unpack(): pl.pallas_call(unpack_kernel, out_shape=tuple((jax.ShapeDtypeStruct(s, f3...  9.07 us

profile of v3, /device:TPU:1, one launch (start us, length us, event | category | flops | bytes accessed | tf_op | source)
XLA Modules:
  0.0 189.4 jit_solution(2067984646745769791)
XLA Ops:
  1.3 1.0 fusion
  2.3 43.2 %project_and_gather.1 = (bf16[128,576]{1,0:T(8,128)(2,1)}, bf16[128,576]{1,0:T(8,128)(2,1)}, s32[8,128]{1,0:T(8,128)}, bf16[4,4,4,2,128,128]{5,4,3,2,1,0:T(8,128...) custom-call(s32[1]{0:T(128)} %copy.24.pair_ref, bf16[576,128]{1,0:T(8,128)(2,1)} %bitcast.39, ...), custom_call_target="tpu_custom_call" | custom-call | tf_op jit(solution)/shard_map/project_and_gather/pallas_call | solution.py:566
  45.5 42.0 %layer.1 = (bf16[576,128]{1,0:T(8,128)(2,1)}, f32[128,576]{1,0:T(8,128)}, f32[128,576]{1,0:T(8,128)}, bf16[16384,128]{1,0:T(8,128)(2,1)}, bf16[16384,128]{1,0:T(...) custom-call(s32[1]{0:T(128)} %copy.24.pair_ref, ...), custom_call_target="tpu_custom_call" | custom-call | tf_op jit(solution)/shard_map/layer/pallas_call | solution.py:883
  87.5 92.6 %reduce_all.1 = (f32[128,576]{1,0:T(8,128)}, bf16[4,4,4,2,80,128]{5,4,3,2,1,0:T(8,128)(2,1)}, bf16[4,4,4,2,80,128]{5,4,3,2,1,0:T(8,128)(2,1)}, bf16[4,4,4,2,80,128]{5,4,3,2,1,0:T(8,128)(2,1)}) custom-call(bf16[4,4,4,2,128,128]{5,4,3,2,1,0:T(8,128)(2,1)} %bitcast.29, bf16[4,4,4,2,128,128]{5,4,3,2,1,0:T(8,128)(2,1)} %bitcast.30, ...), custom_call_target="tpu_custom_call" | custom-call | tf_op jit(solution)/shard_map/reduce_all/pallas_call | solution.py:1014
  180.1 9.1 %unpack.1 = (f32[576,128]{1,0:T(8,128)}, f32[576]{0:T(1024)}, f32[576,576]{1,0:T(8,128)}, f32[192,576]{1,0:T(8,128)}, f32[192,576]{1,0:T(8,128)}, /*index=5*/f32...) custom-call(bf16[128,80,128]{2,1,0:T(8,128)(2,1)} %bitcast.32, ...), custom_call_target="tpu_custom_call" | custom-call | tf_op jit(solution)/shard_map/unpack/pallas_call | solution.py:1114
  (2 shorter events, 0.0 us)

commit v4 on v3

--- a/solution.py
+++ b/solution.py
@@ -293,6 +293,11 @@
         for band in bands:
             sent[band][phase] = shared
     homes, swaps = {}, {}
+
+    def line_at(band, step, sub):
+        order = ORDERS[band]
+        return at_axes(order, (wrap(coords[order[0]], step), wrap(coords[order[1]], steps[sub]), WHOLE))
+
     if ring:
         for step in steps:
             for band in bands:
@@ -311,8 +316,7 @@
                     top += size
             for sub in range(SIDE):
                 for band in bands:
-                    order = ORDERS[band]
-                    line = at_axes(order, (wrap(coords[order[0]], step), sub, WHOLE))
+                    line = line_at(band, step, sub)
                     if band == 0:
                         swaps[step, sub] = pool.new()
                     top = 0
@@ -334,27 +338,31 @@
             send(part.at[:, :, :, 1 - core], sib[band], sibling, sent[band][3], swaps[band])
 
     def add_swap(band, step, sub):
-        order = ORDERS[band]
-        first = wrap(coords[order[0]], step)
         if band == 0:
             if sub == 0:
                 wait_for(blocks(3, 4, 4), homes[step])
             wait_for(blocks(1, 3, 4), swaps[step, sub])
 
-        line = at_axes(order, (first, sub, WHOLE))
+        line = line_at(band, step, sub)
         acc[band][line] = acc[band][line] + sib[band][line]
-
-    jobs = [(sub, band) for sub in range(SIDE) for band in bands]
-
-    def line_at(band, step, sub):
-        order = ORDERS[band]
-        return at_axes(order, (wrap(coords[order[0]], step), sub, WHOLE))
 
     def sum_up(band, region, landed):
         total = acc[band][region].astype(f32)
         for ref in landed:
             total = total + ref[...].astype(f32)
         acc[band][region] = total.astype(bf16)
+
+    second = pool.new()
+
+    def send_second(band, sub):
+        if steps[sub]:
+            send(
+                acc[band].at[line_at(band, 0, sub)],
+                landing[band][1].at[sub],
+                neighbour(me, coords, ORDERS[band][1], steps[sub]),
+                sent[band][1],
+                second,
+            )
 
     if ring:
         passing, ending = {}, {}
@@ -401,6 +409,7 @@
                 sum_up(
                     band, line_at(band, 0, sub), [landing[band][0].at[slot, sub] for slot in (1, 2)]
                 )
+                send_second(band, sub)
     else:
         came = [pool.new() for band in bands]
         yield
@@ -426,21 +435,13 @@
             for slot in range(3):
                 total = total + landing[band][0][slot].astype(f32)
             acc[band][plane] = total.astype(bf16)
-    came = pool.new()
-    for slot, step in enumerate((2, 1, -1)):
-        for band in bands:
-            order = ORDERS[band]
-            line = at_axes(order, (coords[order[0]], wrap(coords[order[1]], step), WHOLE))
-            send(
-                acc[band].at[line],
-                landing[band][1].at[slot],
-                neighbour(me, coords, order[1], step),
-                sent[band][1],
-                came,
-            )
+    if not ring:
+        for sub in range(SIDE):
+            for band in bands:
+                send_second(band, sub)
     yield
     ends = pool.new()
-    wait_for(blocks(3, 3, 4), came)
+    wait_for(blocks(3, 3, 4), second)
     for band in bands:
         order = ORDERS[band]
         line = at_axes(order, (coords[order[0]], coords[order[1]], WHOLE))
@@ -600,8 +601,8 @@
     pltpu.make_async_copy(window, window, sem.at[chunk]).wait()
 
 
-def chunk_mask(chunk, place_row, start_row):
-    keys = chunk * CHUNK + lax.broadcasted_iota(jnp.int32, (CHUNK, COLS), 0)
+def chunk_mask(chunk, count, place_row, start_row):
+    keys = chunk * CHUNK + lax.broadcasted_iota(jnp.int32, (count * CHUNK, COLS), 0)
     return (keys <= place_row) & (keys >= start_row)
 
 
@@ -621,8 +622,6 @@
             ((wo_hbm, wo_ref), (wg_hbm, wg_ref), (wu_hbm, wu_ref), (wd_hbm, wd_ref))
         )
     ]
-    for copy in weights:
-        copy.start()
     pair = pair_ref[0]
     row_starts = starts_ref[1:2, :]
     for block in range(2):
@@ -655,6 +654,8 @@
         return carry
 
     lax.fori_loop(0, CHUNKS, issue, 0)
+    for copy in weights:
+        copy.start()
 
     def spread(rows, place, windows):
         for block in range(2):
@@ -676,8 +677,6 @@
         for band in range(3)
         for row in range(0, TOKENS, BLANK)
     ]
-    for copy in clears:
-        copy.start()
     q_spread[...] = jnp.zeros_like(q_spread)
     g_spread[...] = jnp.zeros_like(g_spread)
     spread(q_ref[...], q_spread, K_AT)
@@ -685,16 +684,16 @@
     top[...] = jnp.full_like(top, NEG)
     total[...] = jnp.zeros_like(total)
 
-    def mask_of(block, chunk):
+    def mask_of(block, chunk, count):
         return chunk_mask(
-            chunk, rows_ref[2 * block : 2 * block + 1, :], rows_ref[2 * block + 1 : 2 * block + 2, :]
+            chunk, count, rows_ref[2 * block : 2 * block + 1, :], rows_ref[2 * block + 1 : 2 * block + 2, :]
         )
 
     def forward(block, chunk, masked, count=1):
         window = chunk_rows(chunk, count)
         scores = nt_dot(held[window, 0:256], q_spread[block])
         if masked:
-            scores = jnp.where(mask_of(block, chunk), scores, NEG)
+            scores = jnp.where(mask_of(block, chunk, count), scores, NEG)
         old = top[block : block + 1, :]
         new = jnp.maximum(old, jnp.max(scores, axis=0, keepdims=True))
         probs = jnp.exp(scores - new)
@@ -730,13 +729,26 @@
         return carry
 
     plain = jnp.minimum(a_hi, b_lo) // 2
+    tail = 2 * plain
+    paired = (a_hi == tail + 1) & (b_lo > a_hi)
+    ahead = jnp.where(paired, tail + 2, tail)
     lax.fori_loop(0, plain, forward_pair, 0)
-    lax.fori_loop(2 * plain, b_hi + 1, forward_step, 0)
+
+    @pl.when(paired)
+    def _():
+        wait_chunk(tail, held, sem)
+        wait_chunk(tail + 1, held, sem)
+        forward(0, tail, True, 2)
+
+    lax.fori_loop(ahead, b_hi + 1, forward_step, 0)
     for block in range(2):
         sums = total[block : block + 1, :]
         top[block : block + 1, :] = top[block : block + 1, :] + jnp.log(sums)
         mixed[block] = mixed[block] / sums
         unspread(mixed.at[block], att_ref, block, V_AT)
+
+    for copy in clears:
+        copy.start()
 
     attended = att_ref[...].astype(bf16)
     cotangent = c_ref[...].astype(f32).T.astype(bf16)
@@ -802,7 +814,7 @@
         scores = nt_dot(keys, q_spread[block])
         probs = jnp.exp(scores - top[block : block + 1, :])
         if masked:
-            probs = jnp.where(mask_of(block, chunk), probs, 0.0)
+            probs = jnp.where(mask_of(block, chunk, count), probs, 0.0)
         grad_probs = nt_dot(values, g_spread[block])
         grad_scores = (probs * (grad_probs - delta_ref[block : block + 1, :])).astype(bf16)
         mixed[block, 0:192] += nn_dot(keys.T[0:192], grad_scores)
@@ -859,7 +871,14 @@
         return carry
 
     lax.fori_loop(0, plain, backward_pair, 0)
-    lax.fori_loop(2 * plain, b_hi + 1, backward_step, 0)
+
+    @pl.when(paired)
+    def _():
+        backward(0, tail, True, "only", 2)
+        put_back(tail)
+        put_back(tail + 1)
+
+    lax.fori_loop(ahead, b_hi + 1, backward_step, 0)
     for block in range(2):
         unspread(mixed.at[block], dq_ref, block, K_AT)
 
@@ -976,6 +995,8 @@
         put(at, jnp.zeros((16, 128), bf16))
     gain_rows[...] = jnp.zeros_like(gain_rows)
     advance(other, SIDE)
+    advance(scatter, 1)
+    advance(other, SIDE)
     run(scatter)
 
     last = turn(
@@ -994,7 +1015,7 @@
     small = scatter_steps([(part,) for part in parts], done_one, third, False)
     advance(small, 1)
     gx_ref[...] = gh_ref[...] + by_x
-    turns = [(other, 3), (small, 1)]
+    turns = [(other, 2), (small, 1)]
     while turns:
         for steps, count in list(turns):
             try:
@@ -1038,8 +1059,8 @@
 
 def unpack_kernel(
     sums0, sums1, sums2, gx_ref,
-    xt_ref, ga_ref, gq_ref, gk_ref, gv_ref, gm_ref, gg_hbm, gu_hbm, gd_hbm, go_hbm,
-    held, held_one, full0, full1, full2, full3, sem_in, sem_one, sem_out,
+    ga_ref, gm_ref, xt_hbm, gq_hbm, gk_hbm, gv_hbm, gg_hbm, gu_hbm, gd_hbm, go_hbm,
+    held, held_one, full0, full1, full2, full3, xt_ref, gq_ref, gk_ref, gv_ref, sem_in, sem_one, sem_out,
 ):
     sums = (sums0, sums1, sums2)
     fulls = (full0, full1, full2, full3)
@@ -1074,8 +1095,14 @@
     ]
     for copy in small:
         copy.start()
+    outs = []
+
+    def leave(src, dst):
+        outs.append(pltpu.make_async_copy(src, dst, sem_out.at[len(outs)]))
+        outs[-1].start()
+
     xt_ref[...] = gx_ref[...].T
-    outs = []
+    leave(xt_ref, xt_hbm)
     for part, (at, rows, columns) in enumerate(FF_PARTS):
         for copy in copies[part]:
             copy.wait()
@@ -1084,8 +1111,7 @@
             for row in range(0, rows, BAND_ROWS):
                 piece = held[(at + tile * rows + row) // BAND_ROWS].astype(f32)
                 fulls[part][row : row + BAND_ROWS, 128 * tile : 128 * tile + width] = piece[:, 0:width]
-        outs.append(pltpu.make_async_copy(fulls[part], spots[part], sem_out.at[part]))
-        outs[-1].start()
+        leave(fulls[part], spots[part])
     for copy in small:
         copy.wait()
 
@@ -1103,6 +1129,9 @@
             gv_ref[row : row + 16, lanes] = fetch_one(KV_AT + tile * 384 + 192 + row)[:, 0:width]
         ga_ref[lanes] = fetch_one(GAIN_ONE_AT)[tile, 0:width]
         gm_ref[lanes] = held[GAIN_AT // BAND_ROWS].astype(f32)[tile, 0:width]
+    leave(gq_ref, gq_hbm)
+    leave(gk_ref, gk_hbm)
+    leave(gv_ref, gv_hbm)
     for copy in outs:
         copy.wait()
 
@@ -1110,12 +1139,12 @@
 def unpack(sums, grad_x):
     vmem = pl.BlockSpec(memory_space=pltpu.VMEM)
     anywhere = pl.BlockSpec(memory_space=pl.ANY)
-    shapes = ((D, ROWS), (D,), (D, D), (192, D), (192, D), (D,), (D, FF), (D, FF), (D, FF), (D, D))
+    shapes = ((D,), (D,), (D, ROWS), (D, D), (192, D), (192, D), (D, FF), (D, FF), (D, FF), (D, D))
     return pl.pallas_call(
         unpack_kernel,
         out_shape=tuple(jax.ShapeDtypeStruct(s, f32) for s in shapes),
         in_specs=[anywhere] * 3 + [vmem],
-        out_specs=(vmem,) * 6 + (anywhere,) * 4,
+        out_specs=(vmem,) * 2 + (anywhere,) * 8,
         scratch_shapes=[
             pltpu.VMEM((3 * N_CTX, BAND_ROWS, 128), bf16),
             pltpu.VMEM((3, N_CTX, BAND_ROWS_ONE, 128), bf16),
@@ -1123,9 +1152,13 @@
             pltpu.VMEM((D, FF), f32),
             pltpu.VMEM((D, FF), f32),
             pltpu.VMEM((D, D), f32),
+            pltpu.VMEM((D, ROWS), f32),
+            pltpu.VMEM((D, D), f32),
+            pltpu.VMEM((192, D), f32),
+            pltpu.VMEM((192, D), f32),
             pltpu.SemaphoreType.DMA((4, 2)),
             pltpu.SemaphoreType.DMA((3,)),
-            pltpu.SemaphoreType.DMA((4,)),
+            pltpu.SemaphoreType.DMA((8,)),
         ],
         compiler_params=pltpu.CompilerParams(vmem_limit_bytes=VMEM_LIMIT),
         name="unpack",
@@ -1191,7 +1224,7 @@
         wk_turned,
         wv_turned,
     )
-    gx, ga, gq, gk, gv, gm, gg, gu, gd, go = unpack(sums, grad_x)
+    ga, gm, gx, gq, gk, gv, gg, gu, gd, go = unpack(sums, grad_x)
     return (result.T, gx.T, ga, gq, gk.T, gv.T, go, gm, gg, gu, gd.T)
 
 

time: 189 us -> 184 us (0.974)
  Pallas kernels: 187 us -> 182 us
    pallas_call x1, Pallas kernels: 42 us -> 30.4 us  [layer(): pl.pallas_call(layer_kernel, out_shape=(jax.ShapeDtypeStruct((D, ROWS), b...]
    pallas_call x1, Pallas kernels: 92.6 us -> 99.2 us  [reduce_all(): pl.pallas_call(reduce_kernel, out_shape=(jax.ShapeDtypeStruct((ROWS, D),...]
where the time goes in v4:
time: 184 us
  Pallas kernels  182 us (99%)
    pallas_call x1, Pallas kernels, reduce_all(): pl.pallas_call(reduce_kernel, out_shape=(jax.ShapeDtypeStruct((ROWS, D),...  99.2 us
    pallas_call x1, Pallas kernels, project_and_gather(): pl.pallas_call(project_kernel, out_shape=(jax.ShapeDtypeStruct((ROWS, D),...  43.2 us
    pallas_call x1, Pallas kernels, layer(): pl.pallas_call(layer_kernel, out_shape=(jax.ShapeDtypeStruct((D, ROWS), b...  30.4 us
    pallas_call x1, Pallas kernels, unpack(): pl.pallas_call(unpack_kernel, out_shape=tuple((jax.ShapeDtypeStruct(s, f3...  8.97 us

profile of v4, /device:TPU:1, one launch (start us, length us, event | category | flops | bytes accessed | tf_op | source)
XLA Modules:
  0.0 184.2 jit_solution(2641888706300401467)
XLA Ops:
  1.3 1.0 fusion
  2.3 43.2 %project_and_gather.1 = (bf16[128,576]{1,0:T(8,128)(2,1)}, bf16[128,576]{1,0:T(8,128)(2,1)}, s32[8,128]{1,0:T(8,128)}, bf16[4,4,4,2,128,128]{5,4,3,2,1,0:T(8,128...) custom-call(s32[1]{0:T(128)} %copy.24.pair_ref, bf16[576,128]{1,0:T(8,128)(2,1)} %bitcast.39, ...), custom_call_target="tpu_custom_call" | custom-call | tf_op jit(solution)/shard_map/project_and_gather/pallas_call | solution.py:567
  45.5 30.4 %layer.1 = (bf16[576,128]{1,0:T(8,128)(2,1)}, f32[128,576]{1,0:T(8,128)}, f32[128,576]{1,0:T(8,128)}, bf16[16384,128]{1,0:T(8,128)(2,1)}, bf16[16384,128]{1,0:T(...) custom-call(s32[1]{0:T(128)} %copy.24.pair_ref, ...), custom_call_target="tpu_custom_call" | custom-call | tf_op jit(solution)/shard_map/layer/pallas_call | solution.py:902
  75.9 99.2 %reduce_all.1 = (f32[128,576]{1,0:T(8,128)}, bf16[4,4,4,2,80,128]{5,4,3,2,1,0:T(8,128)(2,1)}, bf16[4,4,4,2,80,128]{5,4,3,2,1,0:T(8,128)(2,1)}, bf16[4,4,4,2,80,128]{5,4,3,2,1,0:T(8,128)(2,1)}) custom-call(bf16[4,4,4,2,128,128]{5,4,3,2,1,0:T(8,128)(2,1)} %bitcast.29, bf16[4,4,4,2,128,128]{5,4,3,2,1,0:T(8,128)(2,1)} %bitcast.30, ...), custom_call_target="tpu_custom_call" | custom-call | tf_op jit(solution)/shard_map/reduce_all/pallas_call | solution.py:1035
  175.1 9.0 %unpack.1 = (f32[576]{0:T(1024)}, f32[576]{0:T(1024)}, f32[576,128]{1,0:T(8,128)}, f32[576,576]{1,0:T(8,128)}, f32[192,576]{1,0:T(8,128)}, /*index=5*/f32[192,57...) custom-call(bf16[128,80,128]{2,1,0:T(8,128)(2,1)} %bitcast.32, ...), custom_call_target="tpu_custom_call" | custom-call | tf_op jit(solution)/shard_map/unpack/pallas_call | solution.py:1143
  (2 shorter events, 0.0 us)

commit v5 on v4

--- a/solution.py
+++ b/solution.py
@@ -314,6 +314,8 @@
                         homes[step],
                     ).start()
                     top += size
+        yield
+        for step in steps:
             for sub in range(SIDE):
                 for band in bands:
                     line = line_at(band, step, sub)
@@ -335,6 +337,9 @@
             homes[band], swaps[band] = pool.new(), pool.new()
             (part,) = parts[band]
             pltpu.make_async_copy(part.at[:, :, :, core], acc[band], homes[band]).start()
+        yield
+        for band in bands:
+            (part,) = parts[band]
             send(part.at[:, :, :, 1 - core], sib[band], sibling, sent[band][3], swaps[band])
 
     def add_swap(band, step, sub):
@@ -955,7 +960,6 @@
     gain_rows, sems = rest
     me, coords, core = whereabouts()
     greet(me, coords, core)
-    meet()
 
     def advance(steps, count):
         for _ in range(count):
@@ -963,6 +967,9 @@
 
     scatter = scatter_steps([(d,) for d in dkv], done, first, True)
     other = scatter_steps([(dw,) for dw in dws], done_ff, second, True)
+    advance(scatter, 1)
+    advance(other, 1)
+    meet()
     advance(scatter, 1)
     advance(other, 1)
     advance(scatter, 12)
@@ -1013,7 +1020,7 @@
     put(GAIN_ONE_AT, gain_rows[...].astype(bf16))
 
     small = scatter_steps([(part,) for part in parts], done_one, third, False)
-    advance(small, 1)
+    advance(small, 2)
     gx_ref[...] = gh_ref[...] + by_x
     turns = [(other, 2), (small, 1)]
     while turns:

time: 184 us -> 185 us (level)
    pallas_call x1, Pallas kernels: 30.4 us -> 51.4 us  [layer(): pl.pallas_call(layer_kernel, out_shape=(jax.ShapeDtypeStruct((D, ROWS), b...]
    pallas_call x1, Pallas kernels: 99.2 us -> 78.8 us  [reduce_all(): pl.pallas_call(reduce_kernel, out_shape=(jax.ShapeDtypeStruct((ROWS, D),...]
where the time goes in v5:
time: 185 us
  Pallas kernels  182 us (98%)
    pallas_call x1, Pallas kernels, reduce_all(): pl.pallas_call(reduce_kernel, out_shape=(jax.ShapeDtypeStruct((ROWS, D),...  78.8 us
    pallas_call x1, Pallas kernels, layer(): pl.pallas_call(layer_kernel, out_shape=(jax.ShapeDtypeStruct((D, ROWS), b...  51.4 us
    pallas_call x1, Pallas kernels, project_and_gather(): pl.pallas_call(project_kernel, out_shape=(jax.ShapeDtypeStruct((ROWS, D),...  43.2 us
    pallas_call x1, Pallas kernels, unpack(): pl.pallas_call(unpack_kernel, out_shape=tuple((jax.ShapeDtypeStruct(s, f3...  8.97 us

profile of v5, /device:TPU:1, one launch (start us, length us, event | category | flops | bytes accessed | tf_op | source)
XLA Modules:
  0.0 184.8 jit_solution(1183694717459172326)
XLA Ops:
  1.3 1.0 fusion
  2.3 43.2 %project_and_gather.1 = (bf16[128,576]{1,0:T(8,128)(2,1)}, bf16[128,576]{1,0:T(8,128)(2,1)}, s32[8,128]{1,0:T(8,128)}, bf16[4,4,4,2,128,128]{5,4,3,2,1,0:T(8,128...) custom-call(s32[1]{0:T(128)} %copy.24.pair_ref, bf16[576,128]{1,0:T(8,128)(2,1)} %bitcast.39, ...), custom_call_target="tpu_custom_call" | custom-call | tf_op jit(solution)/shard_map/project_and_gather/pallas_call | solution.py:572
  45.5 51.4 %layer.1 = (bf16[576,128]{1,0:T(8,128)(2,1)}, f32[128,576]{1,0:T(8,128)}, f32[128,576]{1,0:T(8,128)}, bf16[16384,128]{1,0:T(8,128)(2,1)}, bf16[16384,128]{1,0:T(...) custom-call(s32[1]{0:T(128)} %copy.24.pair_ref, ...), custom_call_target="tpu_custom_call" | custom-call | tf_op jit(solution)/shard_map/layer/pallas_call | solution.py:907
  96.9 78.8 %reduce_all.1 = (f32[128,576]{1,0:T(8,128)}, bf16[4,4,4,2,80,128]{5,4,3,2,1,0:T(8,128)(2,1)}, bf16[4,4,4,2,80,128]{5,4,3,2,1,0:T(8,128)(2,1)}, bf16[4,4,4,2,80,128]{5,4,3,2,1,0:T(8,128)(2,1)}) custom-call(bf16[4,4,4,2,128,128]{5,4,3,2,1,0:T(8,128)(2,1)} %bitcast.29, bf16[4,4,4,2,128,128]{5,4,3,2,1,0:T(8,128)(2,1)} %bitcast.30, ...), custom_call_target="tpu_custom_call" | custom-call | tf_op jit(solution)/shard_map/reduce_all/pallas_call | solution.py:1042
  175.7 9.0 %unpack.1 = (f32[576]{0:T(1024)}, f32[576]{0:T(1024)}, f32[576,128]{1,0:T(8,128)}, f32[576,576]{1,0:T(8,128)}, f32[192,576]{1,0:T(8,128)}, /*index=5*/f32[192,57...) custom-call(bf16[128,80,128]{2,1,0:T(8,128)(2,1)} %bitcast.32, ...), custom_call_target="tpu_custom_call" | custom-call | tf_op jit(solution)/shard_map/unpack/pallas_call | solution.py:1150
  (2 shorter events, 0.0 us)
